TPU v7x, 32 devices: a whole 2x2x4 slice. The times are simulated.
32 devices in a mesh: scen: 8 (over y, x, core), col: 4 (over z).
Axes of the slice: x: 2, y: 2, z: 4, core: 2. Of those that a mesh axis runs over, the one named last changes fastest.
Arguments:
- private_seeds: float32 [8, 4, 2, 768, 256], P('scen', 'col'), may hold values from -6 to 6
- private_inverse: float32 [8, 4, 2, 768, 768], P('scen', 'col'), as said below
- coupling: bfloat16 [8, 2, 768, 16384], P('scen', None, None, 'col'), may hold values from -0.0546875 to 0.0546875
- shared_seed: float32 [4, 4096, 256], P('col', 'scen'), may hold values from -6 to 6
- shared_inverse: float32 [8, 4, 512, 4, 4096], P(None, None, None, 'col', 'scen')
Outputs:
- private_adjoint: float32 [8, 4, 2, 768, 256], P('scen', 'col')
- shared_adjoint: float32 [4, 4096, 256], P('col')
Inputs may be any that keep to these rules, and one draw needn't show every extreme that they name: `private_inverse`: each 768 x 768 block is upper triangular.
All inputs are finite; a program needn't handle non-finite values.
Results may differ from a plain program's by a relative error of at most 0.0024.
Values sent between devices are 32-bit elements; how exact they have to be, the bound alone decides.
No kernel may reach another device: no remote copies, remote signals or barrier semaphores. Data moves between devices by JAX's collectives and lax.ppermute only.
A program may use at most 192 MiB of HBM per device.

v0:
```python
import functools
import math

import jax
import jax.numpy as jnp
from jax import lax
from jax.experimental import pallas as pl
from jax.experimental.pallas import tpu as pltpu
from jax.sharding import PartitionSpec as P

F32, BF16 = jnp.float32, jnp.bfloat16
AXES = ("scen", "col")
MIB = 1024 * 1024


def split(value):
    high = value.astype(BF16)
    return high, (value - high.astype(F32)).astype(BF16)


def dot(left, right):
    return jnp.dot(left, right, preferred_element_type=F32)


def dot3(left, right):
    (left_high, left_low), (right_high, right_low) = left, right
    return dot(left_high, right_high) + (dot(left_low, right_high) + dot(left_high, right_low))


def tile_of(width):
    return 256 if width % 256 == 0 else width


def bytes_of(spec, dtype):
    shape = spec.block_shape
    return 0 if shape is None else math.prod(shape) * dtype.itemsize


def call(kernel, grid, in_specs, out_specs, out_shape, flops, moved, prefetch=1, scratch=(), room=None, earlier=(), **more):
    inputs = prefetch + len(in_specs)
    body = kernel
    if earlier:
        body = lambda *refs: kernel(*refs[:inputs], *refs[inputs + len(earlier) :])
    in_specs = list(in_specs) + [pl.BlockSpec(memory_space=pl.ANY)] * len(earlier)

    def run(*operands):
        operands += tuple(earlier)
        outs = out_shape if isinstance(out_shape, (list, tuple)) else [out_shape]
        specs = out_specs if isinstance(out_specs, (list, tuple)) else [out_specs]
        need = sum(2 * bytes_of(s, o.dtype) for s, o in zip(in_specs, operands[prefetch:]))
        need += sum(2 * bytes_of(s, o.dtype) for s, o in zip(specs, outs))
        need += sum(
            math.prod(s.shape) * jnp.dtype(s.dtype).itemsize for s in scratch if len(s.shape) > 1
        )
        return pl.pallas_call(
            body,
            grid_spec=pltpu.PrefetchScalarGridSpec(
                num_scalar_prefetch=prefetch,
                grid=grid,
                in_specs=in_specs,
                out_specs=out_specs,
                scratch_shapes=list(scratch),
            ),
            out_shape=out_shape,
            compiler_params=pltpu.CompilerParams(vmem_limit_bytes=room or need + 10 * MIB),
            cost_estimate=pl.CostEstimate(
                flops=int(flops) // 1, bytes_accessed=int(moved) // 1, transcendentals=0
            ),
            **more,
        )(*operands)

    return run


def spread(bits, place):
    unit = 0
    for j, bit in enumerate(bits):
        unit = unit | (((place >> (len(bits) - 1 - j)) & 1) << bit)
    return unit


def place_of(bits, unit):
    place = 0
    for bit in bits:
        place = place * 2 + ((unit >> bit) & 1)
    return place


def first_kernel(seeds_ref, inverse_ref, first_ref, half_ref):
    width = inverse_ref.shape[1]
    tile = tile_of(width)
    seeds = split(seeds_ref[0].T)
    inverse = split(inverse_ref[0])
    for start in range(0, width, tile):
        stop = start + tile
        first = dot3(
            [part[:, :stop] for part in seeds], [part[:stop, start:stop] for part in inverse]
        )
        first_ref[:, start:stop] = first
        half_ref[:, start:stop] = first.astype(BF16)


def first_of(seeds, inverse):
    blocks, width, count = seeds.shape
    across = pl.BlockSpec((count, width), lambda b: (0, b))
    return call(
        first_kernel,
        (blocks,),
        [
            pl.BlockSpec((1, width, count), lambda b: (b, 0, 0)),
            pl.BlockSpec((1, width, width), lambda b: (b, 0, 0)),
        ],
        [across, across],
        [
            jax.ShapeDtypeStruct((count, blocks * width), F32),
            jax.ShapeDtypeStruct((count, blocks * width), BF16),
        ],
        6 * blocks * width * width * count,
        4 * blocks * width * (width + 3 * count),
        prefetch=0,
    )(seeds, inverse)


def seed_kernel(me_ref, coupling_ref, half_ref, *sum_refs):
    total = dot(half_ref[...], coupling_ref[...])
    cols = total.shape[1] // len(sum_refs)
    for chunk, ref in enumerate(sum_refs):
        ref[0] = total[:, chunk * cols : (chunk + 1) * cols]


def seed_products(me, coupling, half, sub, orders, base, offset):
    count, depth = half.shape
    cols = seed_cols(sub)
    wide = cols * len(orders)
    units = 1 << len(orders[0])

    def unit_of(f):
        return spread(orders[0], f) | base

    return call(
        seed_kernel,
        (units,),
        [
            pl.BlockSpec(
                (depth, wide), lambda f, me_ref: (0, ((unit_of(f) ^ me_ref[0]) * sub + offset) // wide)
            ),
            pl.BlockSpec((count, depth), lambda f, me_ref: (0, 0)),
        ],
        [
            pl.BlockSpec(
                (1, count, cols),
                functools.partial(
                    lambda order, f, me_ref: (place_of(order, unit_of(f)), 0, 0), order
                ),
            )
            for order in orders
        ],
        [jax.ShapeDtypeStruct((units, count, cols), F32)] * len(orders),
        2 * units * depth * wide * count,
        units * wide * (2 * depth + 4 * count),
    )(me, coupling, half)


def seed_cols(sub):
    return sub // 2 if sub % 256 == 0 else sub


def reduced_kernel(chunks, seed_ref, *refs):
    *terms, out_ref = refs
    each = len(terms) // chunks
    cols = terms[0].shape[2]
    for chunk in range(chunks):
        place = pl.ds(chunk * cols, cols)
        total = sum(ref[0] for ref in terms[chunk * each : (chunk + 1) * each])
        out_ref[place] = seed_ref[place] - total.T


def reduced_of(seed, terms):
    whole = pl.BlockSpec(seed.shape, lambda i: (0, 0))
    flat = [term for chunk in terms for term in chunk]
    return call(
        functools.partial(reduced_kernel, len(terms)),
        (1,),
        [whole] + [pl.BlockSpec((1, *term.shape[1:]), lambda i: (0, 0, 0)) for term in flat],
        whole,
        jax.ShapeDtypeStruct(seed.shape, F32),
        0,
        16 * seed.size,
        prefetch=0,
    )(seed, *flat)


def rows_of(tile_ref, rows, pieces):
    if pieces == 1:
        return tile_ref[0]
    lanes = tile_ref.shape[2]
    parts = tile_ref[0].reshape(rows // 8, pieces, 8, lanes)
    parts = [parts[:, j] for j in range(pieces)]
    at = lax.broadcasted_iota(jnp.int32, (rows // 8, 8, lanes), 1)
    step = 1
    while step < pieces:
        upper = (at & step) != 0
        for j in range(pieces):
            if j & step == 0:
                low, high = parts[j], parts[j + step]
                parts[j] = jnp.where(upper, pltpu.roll(high, step, 1), low)
                parts[j + step] = jnp.where(upper, high, pltpu.roll(low, 8 - step, 1))
        step *= 2
    return jnp.concatenate([part.reshape(rows, lanes) for part in parts], axis=1)


def share_kernel(chunks, pieces, *refs):
    terms, out_ref, held_ref, order_ref = refs[:-3], *refs[-3:]
    each = len(terms) // chunks
    rows = terms[0].shape[1]
    run = 8 // pieces
    total = jnp.concatenate(
        [sum(ref[0] for ref in terms[at : at + each]) for at in range(0, len(terms), each)], axis=0
    )
    for lane in range(0, total.shape[1], 128):
        held_ref[...] = total[:, lane : lane + 128]
        for place in range(8):
            j, b = place // run, place % run
            order_ref[pl.ds(place, chunks * rows // 8, stride=8), :] = held_ref[
                pl.ds(b * pieces + j, chunks * rows // 8, stride=8), :
            ]
        out_ref[:, lane : lane + 128] = order_ref[...]


def share_of(terms, pieces):
    _, rows, count = terms[0][0].shape
    flat = [term for chunk in terms for term in chunk]
    shape = (len(terms) * rows, count)
    return call(
        functools.partial(share_kernel, len(terms), pieces),
        (1,),
        [pl.BlockSpec((1, rows, count), lambda i: (0, 0, 0)) for _ in flat],
        pl.BlockSpec(shape, lambda i: (0, 0)),
        jax.ShapeDtypeStruct(shape, F32),
        0,
        4 * rows * count * (len(flat) + len(terms)),
        prefetch=0,
        scratch=[pltpu.VMEM((shape[0], 128), F32)] * 2,
    )(*flat)


def shared_kernel(group, rows, pieces, me_ref, *refs):
    tiles, refs = refs[:group], refs[group:]
    seed_ref, out_ref, high_ref, low_ref, seed_high_ref, seed_low_ref = refs

    @pl.when(pl.program_id(0) == 0)
    def _():
        seed_high_ref[...], seed_low_ref[...] = split(seed_ref[...])

    for g in range(group):
        place = pl.ds(g * rows, rows)
        high_ref[place], low_ref[place] = split(rows_of(tiles[g], rows, pieces))
    total = dot3((high_ref[...], low_ref[...]), (seed_high_ref[...], seed_low_ref[...]))
    for g in range(group):
        out_ref[g] = total[g * rows : (g + 1) * rows]


def shared_products(me, tiles, seed, bits, base, offset, rows, earlier):
    depth, count = seed.shape
    lanes = tiles.shape[2]
    pieces = depth // lanes
    units = 1 << len(bits)
    group = min(units, 4)

    def place(g, f, me_ref):
        return (spread(bits, f * group + g) | base) ^ me_ref[0], offset // rows, 0

    halves = pltpu.VMEM((group * rows, depth), BF16)
    seed_halves = pltpu.VMEM((depth, count), BF16)
    return call(
        functools.partial(shared_kernel, group, rows, pieces),
        (units // group,),
        [
            pl.BlockSpec((1, rows * pieces, lanes), functools.partial(place, g))
            for g in range(group)
        ]
        + [pl.BlockSpec((depth, count), lambda f, me_ref: (0, 0))],
        pl.BlockSpec((group, rows, count), lambda f, me_ref: (f, 0, 0)),
        jax.ShapeDtypeStruct((units, rows, count), F32),
        6 * units * rows * depth * count,
        4 * units * rows * (depth + count),
        scratch=[halves, halves, seed_halves, seed_halves],
        room=34 * MIB,
        earlier=earlier,
    )(me, *([tiles] * group), seed)


def coupled_kernel(units, halves, aliased, last, me_ref, coupling_ref, start_ref, *refs):
    pieces, refs = refs[: units * halves], refs[units * halves :]
    refs = refs[1:] if aliased else refs
    u = pl.program_id(0)
    if last:
        inverse_ref, out_ref, adjoint_ref, second_ref, held_ref, sem = refs
        fetch = pltpu.make_async_copy(inverse_ref, held_ref, sem)
    else:
        second_ref, adjoint_ref, packed_ref = refs

    @pl.when(u == 0)
    def _():
        if last:
            fetch.start()
        second_ref[...] = start_ref[...]

    for g in range(units):

        @pl.when(u == g)
        def _():
            block = jnp.concatenate(
                [ref[...] for ref in pieces[g * halves : (g + 1) * halves]], axis=0
            )
            adjoint_ref[...] = block
            if not last:
                packed_ref[0] = block
            second_ref[...] -= dot(coupling_ref[...], block.astype(BF16))

    if last:

        @pl.when(u == units - 1)
        def _():
            fetch.wait()
            blocks, width, _ = held_ref.shape
            tile = tile_of(width)
            for block in range(blocks):
                second = split(second_ref[block * width : (block + 1) * width])
                for start in range(0, width, tile):
                    out_ref[block, start : start + tile] = dot3(
                        split(held_ref[block, start : start + tile, start:]),
                        [part[start:] for part in second],
                    )


def coupled_step(me, coupling, start, pieces, numbers, adjoint, inverse=None):
    depth, count = start.shape
    halves = len(pieces[0])
    sub = sum(piece.shape[0] for piece in pieces[0])
    units = len(numbers)

    def unit_of(u):
        unit = numbers[-1]
        for g in range(units - 1):
            unit = jnp.where(u == g, numbers[g], unit)
        return unit

    whole = pl.BlockSpec((depth, count), lambda u, me_ref: (0, 0))
    in_specs = [
        pl.BlockSpec((depth, sub), lambda u, me_ref: (0, unit_of(u) ^ me_ref[0])),
        whole,
    ]
    operands = [coupling, start]
    for group in pieces:
        for piece in group:
            in_specs.append(pl.BlockSpec(piece.shape, lambda u, me_ref: (0, 0)))
            operands.append(piece)
    more = {}
    if adjoint is not None:
        in_specs.append(pl.BlockSpec(memory_space=pl.ANY))
        operands.append(adjoint)
        more["input_output_aliases"] = {len(operands): 1}
    flops = 2 * units * depth * sub * count
    moved = units * sub * (2 * depth + 8 * count) + 8 * depth * count
    place = pl.BlockSpec((sub, count), lambda u, me_ref: (unit_of(u) ^ me_ref[0], 0))
    adjoint_shape = jax.ShapeDtypeStruct((coupling.shape[1], count), F32)
    if inverse is None:
        out_specs = [whole, place, pl.BlockSpec((1, sub, count), lambda u, me_ref: (u, 0, 0))]
        out_shape = [
            jax.ShapeDtypeStruct((depth, count), F32),
            adjoint_shape,
            jax.ShapeDtypeStruct((units, sub, count), F32),
        ]
        scratch = ()
    else:
        blocks, width, _ = inverse.shape
        in_specs.append(pl.BlockSpec(memory_space=pl.ANY))
        operands.append(inverse)
        out_specs = [pl.BlockSpec((blocks, width, count), lambda u, me_ref: (0, 0, 0)), place]
        out_shape = [jax.ShapeDtypeStruct((blocks, width, count), F32), adjoint_shape]
        scratch = (
            pltpu.VMEM((depth, count), F32),
            pltpu.VMEM(inverse.shape, F32),
            pltpu.SemaphoreType.DMA(()),
        )
        flops += 6 * inverse.size * count
        moved += 4 * inverse.size
    return call(
        functools.partial(
            coupled_kernel, units, halves, adjoint is not None, inverse is not None
        ),
        (units,),
        in_specs,
        out_specs,
        out_shape,
        flops,
        moved,
        scratch=scratch,
        **more,
    )(me, *operands)


def on_device(scen_count, col_count, private_seeds, private_inverse, coupling, shared_seed, shared_inverse):
    blocks, width = private_inverse.shape[2:4]
    count = private_seeds.shape[4]
    shard_cols = coupling.shape[3]
    sub = shared_seed.shape[1]
    depth = shared_inverse.shape[4]
    devices = scen_count * col_count
    scen_bits, col_bits = scen_count.bit_length() - 1, col_count.bit_length() - 1

    my_scen, my_col = lax.axis_index("scen"), lax.axis_index("col")
    me_scen = my_scen.astype(jnp.int32).reshape(1)
    me = (my_scen * col_count + my_col).astype(jnp.int32).reshape(1)

    def exchange(array, bit):
        return lax.ppermute(array, AXES, [(w, w ^ (1 << bit)) for w in range(devices)])

    flat_coupling = coupling[0].reshape(blocks * width, shard_cols)
    first, half = first_of(private_seeds[0, 0], private_inverse[0, 0])

    def halved(own, arrived, order):
        away, kept = own
        half = away.shape[0]
        terms = [kept, arrived, exchange(away + arrived[half:], order[0])]
        for bit in order[1:]:
            half = terms[-1].shape[0] // 2
            terms.append(exchange(sum(term[half : 2 * half] for term in terms), bit))
        return terms

    core = col_bits
    col_order = list(range(col_bits))
    outer = list(range(core + 1, core + scen_bits))

    orders = [outer, outer[::-1]][: sub // seed_cols(sub)]
    scen_orders = [[bit - core for bit in order] for order in orders]
    arrived = []
    for chunk, order in enumerate(scen_orders):
        away = seed_products(me_scen, flat_coupling, half, sub, [order], 1, chunk * seed_cols(sub))
        arrived.append(exchange(away[0], core))
    own = seed_products(me_scen, flat_coupling, half, sub, scen_orders, 0, 0)
    reduced = reduced_of(
        shared_seed[0],
        [
            halved((kept[kept.shape[0] // 2 :], kept), away, order)
            for kept, away, order in zip(own, arrived, orders)
        ],
    )

    lanes = min(depth, 128)
    tiles = shared_inverse.reshape(devices, sub * depth // lanes, lanes)
    orders = [
        outer + col_order,
        outer[1:] + col_order + outer[:1],
        col_order[:1] + outer + col_order[1:],
        outer + col_order,
    ]
    pieces = depth // lanes
    rows = sub // len(orders)

    def products(chunk, bits, base, *earlier):
        return shared_products(me, tiles, reduced, bits, base, chunk * rows, rows, earlier)

    arrived = [
        exchange(products(chunk, order, 1 << core), core) for chunk, order in enumerate(orders)
    ]
    shares = []
    for chunk, order in enumerate(orders):
        away = products(chunk, order[1:], 1 << order[0], arrived[chunk])
        kept = products(chunk, order[1:], 0, arrived[-1])
        shares.append(halved((away, kept), arrived[chunk], order))

    near = []
    for part, way in enumerate((outer, outer[::-1])):
        held = {0: share_of(shares[2 * part : 2 * part + 2], pieces)}
        for bit in way:
            for number, piece in list(held.items()):
                held[number | (1 << (bit - core))] = exchange(piece, bit)
        near.append(held)
    second, adjoint = first.T, None
    inverse = private_inverse[0, 0]
    numbers = sorted(near[0])
    middle, last = numbers[1:-1], numbers[-1]

    def take(numbers, pieces, inverse=None):
        return coupled_step(me_scen, flat_coupling, second, pieces, numbers, adjoint, inverse)

    own = [held[0] for held in near]
    second, adjoint, _ = take([0, 1], [own, [exchange(piece, core) for piece in own]])
    second, adjoint, packed = take(middle, [[held[number] for held in near] for number in middle])
    far = exchange(packed, core)
    second, adjoint, packed = take([last], [[held[last] for held in near]])
    far_last = exchange(packed, core)
    second, adjoint, _ = take(
        [number | 1 for number in middle], [[far[g]] for g in range(len(middle))]
    )
    second, adjoint = take([last | 1], [[far_last[0]]], inverse)
    return second[None, None], adjoint[None]


def solution(mesh):
    in_specs = (
        P("scen", "col", None, None, None),
        P("scen", "col", None, None, None),
        P("scen", None, None, "col"),
        P("col", "scen", None),
        P(None, None, None, "col", "scen"),
    )
    out_specs = (P("scen", "col", None, None, None), P("col", None, None))
    return jax.shard_map(
        functools.partial(on_device, mesh.shape["scen"], mesh.shape["col"]),
        mesh=mesh,
        in_specs=in_specs,
        out_specs=out_specs,
        check_vma=False,
    )
```

profile of v0, /device:TPU:0, one launch (start us, length us, event | category | flops | bytes accessed | tf_op | source)
XLA Modules:
  0.0 214.2 jit_solution(2856822890817938171)
XLA Ops:
  0.6 2.3 %copy-done.8 = f32[1,1,2,768,768]{4,3,2,1,0:T(8,128)S(1)} copy-done((f32[1,1,2,768,768]{4,3,2,1,0:T(8,128)S(1)}, f32[1,1,2,768,768]{4,3,2,1,0:T(8,128)}, u32[]{:S(2)}) %copy-start.8) | copy-done | bytes 4718616
  3.0 1.4 copy-done.20
  4.4 1.8 shard_map.68
  6.2 1.1 copy-done.11
  7.4 4.6 %copy-done = bf16[1,2,768,4096]{3,2,1,0:T(8,128)(2,1)S(1)} copy-done((bf16[1,2,768,4096]{3,2,1,0:T(8,128)(2,1)S(1)}, bf16[1,2,768,4096]{3,2,1,0:T(8,128)(2,1)}, u32[]{:S(2)}) %copy-start) | copy-done | bytes 12582936
  12.0 2.1 shard_map.71
  14.6 2.1 shard_map.70
  16.9 3.0 %shard_map.69 = (f32[4,256,256]{2,1,0:T(8,128)S(1)}, f32[4,256,256]{2,1,0:T(8,128)S(1)}) custom-call(s32[1]{0:T(128)} %bitcast.me_ref, bf16[1536,4096]{1,0:T(8,128)(2,1)S(1)} %bitcast.19, bf16[256,1536]{1,0:T(8,128)(2,1)S(1)} %get-tuple-element.19.half_ref), custom_call_target="tpu_custom_call" | custom-call | flops 1610612736 | bytes 8388608 | tf_op jit(solution)/shard_map/pallas_call | solution.py:55
  19.9 3.0 %collective-permute-start.4 = (f32[2,256,256]{2,1,0:T(8,128)S(1)}, f32[2,256,256]{2,1,0:T(8,128)S(1)}, u32[]{:S(2)}, u32[]{:S(2)}) collective-permute-start(f32[2,256,256]{2,1,0:T(8,128)S(1)} %slice_add_fusion.12), channel_id=1, source_target_pairs={{0,16},{1,17},{2,18},{3,19},{4,20},{5,21},{6,22},{7,23},{8,24},{9,... | collective-permute-start | bytes 1572872 | tf_op jit(solution)/shard_map/ppermute | solution.py:418
  23.0 1.6 collective-permute-start.1
  24.6 10.5 %collective-permute-done.4.refs_6_ = f32[2,256,256]{2,1,0:T(8,128)S(1)} collective-permute-done((f32[2,256,256]{2,1,0:T(8,128)S(1)}, f32[2,256,256]{2,1,0:T(8,128)S(1)}, u32[]{:S(2)}, u32[]{:S(2)}) %collective-permute-start.4) | collective-permute-done | bytes 524320 | tf_op jit(solution)/shard_map/ppermute | solution.py:418
  35.9 1.7 collective-permute-start.5
  39.2 1.5 collective-permute-start.2
  40.8 3.1 %collective-permute-done.5.refs_7_ = f32[1,256,256]{2,1,0:T(8,128)S(1)} collective-permute-done((f32[1,256,256]{2,1,0:T(8,128)}, f32[1,256,256]{2,1,0:T(8,128)S(1)}, u32[]{:S(2)}, u32[]{:S(2)}) %collective-permute-start.5) | collective-permute-done | bytes 262176 | tf_op jit(solution)/shard_map/ppermute | solution.py:418
  43.9 2.8 %collective-permute-done.2.refs_3_ = f32[1,256,256]{2,1,0:T(8,128)} collective-permute-done((f32[1,256,256]{2,1,0:T(8,128)}, f32[1,256,256]{2,1,0:T(8,128)}, u32[]{:S(2)}, u32[]{:S(2)}) %collective-permute-start.2) | collective-permute-done | bytes 262176 | tf_op jit(solution)/shard_map/ppermute | solution.py:418
  46.7 1.2 copy-done.10
  51.0 1.2 shard_map.72.refs_4_.refs_5_
  52.2 4.6 %shard_map.73 = f32[16,128,256]{2,1,0:T(8,128)S(1)} custom-call(s32[1]{0:T(128)} %bitcast.5.me_ref.refs_0_, f32[32,2048,128]{2,1,0:T(8,128)} %bitcast.35, f32[32,2048,128]{2,1,0:T(8,128)} %bitcast.36, f32[32,2048,128]{2,1,0:T(8,128)} %bitcast.37, f32[32,2048,128]{2,1,0:T(8,128)} %bitcast.38, f32[512,256]{1,0:T(8,128)S(1)} %shard_map.72.refs_4_.refs_5_), custom_call_target="tpu_custom_call" | custom-call | flops 1610612736 | bytes 6291456 | tf_op jit(solution)/shard_map/pallas_call | solution.py:55
  56.9 4.6 %shard_map.82 = f32[16,128,256]{2,1,0:T(8,128)S(1)} custom-call(s32[1]{0:T(128)} %bitcast.5.me_ref.refs_0_, f32[32,2048,128]{2,1,0:T(8,128)} %bitcast.39, f32[32,2048,128]{2,1,0:T(8,128)} %bitcast.40, f32[32,2048,128]{2,1,0:T(8,128)} %bitcast.41, f32[32,2048,128]{2,1,0:T(8,128)} %bitcast.42, f32[512,256]{1,0:T(8,128)S(1)} %shard_map.72.refs_4_.refs_5_), custom_call_target="tpu_custom_call" | custom-call | flops 1610612736 | bytes 6291456 | tf_op jit(solution)/shard_map/pallas_call | solution.py:55
  62.1 4.6 %shard_map.78 = f32[16,128,256]{2,1,0:T(8,128)S(1)} custom-call(s32[1]{0:T(128)} %bitcast.5.me_ref.refs_0_, f32[32,2048,128]{2,1,0:T(8,128)} %bitcast.43, f32[32,2048,128]{2,1,0:T(8,128)} %bitcast.44, f32[32,2048,128]{2,1,0:T(8,128)} %bitcast.45, f32[32,2048,128]{2,1,0:T(8,128)} %bitcast.46, f32[512,256]{1,0:T(8,128)S(1)} %shard_map.72.refs_4_.refs_5_), custom_call_target="tpu_custom_call" | custom-call | flops 1610612736 | bytes 6291456 | tf_op jit(solution)/shard_map/pallas_call | solution.py:55
  66.8 4.6 %shard_map.75 = f32[16,128,256]{2,1,0:T(8,128)S(1)} custom-call(s32[1]{0:T(128)} %bitcast.5.me_ref.refs_0_, f32[32,2048,128]{2,1,0:T(8,128)} %bitcast.47, f32[32,2048,128]{2,1,0:T(8,128)} %bitcast.48, f32[32,2048,128]{2,1,0:T(8,128)} %bitcast.49, f32[32,2048,128]{2,1,0:T(8,128)} %bitcast.50, f32[512,256]{1,0:T(8,128)S(1)} %shard_map.72.refs_4_.refs_5_), custom_call_target="tpu_custom_call" | custom-call | flops 1610612736 | bytes 6291456 | tf_op jit(solution)/shard_map/pallas_call | solution.py:55
  71.9 2.7 %shard_map.85 = f32[8,128,256]{2,1,0:T(8,128)S(1)} custom-call(s32[1]{0:T(128)} %bitcast.5.me_ref.refs_0_, f32[32,2048,128]{2,1,0:T(8,128)} %bitcast.51, f32[32,2048,128]{2,1,0:T(8,128)} %bitcast.52, f32[32,2048,128]{2,1,0:T(8,128)} %bitcast.53, f32[32,2048,128]{2,1,0:T(8,128)} %bitcast.54, f32[512,256]{1,0:T(8,128)S(1)} %shard_map.72.refs_4_.refs_5_, ...), custom_call_target="tpu_custom_call" | custom-call | flops 805306368 | bytes 3145728 | tf_op jit(solution)/shard_map/pallas_call | solution.py:55
  74.6 1.1 slice_add_fusion
  76.4 3.4 %shard_map.83 = f32[8,128,256]{2,1,0:T(8,128)S(1)} custom-call(s32[1]{0:T(128)} %bitcast.5.me_ref.refs_0_, f32[32,2048,128]{2,1,0:T(8,128)} %bitcast.58, f32[32,2048,128]{2,1,0:T(8,128)} %bitcast.56, f32[32,2048,128]{2,1,0:T(8,128)} %bitcast.57, f32[32,2048,128]{2,1,0:T(8,128)} %bitcast.55, f32[512,256]{1,0:T(8,128)S(1)} %shard_map.72.refs_4_.refs_5_, ...), custom_call_target="tpu_custom_call" | custom-call | flops 805306368 | bytes 3145728 | tf_op jit(solution)/shard_map/pallas_call | solution.py:55
  80.9 1.5 collective-permute-start.18
  82.5 3.4 %shard_map.79 = f32[8,128,256]{2,1,0:T(8,128)S(1)} custom-call(s32[1]{0:T(128)} %bitcast.5.me_ref.refs_0_, f32[32,2048,128]{2,1,0:T(8,128)} %bitcast.59, f32[32,2048,128]{2,1,0:T(8,128)} %bitcast.60, f32[32,2048,128]{2,1,0:T(8,128)} %bitcast.61, f32[32,2048,128]{2,1,0:T(8,128)} %bitcast.62, f32[512,256]{1,0:T(8,128)S(1)} %shard_map.72.refs_4_.refs_5_, ...), custom_call_target="tpu_custom_call" | custom-call | flops 805306368 | bytes 3145728 | tf_op jit(solution)/shard_map/pallas_call | solution.py:55
  85.9 1.2 slice_add_fusion.2
  87.1 1.5 collective-permute-start.13
  88.6 3.4 %shard_map.76 = f32[8,128,256]{2,1,0:T(8,128)S(1)} custom-call(s32[1]{0:T(128)} %bitcast.5.me_ref.refs_0_, f32[32,2048,128]{2,1,0:T(8,128)} %bitcast.63, f32[32,2048,128]{2,1,0:T(8,128)} %bitcast.64, f32[32,2048,128]{2,1,0:T(8,128)} %bitcast.65, f32[32,2048,128]{2,1,0:T(8,128)} %bitcast.66, f32[512,256]{1,0:T(8,128)S(1)} %shard_map.72.refs_4_.refs_5_, ...), custom_call_target="tpu_custom_call" | custom-call | flops 805306368 | bytes 3145728 | tf_op jit(solution)/shard_map/pallas_call | solution.py:55
  92.1 1.1 slice_add_fusion.3
  93.2 1.5 collective-permute-start.8
  94.7 2.7 %shard_map.84.refs_6_ = f32[8,128,256]{2,1,0:T(8,128)S(1)} custom-call(s32[1]{0:T(128)} %bitcast.5.me_ref.refs_0_, f32[32,2048,128]{2,1,0:T(8,128)} %bitcast.69, f32[32,2048,128]{2,1,0:T(8,128)} %bitcast.68, f32[32,2048,128]{2,1,0:T(8,128)} %bitcast.67, f32[32,2048,128]{2,1,0:T(8,128)} %bitcast.70, f32[512,256]{1,0:T(8,128)S(1)} %shard_map.72.refs_4_.refs_5_, ...), custom_call_target="tpu_custom_call" | custom-call | flops 805306368 | bytes 3145728 | tf_op jit(solution)/shard_map/pallas_call | solution.py:55
  97.4 2.7 %shard_map.81.refs_0_ = f32[8,128,256]{2,1,0:T(8,128)S(1)} custom-call(s32[1]{0:T(128)} %bitcast.5.me_ref.refs_0_, f32[32,2048,128]{2,1,0:T(8,128)} %bitcast.71, f32[32,2048,128]{2,1,0:T(8,128)} %bitcast.72, f32[32,2048,128]{2,1,0:T(8,128)} %bitcast.73, f32[32,2048,128]{2,1,0:T(8,128)} %bitcast.74, f32[512,256]{1,0:T(8,128)S(1)} %shard_map.72.refs_4_.refs_5_, ...), custom_call_target="tpu_custom_call" | custom-call | flops 805306368 | bytes 3145728 | tf_op jit(solution)/shard_map/pallas_call | solution.py:55
  100.1 2.9 %shard_map.77.refs_6_ = f32[8,128,256]{2,1,0:T(8,128)S(1)} custom-call(s32[1]{0:T(128)} %bitcast.5.me_ref.refs_0_, f32[32,2048,128]{2,1,0:T(8,128)} %bitcast.75, f32[32,2048,128]{2,1,0:T(8,128)} %bitcast.76, f32[32,2048,128]{2,1,0:T(8,128)} %bitcast.77, f32[32,2048,128]{2,1,0:T(8,128)} %bitcast.78, f32[512,256]{1,0:T(8,128)S(1)} %shard_map.72.refs_4_.refs_5_, ...), custom_call_target="tpu_custom_call" | custom-call | flops 805306368 | bytes 3145728 | tf_op jit(solution)/shard_map/pallas_call | solution.py:55
  103.0 2.8 %shard_map.74.refs_0_ = f32[8,128,256]{2,1,0:T(8,128)S(1)} custom-call(s32[1]{0:T(128)} %bitcast.5.me_ref.refs_0_, f32[32,2048,128]{2,1,0:T(8,128)} %bitcast.79, f32[32,2048,128]{2,1,0:T(8,128)} %bitcast.80, f32[32,2048,128]{2,1,0:T(8,128)} %bitcast.81, f32[32,2048,128]{2,1,0:T(8,128)} %bitcast.82, f32[512,256]{1,0:T(8,128)S(1)} %shard_map.72.refs_4_.refs_5_, ...), custom_call_target="tpu_custom_call" | custom-call | flops 805306368 | bytes 3145728 | tf_op jit(solution)/shard_map/pallas_call | solution.py:55
  105.8 1.3 slice_add_fusion.4
  107.7 1.2 slice_add_fusion.6
  109.5 4.0 %collective-permute-done.13.refs_8_ = f32[8,128,256]{2,1,0:T(8,128)} collective-permute-done((f32[8,128,256]{2,1,0:T(8,128)}, f32[8,128,256]{2,1,0:T(8,128)}, u32[]{:S(2)}, u32[]{:S(2)}) %collective-permute-start.13) | collective-permute-done | bytes 1048608 | tf_op jit(solution)/shard_map/ppermute | solution.py:418
  113.5 1.1 slice_add_fusion.8
  115.2 9.3 %collective-permute-done.8.refs_2_ = f32[8,128,256]{2,1,0:T(8,128)} collective-permute-done((f32[8,128,256]{2,1,0:T(8,128)}, f32[8,128,256]{2,1,0:T(8,128)}, u32[]{:S(2)}, u32[]{:S(2)}) %collective-permute-start.8) | collective-permute-done | bytes 1048608 | tf_op jit(solution)/shard_map/ppermute | solution.py:418
  124.5 1.1 slice_add_fusion.10
  125.7 1.6 collective-permute-start.9
  128.3 1.6 collective-permute-start.24
  130.0 4.8 %collective-permute-done.19.refs_3_ = f32[4,128,256]{2,1,0:T(8,128)S(1)} collective-permute-done((f32[4,128,256]{2,1,0:T(8,128)S(1)}, f32[4,128,256]{2,1,0:T(8,128)S(1)}, u32[]{:S(2)}, u32[]{:S(2)}) %collective-permute-start.19) | collective-permute-done | bytes 524320 | tf_op jit(solution)/shard_map/ppermute | solution.py:418
  135.8 1.6 collective-permute-start.20
  138.4 2.6 %collective-permute-start.15 = (f32[2,128,256]{2,1,0:T(8,128)S(1)}, f32[2,128,256]{2,1,0:T(8,128)S(1)}, u32[]{:S(2)}, u32[]{:S(2)}) collective-permute-start(f32[2,128,256]{2,1,0:T(8,128)S(1)} %slice_add_fusion.20), channel_id=1, source_target_pairs={{0,2},{1,3},{2,0},{3,1},{4,6},{5,7},{6,4},{7,5},{8,10},{9,11},{10,... | collective-permute-start | bytes 786440 | tf_op jit(solution)/shard_map/ppermute | solution.py:418
  142.1 1.7 collective-permute-start.10
  146.1 2.7 %collective-permute-start.21 = (f32[1,128,256]{2,1,0:T(8,128)S(1)}, f32[1,128,256]{2,1,0:T(8,128)S(1)}, u32[]{:S(2)}, u32[]{:S(2)}) collective-permute-start(f32[1,128,256]{2,1,0:T(8,128)S(1)} %slice_add_fusion.34), channel_id=1, source_target_pairs={{0,2},{1,3},{2,0},{3,1},{4,6},{5,7},{6,4},{7,5},{8,10},{9,11},{10,... | collective-permute-start | bytes 393224 | tf_op jit(solution)/shard_map/ppermute | solution.py:418
  148.7 10.3 %collective-permute-done.15.refs_10_ = f32[2,128,256]{2,1,0:T(8,128)S(1)} collective-permute-done((f32[2,128,256]{2,1,0:T(8,128)S(1)}, f32[2,128,256]{2,1,0:T(8,128)S(1)}, u32[]{:S(2)}, u32[]{:S(2)}) %collective-permute-start.15) | collective-permute-done | bytes 262176 | tf_op jit(solution)/shard_map/ppermute | solution.py:418
  160.6 1.2 collective-permute-done.25.refs_11_
  161.8 1.6 collective-permute-done.21.refs_5_
  163.5 1.2 shard_map.86.refs_1_
  165.8 9.6 %collective-permute-done.11.refs_5_ = f32[1,128,256]{2,1,0:T(8,128)S(1)} collective-permute-done((f32[1,128,256]{2,1,0:T(8,128)S(1)}, f32[1,128,256]{2,1,0:T(8,128)S(1)}, u32[]{:S(2)}, u32[]{:S(2)}) %collective-permute-start.11) | collective-permute-done | bytes 131104 | tf_op jit(solution)/shard_map/ppermute | solution.py:418
  175.4 1.9 shard_map.80.refs_0_
  178.4 1.4 collective-permute-start.28
  180.5 1.5 collective-permute-start.30
  182.5 4.6 %copy-done.1 = bf16[1,2,768,4096]{3,2,1,0:T(8,128)(2,1)S(1)} copy-done((bf16[1,2,768,4096]{3,2,1,0:T(8,128)(2,1)S(1)}, bf16[1,2,768,4096]{3,2,1,0:T(8,128)(2,1)}, u32[]{:S(2)}) %copy-start.1) | copy-done | bytes 12582936
  188.0 3.6 %shard_map.87 = (f32[1536,256]{1,0:T(8,128)S(1)}, f32[4096,256]{1,0:T(8,128)}, f32[2,512,256]{2,1,0:T(8,128)}) custom-call(s32[1]{0:T(128)} %bitcast.me_ref, bf16[1536,4096]{1,0:T(8,128)(2,1)S(1)} %bitcast.20, f32[1536,256]{1,0:T(8,128)S(1)} %bitcast.27, f32[256,256]{1,0:T(8,128)} %shard_map.80.refs_0_, f32[256,256]{1,0:T(8,128)S(1)} %shard_map.86.refs_1_, ...), custom_call_target="tpu_custom_call" | custom-call | flops 805306368 | bytes 8388608 | tf_op jit(solution)/shard_map/pallas_call | solution.py:55
  191.9 3.6 %shard_map.88 = (f32[1536,256]{1,0:T(8,128)S(1)}, f32[4096,256]{1,0:T(8,128)}, f32[2,512,256]{2,1,0:T(8,128)S(1)}) custom-call(s32[1]{0:T(128)} %bitcast.me_ref, bf16[1536,4096]{1,0:T(8,128)(2,1)S(1)} %bitcast.21, f32[1536,256]{1,0:T(8,128)S(1)} %get-tuple-element.22.start_ref, ...), custom_call_target="tpu_custom_call", output_to_operand_aliasing={{1}: (7, {})} | custom-call | flops 805306368 | bytes 8388608 | tf_op jit(solution)/shard_map/pallas_call | solution.py:55
  195.5 1.5 collective-permute-start.33
  197.5 6.9 %collective-permute-done.33.refs_1_ = f32[256,256]{1,0:T(8,128)S(1)} collective-permute-done((f32[256,256]{1,0:T(8,128)}, f32[256,256]{1,0:T(8,128)S(1)}, u32[]{:S(2)}, u32[]{:S(2)}) %collective-permute-start.33) | collective-permute-done | bytes 262176 | tf_op jit(solution)/shard_map/ppermute | solution.py:418
  204.4 1.2 collective-permute-done.32.refs_0_
  206.7 2.6 %shard_map.90 = (f32[1536,256]{1,0:T(8,128)S(1)}, f32[4096,256]{1,0:T(8,128)}, f32[2,512,256]{2,1,0:T(8,128)}) custom-call(s32[1]{0:T(128)} %bitcast.me_ref, bf16[1536,4096]{1,0:T(8,128)(2,1)S(1)} %bitcast.25, f32[1536,256]{1,0:T(8,128)S(1)} %get-tuple-element.26.start_ref, ...), custom_call_target="tpu_custom_call", output_to_operand_aliasing={{1}: (5, {})} | custom-call | flops 805306368 | bytes 8388608 | tf_op jit(solution)/shard_map/pallas_call | solution.py:55
  209.7 4.3 %shard_map.91 = (f32[2,768,256]{2,1,0:T(8,128)}, f32[4096,256]{1,0:T(8,128)}) custom-call(s32[1]{0:T(128)} %bitcast.me_ref, bf16[1536,4096]{1,0:T(8,128)(2,1)S(1)} %bitcast.26, f32[1536,256]{1,0:T(8,128)S(1)} %get-tuple-element.29.start_ref, f32[512,256]{1,0:T(8,128)S(1)} %bitcast.32, ...), custom_call_target="tpu_custom_call", output_to_operand_aliasing={{1}: (4, {})} | custom-call | flops 2214592512 | bytes 10485760 | tf_op jit(solution)/shard_map/pallas_call | solution.py:55
  (115 shorter events, 25.7 us)
Async XLA Ops:
  0.6 2.3 %copy-start.8 = (f32[1,1,2,768,768]{4,3,2,1,0:T(8,128)S(1)}, f32[1,1,2,768,768]{4,3,2,1,0:T(8,128)}, u32[]{:S(2)}) copy-start(f32[1,1,2,768,768]{4,3,2,1,0:T(8,128)} %param.6) | copy-start | bytes 14155780
  3.0 1.4 copy-start.20
  6.2 1.1 copy-start.11
  7.4 4.6 %copy-start = (bf16[1,2,768,4096]{3,2,1,0:T(8,128)(2,1)S(1)}, bf16[1,2,768,4096]{3,2,1,0:T(8,128)(2,1)}, u32[]{:S(2)}) copy-start(bf16[1,2,768,4096]{3,2,1,0:T(8,128)(2,1)} %param.7) | copy-start | bytes 37748740
  11.9 4.9 %slice-start = ((s8[12582912]{0:T(1024)(128)(4,1)}), s8[4194304]{0:T(1024)(128)(4,1)S(1)}, s32[]{:S(2)}) async-start(s8[12582912]{0:T(1024)(128)(4,1)} %bitcast.17), calls=%async_computation | async-start | bytes 8388608
  12.0 4.9 %slice-start.1 = ((s8[12582912]{0:T(1024)(128)(4,1)}), s8[4194304]{0:T(1024)(128)(4,1)S(1)}, s32[]{:S(2)}) async-start(s8[12582912]{0:T(1024)(128)(4,1)} %bitcast.17), calls=%async_computation.1 | async-start | bytes 8388608
  14.1 2.8 %slice-start.2 = ((s8[12582912]{0:T(1024)(128)(4,1)}), s8[4194304]{0:T(1024)(128)(4,1)S(1)}, s32[]{:S(2)}) async-start(s8[12582912]{0:T(1024)(128)(4,1)} %bitcast.17), calls=%async_computation.2 | async-start | bytes 8388608
  14.1 5.8 %collective-permute-start.3 = (f32[4,256,256]{2,1,0:T(8,128)S(1)}, f32[4,256,256]{2,1,0:T(8,128)S(1)}, u32[]{:S(2)}, u32[]{:S(2)}) collective-permute-start(f32[4,256,256]{2,1,0:T(8,128)S(1)} %shard_map.71), channel_id=1, source_target_pairs={{0,4},{1,5},{2,6},{3,7},{4,0},{5,1},{6,2},{7,3},{8,12},{9,13},{10,... | collective-permute-start | bytes 3145736 | tf_op jit(solution)/shard_map/ppermute | solution.py:418
  16.7 6.2 %collective-permute-start = (f32[4,256,256]{2,1,0:T(8,128)S(1)}, f32[4,256,256]{2,1,0:T(8,128)S(1)}, u32[]{:S(2)}, u32[]{:S(2)}) collective-permute-start(f32[4,256,256]{2,1,0:T(8,128)S(1)} %shard_map.70), channel_id=1, source_target_pairs={{0,4},{1,5},{2,6},{3,7},{4,0},{5,1},{6,2},{7,3},{8,12},{9,13},{10,... | collective-permute-start | bytes 3145736 | tf_op jit(solution)/shard_map/ppermute | solution.py:418
  19.8 16.1 %copy-start.9 = (f32[4,256,256]{2,1,0:T(8,128)}, f32[4,256,256]{2,1,0:T(8,128)S(1)}, u32[]{:S(2)}) copy-start(f32[4,256,256]{2,1,0:T(8,128)S(1)} %get-tuple-element.21.refs_4_) | copy-start | bytes 3145732
  19.9 15.2 %collective-permute-start.4 = (f32[2,256,256]{2,1,0:T(8,128)S(1)}, f32[2,256,256]{2,1,0:T(8,128)S(1)}, u32[]{:S(2)}, u32[]{:S(2)}) collective-permute-start(f32[2,256,256]{2,1,0:T(8,128)S(1)} %slice_add_fusion.12), channel_id=1, source_target_pairs={{0,16},{1,17},{2,18},{3,19},{4,20},{5,21},{6,22},{7,23},{8,24},{9,... | collective-permute-start | bytes 1572872 | tf_op jit(solution)/shard_map/ppermute | solution.py:418
  23.0 14.6 %collective-permute-start.1 = (f32[2,256,256]{2,1,0:T(8,128)S(1)}, f32[2,256,256]{2,1,0:T(8,128)S(1)}, u32[]{:S(2)}, u32[]{:S(2)}) collective-permute-start(f32[2,256,256]{2,1,0:T(8,128)S(1)} %slice_add_fusion.13), channel_id=1, source_target_pairs={{0,8},{1,9},{2,10},{3,11},{4,12},{5,13},{6,14},{7,15},{8,0},{9,1},... | collective-permute-start | bytes 1572872 | tf_op jit(solution)/shard_map/ppermute | solution.py:418
  35.1 2.6 %copy-start.13 = (f32[2,256,256]{2,1,0:T(8,128)}, f32[2,256,256]{2,1,0:T(8,128)S(1)}, u32[]{:S(2)}) copy-start(f32[2,256,256]{2,1,0:T(8,128)S(1)} %collective-permute-done.4.refs_6_) | copy-start | bytes 1572868
  35.9 8.0 %collective-permute-start.5 = (f32[1,256,256]{2,1,0:T(8,128)}, f32[1,256,256]{2,1,0:T(8,128)S(1)}, u32[]{:S(2)}, u32[]{:S(2)}) collective-permute-start(f32[1,256,256]{2,1,0:T(8,128)} %slice_add_fusion.26), channel_id=1, source_target_pairs={{0,8},{1,9},{2,10},{3,11},{4,12},{5,13},{6,14},{7,15},{8,0},{9,1},... | collective-permute-start | bytes 786440 | tf_op jit(solution)/shard_map/ppermute | solution.py:418
  38.4 0.8 copy-start.15
  39.2 7.5 %collective-permute-start.2 = (f32[1,256,256]{2,1,0:T(8,128)}, f32[1,256,256]{2,1,0:T(8,128)}, u32[]{:S(2)}, u32[]{:S(2)}) collective-permute-start(f32[1,256,256]{2,1,0:T(8,128)} %slice_add_fusion.28), channel_id=1, source_target_pairs={{0,16},{1,17},{2,18},{3,19},{4,20},{5,21},{6,22},{7,23},{8,24},{9,... | collective-permute-start | bytes 786440 | tf_op jit(solution)/shard_map/ppermute | solution.py:418
  46.7 1.2 copy-start.10
  47.9 1.0 copy-start.14
  49.0 1.0 copy-start.16
  50.0 1.0 copy-start.17
  56.9 15.1 %collective-permute-start.6 = (f32[16,128,256]{2,1,0:T(8,128)S(1)}, f32[16,128,256]{2,1,0:T(8,128)S(1)}, u32[]{:S(2)}, u32[]{:S(2)}) collective-permute-start(f32[16,128,256]{2,1,0:T(8,128)S(1)} %shard_map.73), channel_id=1, source_target_pairs={{0,4},{1,5},{2,6},{3,7},{4,0},{5,1},{6,2},{7,3},{8,12},{9,13},{10,... | collective-permute-start | bytes 6291464 | tf_op jit(solution)/shard_map/ppermute | solution.py:418
  61.6 14.8 %collective-permute-start.17 = (f32[16,128,256]{2,1,0:T(8,128)S(1)}, f32[16,128,256]{2,1,0:T(8,128)S(1)}, u32[]{:S(2)}, u32[]{:S(2)}) collective-permute-start(f32[16,128,256]{2,1,0:T(8,128)S(1)} %shard_map.82), channel_id=1, source_target_pairs={{0,4},{1,5},{2,6},{3,7},{4,0},{5,1},{6,2},{7,3},{8,12},{9,13},{10,... | collective-permute-start | bytes 6291464 | tf_op jit(solution)/shard_map/ppermute | solution.py:418
  66.7 15.8 %collective-permute-start.12 = (f32[16,128,256]{2,1,0:T(8,128)S(1)}, f32[16,128,256]{2,1,0:T(8,128)S(1)}, u32[]{:S(2)}, u32[]{:S(2)}) collective-permute-start(f32[16,128,256]{2,1,0:T(8,128)S(1)} %shard_map.78), channel_id=1, source_target_pairs={{0,4},{1,5},{2,6},{3,7},{4,0},{5,1},{6,2},{7,3},{8,12},{9,13},{10,... | collective-permute-start | bytes 6291464 | tf_op jit(solution)/shard_map/ppermute | solution.py:418
  71.4 17.2 %collective-permute-start.7 = (f32[16,128,256]{2,1,0:T(8,128)S(1)}, f32[16,128,256]{2,1,0:T(8,128)S(1)}, u32[]{:S(2)}, u32[]{:S(2)}) collective-permute-start(f32[16,128,256]{2,1,0:T(8,128)S(1)} %shard_map.75), channel_id=1, source_target_pairs={{0,4},{1,5},{2,6},{3,7},{4,0},{5,1},{6,2},{7,3},{8,12},{9,13},{10,... | collective-permute-start | bytes 6291464 | tf_op jit(solution)/shard_map/ppermute | solution.py:418
  75.7 30.1 %collective-permute-start.22 = (f32[8,128,256]{2,1,0:T(8,128)}, f32[8,128,256]{2,1,0:T(8,128)}, u32[]{:S(2)}, u32[]{:S(2)}) collective-permute-start(f32[8,128,256]{2,1,0:T(8,128)} %slice_add_fusion), channel_id=1, source_target_pairs={{0,8},{1,9},{2,10},{3,11},{4,12},{5,13},{6,14},{7,15},{8,0},{9,1},... | collective-permute-start | bytes 3145736 | tf_op jit(solution)/shard_map/ppermute | solution.py:418
  76.4 3.5 %copy-start.6 = (f32[16,128,256]{2,1,0:T(8,128)}, f32[16,128,256]{2,1,0:T(8,128)S(1)}, u32[]{:S(2)}) copy-start(f32[16,128,256]{2,1,0:T(8,128)S(1)} %collective-permute-done.17.refs_6_.refs_1_) | copy-start | bytes 6291460
  80.9 26.8 %collective-permute-start.18 = (f32[8,128,256]{2,1,0:T(8,128)}, f32[8,128,256]{2,1,0:T(8,128)}, u32[]{:S(2)}, u32[]{:S(2)}) collective-permute-start(f32[8,128,256]{2,1,0:T(8,128)} %slice_add_fusion.1), channel_id=1, source_target_pairs={{0,1},{1,0},{2,3},{3,2},{4,5},{5,4},{6,7},{7,6},{8,9},{9,8},{10,11... | collective-permute-start | bytes 3145736 | tf_op jit(solution)/shard_map/ppermute | solution.py:418
  82.5 3.4 %copy-start.2 = (f32[16,128,256]{2,1,0:T(8,128)}, f32[16,128,256]{2,1,0:T(8,128)S(1)}, u32[]{:S(2)}) copy-start(f32[16,128,256]{2,1,0:T(8,128)S(1)} %collective-permute-done.12.refs_6_.refs_7_) | copy-start | bytes 6291460
  87.1 26.4 %collective-permute-start.13 = (f32[8,128,256]{2,1,0:T(8,128)}, f32[8,128,256]{2,1,0:T(8,128)}, u32[]{:S(2)}, u32[]{:S(2)}) collective-permute-start(f32[8,128,256]{2,1,0:T(8,128)} %slice_add_fusion.2), channel_id=1, source_target_pairs={{0,16},{1,17},{2,18},{3,19},{4,20},{5,21},{6,22},{7,23},{8,24},{9,... | collective-permute-start | bytes 3145736 | tf_op jit(solution)/shard_map/ppermute | solution.py:418
  88.6 3.4 %copy-start.4 = (f32[16,128,256]{2,1,0:T(8,128)}, f32[16,128,256]{2,1,0:T(8,128)S(1)}, u32[]{:S(2)}) copy-start(f32[16,128,256]{2,1,0:T(8,128)S(1)} %collective-permute-done.7.refs_6_.refs_1_) | copy-start | bytes 6291460
  93.2 31.3 %collective-permute-start.8 = (f32[8,128,256]{2,1,0:T(8,128)}, f32[8,128,256]{2,1,0:T(8,128)}, u32[]{:S(2)}, u32[]{:S(2)}) collective-permute-start(f32[8,128,256]{2,1,0:T(8,128)} %slice_add_fusion.3), channel_id=1, source_target_pairs={{0,8},{1,9},{2,10},{3,11},{4,12},{5,13},{6,14},{7,15},{8,0},{9,1},... | collective-permute-start | bytes 3145736 | tf_op jit(solution)/shard_map/ppermute | solution.py:418
  103.0 4.7 %copy-start.7 = (f32[16,128,256]{2,1,0:T(8,128)S(1)}, f32[16,128,256]{2,1,0:T(8,128)}, u32[]{:S(2)}) copy-start(f32[16,128,256]{2,1,0:T(8,128)} %copy-done.6) | copy-start | bytes 6291460
  105.8 7.7 %copy-start.3 = (f32[16,128,256]{2,1,0:T(8,128)S(1)}, f32[16,128,256]{2,1,0:T(8,128)}, u32[]{:S(2)}) copy-start(f32[16,128,256]{2,1,0:T(8,128)} %copy-done.2) | copy-start | bytes 6291460
  107.1 17.4 %copy-start.5 = (f32[16,128,256]{2,1,0:T(8,128)S(1)}, f32[16,128,256]{2,1,0:T(8,128)}, u32[]{:S(2)}) copy-start(f32[16,128,256]{2,1,0:T(8,128)} %copy-done.4) | copy-start | bytes 6291460
  107.1 20.2 %collective-permute-start.23 = (f32[4,128,256]{2,1,0:T(8,128)S(1)}, f32[4,128,256]{2,1,0:T(8,128)S(1)}, u32[]{:S(2)}, u32[]{:S(2)}) collective-permute-start(f32[4,128,256]{2,1,0:T(8,128)S(1)} %slice_add_fusion.4), channel_id=1, source_target_pairs={{0,16},{1,17},{2,18},{3,19},{4,20},{5,21},{6,22},{7,23},{8,24},{9,... | collective-permute-start | bytes 1572872 | tf_op jit(solution)/shard_map/ppermute | solution.py:418
  108.9 25.9 %collective-permute-start.19 = (f32[4,128,256]{2,1,0:T(8,128)S(1)}, f32[4,128,256]{2,1,0:T(8,128)S(1)}, u32[]{:S(2)}, u32[]{:S(2)}) collective-permute-start(f32[4,128,256]{2,1,0:T(8,128)S(1)} %slice_add_fusion.6), channel_id=1, source_target_pairs={{0,8},{1,9},{2,10},{3,11},{4,12},{5,13},{6,14},{7,15},{8,0},{9,1},... | collective-permute-start | bytes 1572872 | tf_op jit(solution)/shard_map/ppermute | solution.py:418
  114.6 22.8 %collective-permute-start.14 = (f32[4,128,256]{2,1,0:T(8,128)S(1)}, f32[4,128,256]{2,1,0:T(8,128)S(1)}, u32[]{:S(2)}, u32[]{:S(2)}) collective-permute-start(f32[4,128,256]{2,1,0:T(8,128)S(1)} %slice_add_fusion.8), channel_id=1, source_target_pairs={{0,1},{1,0},{2,3},{3,2},{4,5},{5,4},{6,7},{7,6},{8,9},{9,8},{10,11... | collective-permute-start | bytes 1572872 | tf_op jit(solution)/shard_map/ppermute | solution.py:418
  125.7 15.4 %collective-permute-start.9 = (f32[4,128,256]{2,1,0:T(8,128)S(1)}, f32[4,128,256]{2,1,0:T(8,128)S(1)}, u32[]{:S(2)}, u32[]{:S(2)}) collective-permute-start(f32[4,128,256]{2,1,0:T(8,128)S(1)} %slice_add_fusion.10), channel_id=1, source_target_pairs={{0,16},{1,17},{2,18},{3,19},{4,20},{5,21},{6,22},{7,23},{8,24},{9,... | collective-permute-start | bytes 1572872 | tf_op jit(solution)/shard_map/ppermute | solution.py:418
  128.3 15.4 %collective-permute-start.24 = (f32[2,128,256]{2,1,0:T(8,128)S(1)}, f32[2,128,256]{2,1,0:T(8,128)S(1)}, u32[]{:S(2)}, u32[]{:S(2)}) collective-permute-start(f32[2,128,256]{2,1,0:T(8,128)S(1)} %slice_add_fusion.14), channel_id=1, source_target_pairs={{0,1},{1,0},{2,3},{3,2},{4,5},{5,4},{6,7},{7,6},{8,9},{9,8},{10,11... | collective-permute-start | bytes 786440 | tf_op jit(solution)/shard_map/ppermute | solution.py:418
  135.8 9.3 %collective-permute-start.20 = (f32[2,128,256]{2,1,0:T(8,128)S(1)}, f32[2,128,256]{2,1,0:T(8,128)S(1)}, u32[]{:S(2)}, u32[]{:S(2)}) collective-permute-start(f32[2,128,256]{2,1,0:T(8,128)S(1)} %slice_add_fusion.17), channel_id=1, source_target_pairs={{0,16},{1,17},{2,18},{3,19},{4,20},{5,21},{6,22},{7,23},{8,24},{9,... | collective-permute-start | bytes 786440 | tf_op jit(solution)/shard_map/ppermute | solution.py:418
  138.4 20.6 %collective-permute-start.15 = (f32[2,128,256]{2,1,0:T(8,128)S(1)}, f32[2,128,256]{2,1,0:T(8,128)S(1)}, u32[]{:S(2)}, u32[]{:S(2)}) collective-permute-start(f32[2,128,256]{2,1,0:T(8,128)S(1)} %slice_add_fusion.20), channel_id=1, source_target_pairs={{0,2},{1,3},{2,0},{3,1},{4,6},{5,7},{6,4},{7,5},{8,10},{9,11},{10,... | collective-permute-start | bytes 786440 | tf_op jit(solution)/shard_map/ppermute | solution.py:418
  142.1 22.6 %collective-permute-start.10 = (f32[2,128,256]{2,1,0:T(8,128)S(1)}, f32[2,128,256]{2,1,0:T(8,128)S(1)}, u32[]{:S(2)}, u32[]{:S(2)}) collective-permute-start(f32[2,128,256]{2,1,0:T(8,128)S(1)} %slice_add_fusion.23), channel_id=1, source_target_pairs={{0,1},{1,0},{2,3},{3,2},{4,5},{5,4},{6,7},{7,6},{8,9},{9,8},{10,11... | collective-permute-start | bytes 786440 | tf_op jit(solution)/shard_map/ppermute | solution.py:418
  144.7 17.1 %collective-permute-start.25 = (f32[1,128,256]{2,1,0:T(8,128)S(1)}, f32[1,128,256]{2,1,0:T(8,128)S(1)}, u32[]{:S(2)}, u32[]{:S(2)}) collective-permute-start(f32[1,128,256]{2,1,0:T(8,128)S(1)} %slice_add_fusion.30), channel_id=1, source_target_pairs={{0,2},{1,3},{2,0},{3,1},{4,6},{5,7},{6,4},{7,5},{8,10},{9,11},{10,... | collective-permute-start | bytes 393224 | tf_op jit(solution)/shard_map/ppermute | solution.py:418
  146.1 17.4 %collective-permute-start.21 = (f32[1,128,256]{2,1,0:T(8,128)S(1)}, f32[1,128,256]{2,1,0:T(8,128)S(1)}, u32[]{:S(2)}, u32[]{:S(2)}) collective-permute-start(f32[1,128,256]{2,1,0:T(8,128)S(1)} %slice_add_fusion.34), channel_id=1, source_target_pairs={{0,2},{1,3},{2,0},{3,1},{4,6},{5,7},{6,4},{7,5},{8,10},{9,11},{10,... | collective-permute-start | bytes 393224 | tf_op jit(solution)/shard_map/ppermute | solution.py:418
  160.0 5.8 %collective-permute-start.16 = (f32[1,128,256]{2,1,0:T(8,128)S(1)}, f32[1,128,256]{2,1,0:T(8,128)S(1)}, u32[]{:S(2)}, u32[]{:S(2)}) collective-permute-start(f32[1,128,256]{2,1,0:T(8,128)S(1)} %slice_add_fusion.38), channel_id=1, source_target_pairs={{0,8},{1,9},{2,10},{3,11},{4,12},{5,13},{6,14},{7,15},{8,0},{9,1},... | collective-permute-start | bytes 393224 | tf_op jit(solution)/shard_map/ppermute | solution.py:418
  164.6 15.1 %collective-permute-start.27 = (f32[256,256]{1,0:T(8,128)S(1)}, f32[256,256]{1,0:T(8,128)S(1)}, u32[]{:S(2)}, u32[]{:S(2)}) collective-permute-start(f32[256,256]{1,0:T(8,128)S(1)} %shard_map.86.refs_1_), channel_id=1, source_target_pairs={{0,4},{1,5},{2,6},{3,7},{4,0},{5,1},{6,2},{7,3},{8,12},{9,13},{10,... | collective-permute-start | bytes 786440 | tf_op jit(solution)/shard_map/ppermute | solution.py:418
  165.7 16.3 %copy-start.12 = (f32[256,1536]{1,0:T(8,128)S(1)}, f32[256,1536]{1,0:T(8,128)}, u32[]{:S(2)}) copy-start(f32[256,1536]{1,0:T(8,128)} %copy-done.11) | copy-start | bytes 4718596
  165.7 9.7 %collective-permute-start.11 = (f32[1,128,256]{2,1,0:T(8,128)S(1)}, f32[1,128,256]{2,1,0:T(8,128)S(1)}, u32[]{:S(2)}, u32[]{:S(2)}) collective-permute-start(f32[1,128,256]{2,1,0:T(8,128)S(1)} %slice_add_fusion.42), channel_id=1, source_target_pairs={{0,2},{1,3},{2,0},{3,1},{4,6},{5,7},{6,4},{7,5},{8,10},{9,11},{10,... | collective-permute-start | bytes 393224 | tf_op jit(solution)/shard_map/ppermute | solution.py:418
  177.2 5.2 %collective-permute-start.26 = (f32[256,256]{1,0:T(8,128)}, f32[256,256]{1,0:T(8,128)}, u32[]{:S(2)}, u32[]{:S(2)}) collective-permute-start(f32[256,256]{1,0:T(8,128)} %shard_map.80.refs_0_), channel_id=1, source_target_pairs={{0,4},{1,5},{2,6},{3,7},{4,0},{5,1},{6,2},{7,3},{8,12},{9,13},{10,... | collective-permute-start | bytes 786440 | tf_op jit(solution)/shard_map/ppermute | solution.py:418
  177.2 14.4 %collective-permute-start.29 = (f32[256,256]{1,0:T(8,128)S(1)}, f32[256,256]{1,0:T(8,128)}, u32[]{:S(2)}, u32[]{:S(2)}) collective-permute-start(f32[256,256]{1,0:T(8,128)S(1)} %shard_map.86.refs_1_), channel_id=1, source_target_pairs={{0,8},{1,9},{2,10},{3,11},{4,12},{5,13},{6,14},{7,15},{8,0},{9,1},... | collective-permute-start | bytes 786440 | tf_op jit(solution)/shard_map/ppermute | solution.py:418
  177.8 13.9 %collective-permute-start.31 = (f32[256,256]{1,0:T(8,128)S(1)}, f32[256,256]{1,0:T(8,128)}, u32[]{:S(2)}, u32[]{:S(2)}) collective-permute-start(f32[256,256]{1,0:T(8,128)S(1)} %shard_map.86.refs_1_), channel_id=1, source_target_pairs={{0,16},{1,17},{2,18},{3,19},{4,20},{5,21},{6,22},{7,23},{8,24},{9,... | collective-permute-start | bytes 786440 | tf_op jit(solution)/shard_map/ppermute | solution.py:418
  178.4 13.3 %collective-permute-start.28 = (f32[256,256]{1,0:T(8,128)}, f32[256,256]{1,0:T(8,128)}, u32[]{:S(2)}, u32[]{:S(2)}) collective-permute-start(f32[256,256]{1,0:T(8,128)} %shard_map.80.refs_0_), channel_id=1, source_target_pairs={{0,8},{1,9},{2,10},{3,11},{4,12},{5,13},{6,14},{7,15},{8,0},{9,1},... | collective-permute-start | bytes 786440 | tf_op jit(solution)/shard_map/ppermute | solution.py:418
  180.5 11.5 %collective-permute-start.30 = (f32[256,256]{1,0:T(8,128)}, f32[256,256]{1,0:T(8,128)}, u32[]{:S(2)}, u32[]{:S(2)}) collective-permute-start(f32[256,256]{1,0:T(8,128)} %shard_map.80.refs_0_), channel_id=1, source_target_pairs={{0,16},{1,17},{2,18},{3,19},{4,20},{5,21},{6,22},{7,23},{8,24},{9,... | collective-permute-start | bytes 786440 | tf_op jit(solution)/shard_map/ppermute | solution.py:418
  182.5 4.6 %copy-start.1 = (bf16[1,2,768,4096]{3,2,1,0:T(8,128)(2,1)S(1)}, bf16[1,2,768,4096]{3,2,1,0:T(8,128)(2,1)}, u32[]{:S(2)}) copy-start(bf16[1,2,768,4096]{3,2,1,0:T(8,128)(2,1)} %param.7) | copy-start | bytes 37748740
  187.1 0.9 copy-start.19
  188.0 17.7 %slice-start.3 = ((s8[12582912]{0:T(1024)(128)(4,1)}), s8[4194304]{0:T(1024)(128)(4,1)S(1)}, s32[]{:S(2)}) async-start(s8[12582912]{0:T(1024)(128)(4,1)} %bitcast.22), calls=%async_computation.3 | async-start | bytes 8388608
  188.0 17.7 %slice-start.4 = ((s8[12582912]{0:T(1024)(128)(4,1)}), s8[4194304]{0:T(1024)(128)(4,1)S(1)}, s32[]{:S(2)}) async-start(s8[12582912]{0:T(1024)(128)(4,1)} %bitcast.22), calls=%async_computation.4 | async-start | bytes 8388608
  191.9 13.8 %slice-start.5 = ((s8[12582912]{0:T(1024)(128)(4,1)}), s8[4194304]{0:T(1024)(128)(4,1)S(1)}, s32[]{:S(2)}) async-start(s8[12582912]{0:T(1024)(128)(4,1)} %bitcast.22), calls=%async_computation.5 | async-start | bytes 8388608
  195.5 11.1 %collective-permute-start.34 = (f32[2,512,256]{2,1,0:T(8,128)S(1)}, f32[2,512,256]{2,1,0:T(8,128)S(1)}, u32[]{:S(2)}, u32[]{:S(2)}) collective-permute-start(f32[2,512,256]{2,1,0:T(8,128)S(1)} %get-tuple-element.27), channel_id=1, source_target_pairs={{0,4},{1,5},{2,6},{3,7},{4,0},{5,1},{6,2},{7,3},{8,12},{9,13},{10,... | collective-permute-start | bytes 3145736 | tf_op jit(solution)/shard_map/ppermute | solution.py:418
  195.5 8.9 %collective-permute-start.33 = (f32[256,256]{1,0:T(8,128)}, f32[256,256]{1,0:T(8,128)S(1)}, u32[]{:S(2)}, u32[]{:S(2)}) collective-permute-start(f32[256,256]{1,0:T(8,128)} %collective-permute-done.31.refs_3_), channel_id=1, source_target_pairs={{0,8},{1,9},{2,10},{3,11},{4,12},{5,13},{6,14},{7,15},{8,0},{9,1},... | collective-permute-start | bytes 786440 | tf_op jit(solution)/shard_map/ppermute | solution.py:418
  197.0 8.6 %collective-permute-start.32 = (f32[256,256]{1,0:T(8,128)}, f32[256,256]{1,0:T(8,128)S(1)}, u32[]{:S(2)}, u32[]{:S(2)}) collective-permute-start(f32[256,256]{1,0:T(8,128)} %collective-permute-done.28.refs_0_), channel_id=1, source_target_pairs={{0,16},{1,17},{2,18},{3,19},{4,20},{5,21},{6,22},{7,23},{8,24},{9,... | collective-permute-start | bytes 786440 | tf_op jit(solution)/shard_map/ppermute | solution.py:418
  206.6 2.7 %collective-permute-start.35 = (f32[1,512,256]{2,1,0:T(8,128)S(1)}, f32[1,512,256]{2,1,0:T(8,128)S(1)}, u32[]{:S(2)}, u32[]{:S(2)}) collective-permute-start(f32[1,512,256]{2,1,0:T(8,128)S(1)} %get-tuple-element.30), channel_id=1, source_target_pairs={{0,4},{1,5},{2,6},{3,7},{4,0},{5,1},{6,2},{7,3},{8,12},{9,13},{10,... | collective-permute-start | bytes 1572872 | tf_op jit(solution)/shard_map/ppermute | solution.py:418
  206.7 2.6 %slice-start.6 = ((s8[4718592]{0:T(1024)(128)(4,1)}), s8[4194304]{0:T(1024)(128)(4,1)S(1)}, s32[]{:S(2)}) async-start(s8[4718592]{0:T(1024)(128)(4,1)} %bitcast.29), calls=%async_computation.6 | async-start | bytes 8388608
  206.7 3.0 %slice-start.7 = ((s8[4718592]{0:T(1024)(128)(4,1)}), s8[524288]{0:T(1024)(128)(4,1)S(1)}, s32[]{:S(2)}) async-start(s8[4718592]{0:T(1024)(128)(4,1)} %bitcast.29), calls=%async_computation.7 | async-start | bytes 1048576
  (1 other events, 0.7 us)
where the time goes:
time: 216 us; the launch traced here: 214 us
  Pallas kernels  70.7 us (33%)
  waiting for transfers between devices  65.8 us (30%)
  starting transfers between devices  35.6 us (16%)
  local copies, waits for them, and re-layouts  21.9 us (10%)
  other arithmetic  19 us (9%)
    pallas_call x24, Pallas kernels, run(): pl.pallas_call(body, grid_spec=pltpu.PrefetchScalarGridSpec(num_scalar_pr...  70.7 us
    ppermute x36, waiting for transfers between devices, exchange(): lax.ppermute(array, AXES, [(w, w ^ 1 << bit) for w in range(devices)])  65.8 us
    ppermute x36, starting transfers between devices, exchange(): lax.ppermute(array, AXES, [(w, w ^ 1 << bit) for w in range(devices)])  35.6 us
    unnamed x58, local copies, waits for them, and re-layouts  21.4 us
    add x14, other arithmetic, halved(): terms.append(exchange(sum((term[half:2 * half] for term in terms)), bit))  14.3 us
    add x6, other arithmetic, halved(): terms = [kept, arrived, exchange(away + arrived[half:], order[0])]  4.69 us
  transfers between devices with their start and end apart: 36, of which 14 were waited for; matrix products, arithmetic and copies ran while one was open for 9% of the time, Pallas kernels for 25%

commit v1 on v0

--- a/solution.py
+++ b/solution.py
@@ -187,6 +187,7 @@
         0,
         16 * seed.size,
         prefetch=0,
+        room=40 * MIB,
     )(seed, *flat)
 
 
@@ -244,23 +245,31 @@
     )(*flat)
 
 
-def shared_kernel(group, rows, pieces, me_ref, *refs):
+def shared_kernel(group, rows, pieces, arrived, me_ref, *refs):
     tiles, refs = refs[:group], refs[group:]
-    seed_ref, out_ref, high_ref, low_ref, seed_high_ref, seed_low_ref = refs
+    seed_ref, *received, out_ref, parts_ref, seed_parts_ref = refs
+    depth = seed_ref.shape[0]
 
     @pl.when(pl.program_id(0) == 0)
     def _():
-        seed_high_ref[...], seed_low_ref[...] = split(seed_ref[...])
+        high, low = split(seed_ref[...])
+        seed_parts_ref[:depth] = high
+        seed_parts_ref[depth : 2 * depth] = high
+        seed_parts_ref[2 * depth :] = low
 
     for g in range(group):
         place = pl.ds(g * rows, rows)
-        high_ref[place], low_ref[place] = split(rows_of(tiles[g], rows, pieces))
-    total = dot3((high_ref[...], low_ref[...]), (seed_high_ref[...], seed_low_ref[...]))
+        high, low = split(rows_of(tiles[g], rows, pieces))
+        parts_ref[place, :depth] = high
+        parts_ref[place, depth : 2 * depth] = low
+        parts_ref[place, 2 * depth :] = high
+    total = dot(parts_ref[...], seed_parts_ref[...])
     for g in range(group):
-        out_ref[g] = total[g * rows : (g + 1) * rows]
-
-
-def shared_products(me, tiles, seed, bits, base, offset, rows, earlier):
+        term = total[g * rows : (g + 1) * rows]
+        out_ref[g] = term + received[0][g] if arrived else term
+
+
+def shared_products(me, tiles, seed, bits, base, offset, rows, received=None, earlier=()):
     depth, count = seed.shape
     lanes = tiles.shape[2]
     pieces = depth // lanes
@@ -270,24 +279,26 @@
     def place(g, f, me_ref):
         return (spread(bits, f * group + g) | base) ^ me_ref[0], offset // rows, 0
 
-    halves = pltpu.VMEM((group * rows, depth), BF16)
-    seed_halves = pltpu.VMEM((depth, count), BF16)
+    in_specs = [
+        pl.BlockSpec((1, rows * pieces, lanes), functools.partial(place, g)) for g in range(group)
+    ] + [pl.BlockSpec((depth, count), lambda f, me_ref: (0, 0))]
+    operands = [tiles] * group + [seed]
+    if received is not None:
+        skip = received.shape[0] // group - units // group
+        in_specs.append(pl.BlockSpec((group, rows, count), lambda f, me_ref: (skip + f, 0, 0)))
+        operands.append(received)
     return call(
-        functools.partial(shared_kernel, group, rows, pieces),
+        functools.partial(shared_kernel, group, rows, pieces, received is not None),
         (units // group,),
-        [
-            pl.BlockSpec((1, rows * pieces, lanes), functools.partial(place, g))
-            for g in range(group)
-        ]
-        + [pl.BlockSpec((depth, count), lambda f, me_ref: (0, 0))],
+        in_specs,
         pl.BlockSpec((group, rows, count), lambda f, me_ref: (f, 0, 0)),
         jax.ShapeDtypeStruct((units, rows, count), F32),
         6 * units * rows * depth * count,
         4 * units * rows * (depth + count),
-        scratch=[halves, halves, seed_halves, seed_halves],
+        scratch=[pltpu.VMEM((group * rows, 3 * depth), BF16), pltpu.VMEM((3 * depth, count), BF16)],
         room=34 * MIB,
         earlier=earlier,
-    )(me, *([tiles] * group), seed)
+    )(me, *operands)
 
 
 def coupled_kernel(units, halves, aliased, last, me_ref, coupling_ref, start_ref, *refs):
@@ -397,6 +408,7 @@
         flops,
         moved,
         scratch=scratch,
+        room=52 * MIB,
         **more,
     )(me, *operands)
 
@@ -420,13 +432,12 @@
     flat_coupling = coupling[0].reshape(blocks * width, shard_cols)
     first, half = first_of(private_seeds[0, 0], private_inverse[0, 0])
 
-    def halved(own, arrived, order):
-        away, kept = own
-        half = away.shape[0]
-        terms = [kept, arrived, exchange(away + arrived[half:], order[0])]
-        for bit in order[1:]:
-            half = terms[-1].shape[0] // 2
-            terms.append(exchange(sum(term[half : 2 * half] for term in terms), bit))
+    def halved(away, terms, order):
+        for step, bit in enumerate(order):
+            if step > 0:
+                half = terms[-1].shape[0] // 2
+                away = sum(term[half : 2 * half] for term in terms)
+            terms = terms + [exchange(away, bit)]
         return terms
 
     core = col_bits
@@ -443,8 +454,8 @@
     reduced = reduced_of(
         shared_seed[0],
         [
-            halved((kept[kept.shape[0] // 2 :], kept), away, order)
-            for kept, away, order in zip(own, arrived, orders)
+            halved(sum(term[term.shape[0] // 2 :] for term in pair), list(pair), order)
+            for *pair, order in zip(own, arrived, orders)
         ],
     )
 
@@ -459,17 +470,20 @@
     pieces = depth // lanes
     rows = sub // len(orders)
 
-    def products(chunk, bits, base, *earlier):
-        return shared_products(me, tiles, reduced, bits, base, chunk * rows, rows, earlier)
-
-    arrived = [
-        exchange(products(chunk, order, 1 << core), core) for chunk, order in enumerate(orders)
+    def products(chunk, base, received=None, earlier=()):
+        bits = orders[chunk] if base == 1 << core else orders[chunk][1:]
+        return shared_products(
+            me, tiles, reduced, bits, base, chunk * rows, rows, received, earlier
+        )
+
+    arrived = [exchange(products(chunk, 1 << core), core) for chunk in range(len(orders))]
+    away = [
+        products(chunk, 1 << order[0], arrived[chunk]) for chunk, order in enumerate(orders)
     ]
     shares = []
     for chunk, order in enumerate(orders):
-        away = products(chunk, order[1:], 1 << order[0], arrived[chunk])
-        kept = products(chunk, order[1:], 0, arrived[-1])
-        shares.append(halved((away, kept), arrived[chunk], order))
+        kept = products(chunk, 0, earlier=away)
+        shares.append(halved(away[chunk], [kept, arrived[chunk]], order))
 
     near = []
     for part, way in enumerate((outer, outer[::-1])):
@@ -488,13 +502,11 @@
 
     own = [held[0] for held in near]
     second, adjoint, _ = take([0, 1], [own, [exchange(piece, core) for piece in own]])
-    second, adjoint, packed = take(middle, [[held[number] for held in near] for number in middle])
-    far = exchange(packed, core)
+    far = [[exchange(held[number], core) for held in near] for number in middle]
+    second, adjoint, _ = take(middle, [[held[number] for held in near] for number in middle])
     second, adjoint, packed = take([last], [[held[last] for held in near]])
     far_last = exchange(packed, core)
-    second, adjoint, _ = take(
-        [number | 1 for number in middle], [[far[g]] for g in range(len(middle))]
-    )
+    second, adjoint, _ = take([number | 1 for number in middle], far)
     second, adjoint = take([last | 1], [[far_last[0]]], inverse)
     return second[None, None], adjoint[None]
 

time: 216 us -> 203 us (0.940)
  waiting for transfers between devices: 65.8 us -> 47.8 us
  Pallas kernels: 70.7 us -> 81.7 us
  local copies, waits for them, and re-layouts: 21.9 us -> 15.5 us
  starting transfers between devices: 35.6 us -> 41.2 us
  other arithmetic: 19 us -> 14.4 us
    ppermute x36 -> x39, waiting for transfers between devices: 65.8 us -> 47.8 us  [exchange(): lax.ppermute(array, AXES, [(w, w ^ 1 << bit) for w in range(devices)])]
    pallas_call x24, Pallas kernels: 70.7 us -> 81.7 us  [run(): pl.pallas_call(body, grid_spec=pltpu.PrefetchScalarGridSpec(num_scalar_pr...]
    unnamed x58 -> x34, local copies, waits for them, and re-layouts: 21.4 us -> 13.9 us
    ppermute x36 -> x39, starting transfers between devices: 35.6 us -> 41.2 us  [exchange(): lax.ppermute(array, AXES, [(w, w ^ 1 << bit) for w in range(devices)])]
    add x20 -> x16, other arithmetic: 19 us -> 14.4 us  [the longest x14 14.3 us: halved(): away = sum((term[half:2 * half] for term in terms))]
  transfers between devices with their start and end apart: 36 -> 39, of which waited for: 14 -> 17; matrix products, arithmetic and copies ran while one was open for 9% -> 8% of each run, Pallas kernels for 25% -> 30%
where the time goes in v1:
time: 203 us; the launch traced here: 202 us
  Pallas kernels  81.7 us (40%)
  waiting for transfers between devices  47.8 us (24%)
  starting transfers between devices  41.2 us (20%)
  local copies, waits for them, and re-layouts  15.5 us (8%)
  other arithmetic  14.4 us (7%)
    pallas_call x24, Pallas kernels, run(): pl.pallas_call(body, grid_spec=pltpu.PrefetchScalarGridSpec(num_scalar_pr...  81.7 us
    ppermute x39, waiting for transfers between devices, exchange(): lax.ppermute(array, AXES, [(w, w ^ 1 << bit) for w in range(devices)])  47.8 us
    ppermute x39, starting transfers between devices, exchange(): lax.ppermute(array, AXES, [(w, w ^ 1 << bit) for w in range(devices)])  41.2 us
    add x14, other arithmetic, halved(): away = sum((term[half:2 * half] for term in terms))  14.3 us
    unnamed x34, local copies, waits for them, and re-layouts  13.9 us
  transfers between devices with their start and end apart: 39, of which 17 were waited for; matrix products, arithmetic and copies ran while one was open for 8% of the time, Pallas kernels for 30%

profile of v1, /device:TPU:0, one launch (start us, length us, event | category | flops | bytes accessed | tf_op | source)
XLA Modules:
  0.0 201.8 jit_solution(7444304541490198007)
XLA Ops:
  0.6 2.3 %copy-done.3 = f32[1,1,2,768,768]{4,3,2,1,0:T(8,128)S(1)} copy-done((f32[1,1,2,768,768]{4,3,2,1,0:T(8,128)S(1)}, f32[1,1,2,768,768]{4,3,2,1,0:T(8,128)}, u32[]{:S(2)}) %copy-start.3) | copy-done | bytes 4718616
  3.0 1.4 copy-done.13
  4.4 1.8 shard_map.68
  7.4 4.6 %copy-done = bf16[1,2,768,4096]{3,2,1,0:T(8,128)(2,1)S(1)} copy-done((bf16[1,2,768,4096]{3,2,1,0:T(8,128)(2,1)S(1)}, bf16[1,2,768,4096]{3,2,1,0:T(8,128)(2,1)}, u32[]{:S(2)}) %copy-start) | copy-done | bytes 12582936
  12.0 2.1 %shard_map.70 = f32[4,256,256]{2,1,0:T(8,128)S(1)} custom-call(s32[1]{0:T(128)} %bitcast.me_ref, bf16[1536,4096]{1,0:T(8,128)(2,1)S(1)} %bitcast.16, bf16[256,1536]{1,0:T(8,128)(2,1)S(1)} %get-tuple-element.18.half_ref), custom_call_target="tpu_custom_call" | custom-call | flops 805306368 | bytes 4194304 | tf_op jit(solution)/shard_map/pallas_call | solution.py:55
  14.6 2.1 %shard_map.71 = f32[4,256,256]{2,1,0:T(8,128)S(1)} custom-call(s32[1]{0:T(128)} %bitcast.me_ref, bf16[1536,4096]{1,0:T(8,128)(2,1)S(1)} %bitcast.17, bf16[256,1536]{1,0:T(8,128)(2,1)S(1)} %get-tuple-element.18.half_ref), custom_call_target="tpu_custom_call" | custom-call | flops 805306368 | bytes 4194304 | tf_op jit(solution)/shard_map/pallas_call | solution.py:55
  16.9 3.0 %shard_map.69 = (f32[4,256,256]{2,1,0:T(8,128)S(1)}, f32[4,256,256]{2,1,0:T(8,128)S(1)}) custom-call(s32[1]{0:T(128)} %bitcast.me_ref, bf16[1536,4096]{1,0:T(8,128)(2,1)S(1)} %bitcast.20, bf16[256,1536]{1,0:T(8,128)(2,1)S(1)} %get-tuple-element.18.half_ref), custom_call_target="tpu_custom_call" | custom-call | flops 1610612736 | bytes 8388608 | tf_op jit(solution)/shard_map/pallas_call | solution.py:55
  19.9 3.0 %collective-permute-start.1 = (f32[2,256,256]{2,1,0:T(8,128)S(1)}, f32[2,256,256]{2,1,0:T(8,128)S(1)}, u32[]{:S(2)}, u32[]{:S(2)}) collective-permute-start(f32[2,256,256]{2,1,0:T(8,128)S(1)} %slice_add_fusion.9), channel_id=1, source_target_pairs={{0,8},{1,9},{2,10},{3,11},{4,12},{5,13},{6,14},{7,15},{8,0},{9,1},... | collective-permute-start | bytes 1572872 | tf_op jit(solution)/shard_map/ppermute | solution.py:430
  23.0 1.6 collective-permute-start.4
  24.6 10.5 %collective-permute-done.1.refs_2_ = f32[2,256,256]{2,1,0:T(8,128)S(1)} collective-permute-done((f32[2,256,256]{2,1,0:T(8,128)S(1)}, f32[2,256,256]{2,1,0:T(8,128)S(1)}, u32[]{:S(2)}, u32[]{:S(2)}) %collective-permute-start.1) | collective-permute-done | bytes 524320 | tf_op jit(solution)/shard_map/ppermute | solution.py:430
  35.9 1.8 collective-permute-start.2
  38.6 1.5 collective-permute-start.5
  40.1 3.8 %collective-permute-done.2.refs_3_ = f32[1,256,256]{2,1,0:T(8,128)S(1)} collective-permute-done((f32[1,256,256]{2,1,0:T(8,128)}, f32[1,256,256]{2,1,0:T(8,128)S(1)}, u32[]{:S(2)}, u32[]{:S(2)}) %collective-permute-start.2) | collective-permute-done | bytes 262176 | tf_op jit(solution)/shard_map/ppermute | solution.py:430
  43.9 2.2 %collective-permute-done.5.refs_7_ = f32[1,256,256]{2,1,0:T(8,128)} collective-permute-done((f32[1,256,256]{2,1,0:T(8,128)}, f32[1,256,256]{2,1,0:T(8,128)}, u32[]{:S(2)}, u32[]{:S(2)}) %collective-permute-start.5) | collective-permute-done | bytes 262176 | tf_op jit(solution)/shard_map/ppermute | solution.py:430
  46.0 1.2 copy-done.5
  50.4 1.2 shard_map.72.refs_4_.refs_5_
  51.5 4.6 %shard_map.73 = f32[16,128,256]{2,1,0:T(8,128)S(1)} custom-call(s32[1]{0:T(128)} %bitcast.5.me_ref.refs_0_, f32[32,2048,128]{2,1,0:T(8,128)} %bitcast.26, f32[32,2048,128]{2,1,0:T(8,128)} %bitcast.27, f32[32,2048,128]{2,1,0:T(8,128)} %bitcast.28, f32[32,2048,128]{2,1,0:T(8,128)} %bitcast.29, f32[512,256]{1,0:T(8,128)S(1)} %shard_map.72.refs_4_.refs_5_), custom_call_target="tpu_custom_call" | custom-call | flops 1610612736 | bytes 6291456 | tf_op jit(solution)/shard_map/pallas_call | solution.py:55
  56.2 4.6 %shard_map.75 = f32[16,128,256]{2,1,0:T(8,128)S(1)} custom-call(s32[1]{0:T(128)} %bitcast.5.me_ref.refs_0_, f32[32,2048,128]{2,1,0:T(8,128)} %bitcast.30, f32[32,2048,128]{2,1,0:T(8,128)} %bitcast.31, f32[32,2048,128]{2,1,0:T(8,128)} %bitcast.32, f32[32,2048,128]{2,1,0:T(8,128)} %bitcast.33, f32[512,256]{1,0:T(8,128)S(1)} %shard_map.72.refs_4_.refs_5_), custom_call_target="tpu_custom_call" | custom-call | flops 1610612736 | bytes 6291456 | tf_op jit(solution)/shard_map/pallas_call | solution.py:55
  61.4 4.6 %shard_map.77 = f32[16,128,256]{2,1,0:T(8,128)S(1)} custom-call(s32[1]{0:T(128)} %bitcast.5.me_ref.refs_0_, f32[32,2048,128]{2,1,0:T(8,128)} %bitcast.34, f32[32,2048,128]{2,1,0:T(8,128)} %bitcast.35, f32[32,2048,128]{2,1,0:T(8,128)} %bitcast.36, f32[32,2048,128]{2,1,0:T(8,128)} %bitcast.37, f32[512,256]{1,0:T(8,128)S(1)} %shard_map.72.refs_4_.refs_5_), custom_call_target="tpu_custom_call" | custom-call | flops 1610612736 | bytes 6291456 | tf_op jit(solution)/shard_map/pallas_call | solution.py:55
  66.1 4.6 %shard_map.79 = f32[16,128,256]{2,1,0:T(8,128)S(1)} custom-call(s32[1]{0:T(128)} %bitcast.5.me_ref.refs_0_, f32[32,2048,128]{2,1,0:T(8,128)} %bitcast.38, f32[32,2048,128]{2,1,0:T(8,128)} %bitcast.39, f32[32,2048,128]{2,1,0:T(8,128)} %bitcast.40, f32[32,2048,128]{2,1,0:T(8,128)} %bitcast.41, f32[512,256]{1,0:T(8,128)S(1)} %shard_map.72.refs_4_.refs_5_), custom_call_target="tpu_custom_call" | custom-call | flops 1610612736 | bytes 6291456 | tf_op jit(solution)/shard_map/pallas_call | solution.py:55
  71.3 3.4 %shard_map.74.refs_6_ = f32[8,128,256]{2,1,0:T(8,128)} custom-call(s32[1]{0:T(128)} %bitcast.5.me_ref.refs_0_, f32[32,2048,128]{2,1,0:T(8,128)} %bitcast.42, f32[32,2048,128]{2,1,0:T(8,128)} %bitcast.43, f32[32,2048,128]{2,1,0:T(8,128)} %bitcast.44, f32[32,2048,128]{2,1,0:T(8,128)} %bitcast.45, f32[512,256]{1,0:T(8,128)S(1)} %shard_map.72.refs_4_.refs_5_, ...), custom_call_target="tpu_custom_call" | custom-call | flops 805306368 | bytes 3145728 | tf_op jit(solution)/shard_map/pallas_call | solution.py:55
  74.7 1.5 collective-permute-start.10
  76.2 3.4 %shard_map.76.refs_7_ = f32[8,128,256]{2,1,0:T(8,128)} custom-call(s32[1]{0:T(128)} %bitcast.5.me_ref.refs_0_, f32[32,2048,128]{2,1,0:T(8,128)} %bitcast.49, f32[32,2048,128]{2,1,0:T(8,128)} %bitcast.47, f32[32,2048,128]{2,1,0:T(8,128)} %bitcast.48, f32[32,2048,128]{2,1,0:T(8,128)} %bitcast.46, f32[512,256]{1,0:T(8,128)S(1)} %shard_map.72.refs_4_.refs_5_, ...), custom_call_target="tpu_custom_call" | custom-call | flops 805306368 | bytes 3145728 | tf_op jit(solution)/shard_map/pallas_call | solution.py:55
  80.2 4.2 %shard_map.78.refs_8_ = f32[8,128,256]{2,1,0:T(8,128)} custom-call(s32[1]{0:T(128)} %bitcast.5.me_ref.refs_0_, f32[32,2048,128]{2,1,0:T(8,128)} %bitcast.50, f32[32,2048,128]{2,1,0:T(8,128)} %bitcast.51, f32[32,2048,128]{2,1,0:T(8,128)} %bitcast.52, f32[32,2048,128]{2,1,0:T(8,128)} %bitcast.53, f32[512,256]{1,0:T(8,128)S(1)} %shard_map.72.refs_4_.refs_5_, ...), custom_call_target="tpu_custom_call" | custom-call | flops 805306368 | bytes 3145728 | tf_op jit(solution)/shard_map/pallas_call | solution.py:55
  84.4 1.6 collective-permute-start.18
  85.9 3.5 %shard_map.80.refs_9_ = f32[8,128,256]{2,1,0:T(8,128)} custom-call(s32[1]{0:T(128)} %bitcast.5.me_ref.refs_0_, f32[32,2048,128]{2,1,0:T(8,128)} %bitcast.54, f32[32,2048,128]{2,1,0:T(8,128)} %bitcast.55, f32[32,2048,128]{2,1,0:T(8,128)} %bitcast.56, f32[32,2048,128]{2,1,0:T(8,128)} %bitcast.57, f32[512,256]{1,0:T(8,128)S(1)} %shard_map.72.refs_4_.refs_5_, ...), custom_call_target="tpu_custom_call" | custom-call | flops 805306368 | bytes 3145728 | tf_op jit(solution)/shard_map/pallas_call | solution.py:55
  90.0 2.7 %shard_map.81.refs_0_ = f32[8,128,256]{2,1,0:T(8,128)S(1)} custom-call(s32[1]{0:T(128)} %bitcast.5.me_ref.refs_0_, f32[32,2048,128]{2,1,0:T(8,128)} %bitcast.60, f32[32,2048,128]{2,1,0:T(8,128)} %bitcast.59, f32[32,2048,128]{2,1,0:T(8,128)} %bitcast.58, f32[32,2048,128]{2,1,0:T(8,128)} %bitcast.61, f32[512,256]{1,0:T(8,128)S(1)} %shard_map.72.refs_4_.refs_5_, ...), custom_call_target="tpu_custom_call" | custom-call | flops 805306368 | bytes 3145728 | tf_op jit(solution)/shard_map/pallas_call | solution.py:55
  92.6 2.7 %shard_map.82.refs_6_ = f32[8,128,256]{2,1,0:T(8,128)S(1)} custom-call(s32[1]{0:T(128)} %bitcast.5.me_ref.refs_0_, f32[32,2048,128]{2,1,0:T(8,128)} %bitcast.62, f32[32,2048,128]{2,1,0:T(8,128)} %bitcast.63, f32[32,2048,128]{2,1,0:T(8,128)} %bitcast.64, f32[32,2048,128]{2,1,0:T(8,128)} %bitcast.65, f32[512,256]{1,0:T(8,128)S(1)} %shard_map.72.refs_4_.refs_5_, ...), custom_call_target="tpu_custom_call" | custom-call | flops 805306368 | bytes 3145728 | tf_op jit(solution)/shard_map/pallas_call | solution.py:55
  95.3 2.7 %shard_map.84.refs_0_ = f32[8,128,256]{2,1,0:T(8,128)S(1)} custom-call(s32[1]{0:T(128)} %bitcast.5.me_ref.refs_0_, f32[32,2048,128]{2,1,0:T(8,128)} %bitcast.66, f32[32,2048,128]{2,1,0:T(8,128)} %bitcast.67, f32[32,2048,128]{2,1,0:T(8,128)} %bitcast.68, f32[32,2048,128]{2,1,0:T(8,128)} %bitcast.69, f32[512,256]{1,0:T(8,128)S(1)} %shard_map.72.refs_4_.refs_5_, ...), custom_call_target="tpu_custom_call" | custom-call | flops 805306368 | bytes 3145728 | tf_op jit(solution)/shard_map/pallas_call | solution.py:55
  98.0 2.9 %shard_map.85.refs_6_ = f32[8,128,256]{2,1,0:T(8,128)S(1)} custom-call(s32[1]{0:T(128)} %bitcast.5.me_ref.refs_0_, f32[32,2048,128]{2,1,0:T(8,128)} %bitcast.70, f32[32,2048,128]{2,1,0:T(8,128)} %bitcast.71, f32[32,2048,128]{2,1,0:T(8,128)} %bitcast.72, f32[32,2048,128]{2,1,0:T(8,128)} %bitcast.73, f32[512,256]{1,0:T(8,128)S(1)} %shard_map.72.refs_4_.refs_5_, ...), custom_call_target="tpu_custom_call" | custom-call | flops 805306368 | bytes 3145728 | tf_op jit(solution)/shard_map/pallas_call | solution.py:55
  101.0 1.3 slice_add_fusion.6
  102.3 1.5 collective-permute-start.11
  103.8 1.8 collective-permute-done.14.refs_8_
  105.6 1.1 slice_add_fusion.4
  106.7 2.1 %collective-permute-start.15 = (f32[4,128,256]{2,1,0:T(8,128)S(1)}, f32[4,128,256]{2,1,0:T(8,128)S(1)}, u32[]{:S(2)}, u32[]{:S(2)}) collective-permute-start(f32[4,128,256]{2,1,0:T(8,128)S(1)} %slice_add_fusion.4), channel_id=1, source_target_pairs={{0,1},{1,0},{2,3},{3,2},{4,5},{5,4},{6,7},{7,6},{8,9},{9,8},{10,11... | collective-permute-start | bytes 1572872 | tf_op jit(solution)/shard_map/ppermute | solution.py:430
  108.8 2.0 collective-permute-done.18.refs_2_
  110.8 1.1 slice_add_fusion.2
  112.6 10.9 %collective-permute-done.22.refs_8_ = f32[8,128,256]{2,1,0:T(8,128)} collective-permute-done((f32[8,128,256]{2,1,0:T(8,128)}, f32[8,128,256]{2,1,0:T(8,128)}, u32[]{:S(2)}, u32[]{:S(2)}) %collective-permute-start.22) | collective-permute-done | bytes 1048608 | tf_op jit(solution)/shard_map/ppermute | solution.py:430
  123.5 1.1 slice_add_fusion
  126.3 1.6 collective-permute-start.12
  128.9 2.7 %collective-permute-start.16 = (f32[2,128,256]{2,1,0:T(8,128)S(1)}, f32[2,128,256]{2,1,0:T(8,128)S(1)}, u32[]{:S(2)}, u32[]{:S(2)}) collective-permute-start(f32[2,128,256]{2,1,0:T(8,128)S(1)} %slice_add_fusion.16), channel_id=1, source_target_pairs={{0,2},{1,3},{2,0},{3,1},{4,6},{5,7},{6,4},{7,5},{8,10},{9,11},{10,... | collective-permute-start | bytes 786440 | tf_op jit(solution)/shard_map/ppermute | solution.py:430
  131.6 2.2 %collective-permute-done.19.refs_3_ = f32[4,128,256]{2,1,0:T(8,128)S(1)} collective-permute-done((f32[4,128,256]{2,1,0:T(8,128)S(1)}, f32[4,128,256]{2,1,0:T(8,128)S(1)}, u32[]{:S(2)}, u32[]{:S(2)}) %collective-permute-start.19) | collective-permute-done | bytes 524320 | tf_op jit(solution)/shard_map/ppermute | solution.py:430
  135.4 1.6 collective-permute-done.23.refs_9_
  138.1 1.7 collective-permute-start.24
  140.7 2.6 %collective-permute-start.13 = (f32[1,128,256]{2,1,0:T(8,128)S(1)}, f32[1,128,256]{2,1,0:T(8,128)S(1)}, u32[]{:S(2)}, u32[]{:S(2)}) collective-permute-start(f32[1,128,256]{2,1,0:T(8,128)S(1)} %slice_add_fusion.38), channel_id=1, source_target_pairs={{0,2},{1,3},{2,0},{3,1},{4,6},{5,7},{6,4},{7,5},{8,10},{9,11},{10,... | collective-permute-start | bytes 393224 | tf_op jit(solution)/shard_map/ppermute | solution.py:430
  144.3 1.6 collective-permute-start.17
  147.2 1.2 collective-permute-done.24.refs_10_
  149.4 2.9 %collective-permute-start.25 = (f32[1,128,256]{2,1,0:T(8,128)S(1)}, f32[1,128,256]{2,1,0:T(8,128)S(1)}, u32[]{:S(2)}, u32[]{:S(2)}) collective-permute-start(f32[1,128,256]{2,1,0:T(8,128)S(1)} %slice_add_fusion.26), channel_id=1, source_target_pairs={{0,2},{1,3},{2,0},{3,1},{4,6},{5,7},{6,4},{7,5},{8,10},{9,11},{10,... | collective-permute-start | bytes 393224 | tf_op jit(solution)/shard_map/ppermute | solution.py:430
  152.2 1.2 shard_map.83.refs_0_
  154.5 3.7 %collective-permute-done.21.refs_5_ = f32[1,128,256]{2,1,0:T(8,128)S(1)} collective-permute-done((f32[1,128,256]{2,1,0:T(8,128)S(1)}, f32[1,128,256]{2,1,0:T(8,128)S(1)}, u32[]{:S(2)}, u32[]{:S(2)}) %collective-permute-start.21) | collective-permute-done | bytes 131104 | tf_op jit(solution)/shard_map/ppermute | solution.py:430
  158.2 1.4 collective-permute-done.25.refs_11_
  159.7 1.2 shard_map.86.refs_1_
  160.8 1.3 collective-permute-start.31
  162.2 1.3 collective-permute-start.29
  164.1 1.4 collective-permute-start.32
  165.5 4.2 %collective-permute-done.31.refs_3_ = f32[256,256]{1,0:T(8,128)S(1)} collective-permute-done((f32[256,256]{1,0:T(8,128)S(1)}, f32[256,256]{1,0:T(8,128)S(1)}, u32[]{:S(2)}, u32[]{:S(2)}) %collective-permute-start.31) | collective-permute-done | bytes 262176 | tf_op jit(solution)/shard_map/ppermute | solution.py:430
  169.7 1.6 collective-permute-start.33
  171.3 1.6 copy.11
  172.9 4.7 %shard_map.87 = (f32[1536,256]{1,0:T(8,128)}, f32[4096,256]{1,0:T(8,128)}, f32[2,512,256]{2,1,0:T(8,128)}) custom-call(s32[1]{0:T(128)} %bitcast.me_ref, bf16[1536,4096]{1,0:T(8,128)(2,1)} %bitcast.11, f32[1536,256]{1,0:T(8,128)} %bitcast.75, f32[256,256]{1,0:T(8,128)S(1)} %shard_map.83.refs_0_, f32[256,256]{1,0:T(8,128)S(1)} %shard_map.86.refs_1_, ...), custom_call_target="tpu_custom_call" | custom-call | flops 805306368 | bytes 8388608 | tf_op jit(solution)/shard_map/pallas_call | solution.py:55
  177.6 4.7 %shard_map.88 = (f32[1536,256]{1,0:T(8,128)}, f32[4096,256]{1,0:T(8,128)}, f32[2,512,256]{2,1,0:T(8,128)}) custom-call(s32[1]{0:T(128)} %bitcast.me_ref, bf16[1536,4096]{1,0:T(8,128)(2,1)} %bitcast.12, f32[1536,256]{1,0:T(8,128)} %get-tuple-element.21.start_ref, f32[256,256]{1,0:T(8,128)S(1)} %collective-permute-done.28.refs_0_, ...), custom_call_target="tpu_custom_call", output_to_operand_aliasing={{1}: (7, {})} | custom-call | flops 805306368 | bytes 8388608 | tf_op jit(solution)/shard_map/pallas_call | solution.py:55
  182.3 3.8 %shard_map.89 = (f32[1536,256]{1,0:T(8,128)}, f32[4096,256]{1,0:T(8,128)}, f32[1,512,256]{2,1,0:T(8,128)S(1)}) custom-call(s32[1]{0:T(128)} %bitcast.me_ref, bf16[1536,4096]{1,0:T(8,128)(2,1)} %bitcast.13, f32[1536,256]{1,0:T(8,128)} %get-tuple-element.23.start_ref, f32[256,256]{1,0:T(8,128)} %collective-permute-done.32.refs_0_, ...), custom_call_target="tpu_custom_call", output_to_operand_aliasing={{1}: (5, {})} | custom-call | flops 402653184 | bytes 5767168 | tf_op jit(solution)/shard_map/pallas_call | solution.py:55
  187.1 1.3 collective-permute-done.34.refs_0_
  189.5 4.6 %shard_map.90 = (f32[1536,256]{1,0:T(8,128)}, f32[4096,256]{1,0:T(8,128)}, f32[2,512,256]{2,1,0:T(8,128)}) custom-call(s32[1]{0:T(128)} %bitcast.me_ref, bf16[1536,4096]{1,0:T(8,128)(2,1)} %bitcast.14, f32[1536,256]{1,0:T(8,128)} %get-tuple-element.25.start_ref, f32[256,256]{1,0:T(8,128)S(1)} %collective-permute-done.34.refs_0_, ...), custom_call_target="tpu_custom_call", output_to_operand_aliasing={{1}: (7, {})} | custom-call | flops 805306368 | bytes 8388608 | tf_op jit(solution)/shard_map/pallas_call | solution.py:55
  194.1 7.5 %shard_map.91 = (f32[2,768,256]{2,1,0:T(8,128)}, f32[4096,256]{1,0:T(8,128)}) custom-call(s32[1]{0:T(128)} %bitcast.me_ref, bf16[1536,4096]{1,0:T(8,128)(2,1)} %bitcast.15, f32[1536,256]{1,0:T(8,128)} %get-tuple-element.27.start_ref, f32[512,256]{1,0:T(8,128)S(1)} %bitcast.23, ...), custom_call_target="tpu_custom_call", output_to_operand_aliasing={{1}: (4, {})} | custom-call | flops 2214592512 | bytes 10485760 | tf_op jit(solution)/shard_map/pallas_call | solution.py:55
  (90 shorter events, 23.4 us)
Async XLA Ops:
  0.6 2.3 %copy-start.3 = (f32[1,1,2,768,768]{4,3,2,1,0:T(8,128)S(1)}, f32[1,1,2,768,768]{4,3,2,1,0:T(8,128)}, u32[]{:S(2)}) copy-start(f32[1,1,2,768,768]{4,3,2,1,0:T(8,128)} %param.6) | copy-start | bytes 14155780
  3.0 1.4 copy-start.13
  6.2 1.1 copy-start.6
  7.4 4.6 %copy-start = (bf16[1,2,768,4096]{3,2,1,0:T(8,128)(2,1)S(1)}, bf16[1,2,768,4096]{3,2,1,0:T(8,128)(2,1)}, u32[]{:S(2)}) copy-start(bf16[1,2,768,4096]{3,2,1,0:T(8,128)(2,1)} %param.7) | copy-start | bytes 37748740
  11.9 4.9 %slice-start = ((s8[12582912]{0:T(1024)(128)(4,1)}), s8[4194304]{0:T(1024)(128)(4,1)S(1)}, s32[]{:S(2)}) async-start(s8[12582912]{0:T(1024)(128)(4,1)} %bitcast.18), calls=%async_computation | async-start | bytes 8388608
  12.0 4.9 %slice-start.1 = ((s8[12582912]{0:T(1024)(128)(4,1)}), s8[4194304]{0:T(1024)(128)(4,1)S(1)}, s32[]{:S(2)}) async-start(s8[12582912]{0:T(1024)(128)(4,1)} %bitcast.18), calls=%async_computation.1 | async-start | bytes 8388608
  14.1 2.8 %slice-start.2 = ((s8[12582912]{0:T(1024)(128)(4,1)}), s8[4194304]{0:T(1024)(128)(4,1)S(1)}, s32[]{:S(2)}) async-start(s8[12582912]{0:T(1024)(128)(4,1)} %bitcast.18), calls=%async_computation.2 | async-start | bytes 8388608
  14.1 5.8 %collective-permute-start = (f32[4,256,256]{2,1,0:T(8,128)S(1)}, f32[4,256,256]{2,1,0:T(8,128)S(1)}, u32[]{:S(2)}, u32[]{:S(2)}) collective-permute-start(f32[4,256,256]{2,1,0:T(8,128)S(1)} %shard_map.70), channel_id=1, source_target_pairs={{0,4},{1,5},{2,6},{3,7},{4,0},{5,1},{6,2},{7,3},{8,12},{9,13},{10,... | collective-permute-start | bytes 3145736 | tf_op jit(solution)/shard_map/ppermute | solution.py:430
  16.7 6.2 %collective-permute-start.3 = (f32[4,256,256]{2,1,0:T(8,128)S(1)}, f32[4,256,256]{2,1,0:T(8,128)S(1)}, u32[]{:S(2)}, u32[]{:S(2)}) collective-permute-start(f32[4,256,256]{2,1,0:T(8,128)S(1)} %shard_map.71), channel_id=1, source_target_pairs={{0,4},{1,5},{2,6},{3,7},{4,0},{5,1},{6,2},{7,3},{8,12},{9,13},{10,... | collective-permute-start | bytes 3145736 | tf_op jit(solution)/shard_map/ppermute | solution.py:430
  19.8 17.8 %copy-start.4 = (f32[4,256,256]{2,1,0:T(8,128)}, f32[4,256,256]{2,1,0:T(8,128)S(1)}, u32[]{:S(2)}) copy-start(f32[4,256,256]{2,1,0:T(8,128)S(1)} %get-tuple-element.20.refs_4_) | copy-start | bytes 3145732
  19.9 15.1 %collective-permute-start.1 = (f32[2,256,256]{2,1,0:T(8,128)S(1)}, f32[2,256,256]{2,1,0:T(8,128)S(1)}, u32[]{:S(2)}, u32[]{:S(2)}) collective-permute-start(f32[2,256,256]{2,1,0:T(8,128)S(1)} %slice_add_fusion.9), channel_id=1, source_target_pairs={{0,8},{1,9},{2,10},{3,11},{4,12},{5,13},{6,14},{7,15},{8,0},{9,1},... | collective-permute-start | bytes 1572872 | tf_op jit(solution)/shard_map/ppermute | solution.py:430
  23.0 14.7 %collective-permute-start.4 = (f32[2,256,256]{2,1,0:T(8,128)S(1)}, f32[2,256,256]{2,1,0:T(8,128)S(1)}, u32[]{:S(2)}, u32[]{:S(2)}) collective-permute-start(f32[2,256,256]{2,1,0:T(8,128)S(1)} %slice_add_fusion.8), channel_id=1, source_target_pairs={{0,16},{1,17},{2,18},{3,19},{4,20},{5,21},{6,22},{7,23},{8,24},{9,... | collective-permute-start | bytes 1572872 | tf_op jit(solution)/shard_map/ppermute | solution.py:430
  35.1 3.4 %copy-start.8 = (f32[2,256,256]{2,1,0:T(8,128)}, f32[2,256,256]{2,1,0:T(8,128)S(1)}, u32[]{:S(2)}) copy-start(f32[2,256,256]{2,1,0:T(8,128)S(1)} %collective-permute-done.1.refs_2_) | copy-start | bytes 1572868
  35.9 8.0 %collective-permute-start.2 = (f32[1,256,256]{2,1,0:T(8,128)}, f32[1,256,256]{2,1,0:T(8,128)S(1)}, u32[]{:S(2)}, u32[]{:S(2)}) collective-permute-start(f32[1,256,256]{2,1,0:T(8,128)} %slice_add_fusion.24), channel_id=1, source_target_pairs={{0,16},{1,17},{2,18},{3,19},{4,20},{5,21},{6,22},{7,23},{8,24},{9,... | collective-permute-start | bytes 786440 | tf_op jit(solution)/shard_map/ppermute | solution.py:430
  37.7 0.9 copy-start.10
  38.6 7.5 %collective-permute-start.5 = (f32[1,256,256]{2,1,0:T(8,128)}, f32[1,256,256]{2,1,0:T(8,128)}, u32[]{:S(2)}, u32[]{:S(2)}) collective-permute-start(f32[1,256,256]{2,1,0:T(8,128)} %slice_add_fusion.22), channel_id=1, source_target_pairs={{0,8},{1,9},{2,10},{3,11},{4,12},{5,13},{6,14},{7,15},{8,0},{9,1},... | collective-permute-start | bytes 786440 | tf_op jit(solution)/shard_map/ppermute | solution.py:430
  46.0 1.2 copy-start.5
  47.2 1.0 copy-start.9
  48.3 1.0 copy-start.11
  49.3 1.0 copy-start.12
  56.2 15.1 %collective-permute-start.6 = (f32[16,128,256]{2,1,0:T(8,128)S(1)}, f32[16,128,256]{2,1,0:T(8,128)S(1)}, u32[]{:S(2)}, u32[]{:S(2)}) collective-permute-start(f32[16,128,256]{2,1,0:T(8,128)S(1)} %shard_map.73), channel_id=1, source_target_pairs={{0,4},{1,5},{2,6},{3,7},{4,0},{5,1},{6,2},{7,3},{8,12},{9,13},{10,... | collective-permute-start | bytes 6291464 | tf_op jit(solution)/shard_map/ppermute | solution.py:430
  60.9 15.3 %collective-permute-start.7 = (f32[16,128,256]{2,1,0:T(8,128)S(1)}, f32[16,128,256]{2,1,0:T(8,128)S(1)}, u32[]{:S(2)}, u32[]{:S(2)}) collective-permute-start(f32[16,128,256]{2,1,0:T(8,128)S(1)} %shard_map.75), channel_id=1, source_target_pairs={{0,4},{1,5},{2,6},{3,7},{4,0},{5,1},{6,2},{7,3},{8,12},{9,13},{10,... | collective-permute-start | bytes 6291464 | tf_op jit(solution)/shard_map/ppermute | solution.py:430
  66.0 14.1 %collective-permute-start.8 = (f32[16,128,256]{2,1,0:T(8,128)S(1)}, f32[16,128,256]{2,1,0:T(8,128)S(1)}, u32[]{:S(2)}, u32[]{:S(2)}) collective-permute-start(f32[16,128,256]{2,1,0:T(8,128)S(1)} %shard_map.77), channel_id=1, source_target_pairs={{0,4},{1,5},{2,6},{3,7},{4,0},{5,1},{6,2},{7,3},{8,12},{9,13},{10,... | collective-permute-start | bytes 6291464 | tf_op jit(solution)/shard_map/ppermute | solution.py:430
  70.8 15.2 %collective-permute-start.9 = (f32[16,128,256]{2,1,0:T(8,128)S(1)}, f32[16,128,256]{2,1,0:T(8,128)S(1)}, u32[]{:S(2)}, u32[]{:S(2)}) collective-permute-start(f32[16,128,256]{2,1,0:T(8,128)S(1)} %shard_map.79), channel_id=1, source_target_pairs={{0,4},{1,5},{2,6},{3,7},{4,0},{5,1},{6,2},{7,3},{8,12},{9,13},{10,... | collective-permute-start | bytes 6291464 | tf_op jit(solution)/shard_map/ppermute | solution.py:430
  74.7 26.3 %collective-permute-start.10 = (f32[8,128,256]{2,1,0:T(8,128)}, f32[8,128,256]{2,1,0:T(8,128)}, u32[]{:S(2)}, u32[]{:S(2)}) collective-permute-start(f32[8,128,256]{2,1,0:T(8,128)} %shard_map.74.refs_6_), channel_id=1, source_target_pairs={{0,8},{1,9},{2,10},{3,11},{4,12},{5,13},{6,14},{7,15},{8,0},{9,1},... | collective-permute-start | bytes 3145736 | tf_op jit(solution)/shard_map/ppermute | solution.py:430
  79.6 26.0 %collective-permute-start.14 = (f32[8,128,256]{2,1,0:T(8,128)}, f32[8,128,256]{2,1,0:T(8,128)}, u32[]{:S(2)}, u32[]{:S(2)}) collective-permute-start(f32[8,128,256]{2,1,0:T(8,128)} %shard_map.76.refs_7_), channel_id=1, source_target_pairs={{0,16},{1,17},{2,18},{3,19},{4,20},{5,21},{6,22},{7,23},{8,24},{9,... | collective-permute-start | bytes 3145736 | tf_op jit(solution)/shard_map/ppermute | solution.py:430
  80.1 4.2 %copy-start.1 = (f32[16,128,256]{2,1,0:T(8,128)}, f32[16,128,256]{2,1,0:T(8,128)S(1)}, u32[]{:S(2)}) copy-start(f32[16,128,256]{2,1,0:T(8,128)S(1)} %collective-permute-done.8.refs_5_.refs_1_) | copy-start | bytes 6291460
  84.4 26.4 %collective-permute-start.18 = (f32[8,128,256]{2,1,0:T(8,128)}, f32[8,128,256]{2,1,0:T(8,128)}, u32[]{:S(2)}, u32[]{:S(2)}) collective-permute-start(f32[8,128,256]{2,1,0:T(8,128)} %shard_map.78.refs_8_), channel_id=1, source_target_pairs={{0,1},{1,0},{2,3},{3,2},{4,5},{5,4},{6,7},{7,6},{8,9},{9,8},{10,11... | collective-permute-start | bytes 3145736 | tf_op jit(solution)/shard_map/ppermute | solution.py:430
  89.4 34.1 %collective-permute-start.22 = (f32[8,128,256]{2,1,0:T(8,128)}, f32[8,128,256]{2,1,0:T(8,128)}, u32[]{:S(2)}, u32[]{:S(2)}) collective-permute-start(f32[8,128,256]{2,1,0:T(8,128)} %shard_map.80.refs_9_), channel_id=1, source_target_pairs={{0,8},{1,9},{2,10},{3,11},{4,12},{5,13},{6,14},{7,15},{8,0},{9,1},... | collective-permute-start | bytes 3145736 | tf_op jit(solution)/shard_map/ppermute | solution.py:430
  100.9 9.8 %copy-start.2 = (f32[16,128,256]{2,1,0:T(8,128)S(1)}, f32[16,128,256]{2,1,0:T(8,128)}, u32[]{:S(2)}) copy-start(f32[16,128,256]{2,1,0:T(8,128)} %copy-done.1) | copy-start | bytes 6291460
  102.3 23.0 %collective-permute-start.11 = (f32[4,128,256]{2,1,0:T(8,128)S(1)}, f32[4,128,256]{2,1,0:T(8,128)S(1)}, u32[]{:S(2)}, u32[]{:S(2)}) collective-permute-start(f32[4,128,256]{2,1,0:T(8,128)S(1)} %slice_add_fusion.6), channel_id=1, source_target_pairs={{0,16},{1,17},{2,18},{3,19},{4,20},{5,21},{6,22},{7,23},{8,24},{9,... | collective-permute-start | bytes 1572872 | tf_op jit(solution)/shard_map/ppermute | solution.py:430
  106.7 21.2 %collective-permute-start.15 = (f32[4,128,256]{2,1,0:T(8,128)S(1)}, f32[4,128,256]{2,1,0:T(8,128)S(1)}, u32[]{:S(2)}, u32[]{:S(2)}) collective-permute-start(f32[4,128,256]{2,1,0:T(8,128)S(1)} %slice_add_fusion.4), channel_id=1, source_target_pairs={{0,1},{1,0},{2,3},{3,2},{4,5},{5,4},{6,7},{7,6},{8,9},{9,8},{10,11... | collective-permute-start | bytes 1572872 | tf_op jit(solution)/shard_map/ppermute | solution.py:430
  111.9 21.8 %collective-permute-start.19 = (f32[4,128,256]{2,1,0:T(8,128)S(1)}, f32[4,128,256]{2,1,0:T(8,128)S(1)}, u32[]{:S(2)}, u32[]{:S(2)}) collective-permute-start(f32[4,128,256]{2,1,0:T(8,128)S(1)} %slice_add_fusion.2), channel_id=1, source_target_pairs={{0,8},{1,9},{2,10},{3,11},{4,12},{5,13},{6,14},{7,15},{8,0},{9,1},... | collective-permute-start | bytes 1572872 | tf_op jit(solution)/shard_map/ppermute | solution.py:430
  124.6 12.4 %collective-permute-start.23 = (f32[4,128,256]{2,1,0:T(8,128)S(1)}, f32[4,128,256]{2,1,0:T(8,128)S(1)}, u32[]{:S(2)}, u32[]{:S(2)}) collective-permute-start(f32[4,128,256]{2,1,0:T(8,128)S(1)} %slice_add_fusion), channel_id=1, source_target_pairs={{0,16},{1,17},{2,18},{3,19},{4,20},{5,21},{6,22},{7,23},{8,24},{9,... | collective-permute-start | bytes 1572872 | tf_op jit(solution)/shard_map/ppermute | solution.py:430
  126.3 13.4 %collective-permute-start.12 = (f32[2,128,256]{2,1,0:T(8,128)S(1)}, f32[2,128,256]{2,1,0:T(8,128)S(1)}, u32[]{:S(2)}, u32[]{:S(2)}) collective-permute-start(f32[2,128,256]{2,1,0:T(8,128)S(1)} %slice_add_fusion.19), channel_id=1, source_target_pairs={{0,1},{1,0},{2,3},{3,2},{4,5},{5,4},{6,7},{7,6},{8,9},{9,8},{10,11... | collective-permute-start | bytes 786440 | tf_op jit(solution)/shard_map/ppermute | solution.py:430
  128.9 14.4 %collective-permute-start.16 = (f32[2,128,256]{2,1,0:T(8,128)S(1)}, f32[2,128,256]{2,1,0:T(8,128)S(1)}, u32[]{:S(2)}, u32[]{:S(2)}) collective-permute-start(f32[2,128,256]{2,1,0:T(8,128)S(1)} %slice_add_fusion.16), channel_id=1, source_target_pairs={{0,2},{1,3},{2,0},{3,1},{4,6},{5,7},{6,4},{7,5},{8,10},{9,11},{10,... | collective-permute-start | bytes 786440 | tf_op jit(solution)/shard_map/ppermute | solution.py:430
  134.8 11.1 %collective-permute-start.20 = (f32[2,128,256]{2,1,0:T(8,128)S(1)}, f32[2,128,256]{2,1,0:T(8,128)S(1)}, u32[]{:S(2)}, u32[]{:S(2)}) collective-permute-start(f32[2,128,256]{2,1,0:T(8,128)S(1)} %slice_add_fusion.13), channel_id=1, source_target_pairs={{0,16},{1,17},{2,18},{3,19},{4,20},{5,21},{6,22},{7,23},{8,24},{9,... | collective-permute-start | bytes 786440 | tf_op jit(solution)/shard_map/ppermute | solution.py:430
  138.1 10.3 %collective-permute-start.24 = (f32[2,128,256]{2,1,0:T(8,128)S(1)}, f32[2,128,256]{2,1,0:T(8,128)S(1)}, u32[]{:S(2)}, u32[]{:S(2)}) collective-permute-start(f32[2,128,256]{2,1,0:T(8,128)S(1)} %slice_add_fusion.10), channel_id=1, source_target_pairs={{0,1},{1,0},{2,3},{3,2},{4,5},{5,4},{6,7},{7,6},{8,9},{9,8},{10,11... | collective-permute-start | bytes 786440 | tf_op jit(solution)/shard_map/ppermute | solution.py:430
  140.7 11.5 %collective-permute-start.13 = (f32[1,128,256]{2,1,0:T(8,128)S(1)}, f32[1,128,256]{2,1,0:T(8,128)S(1)}, u32[]{:S(2)}, u32[]{:S(2)}) collective-permute-start(f32[1,128,256]{2,1,0:T(8,128)S(1)} %slice_add_fusion.38), channel_id=1, source_target_pairs={{0,2},{1,3},{2,0},{3,1},{4,6},{5,7},{6,4},{7,5},{8,10},{9,11},{10,... | collective-permute-start | bytes 393224 | tf_op jit(solution)/shard_map/ppermute | solution.py:430
  144.3 7.9 %collective-permute-start.17 = (f32[1,128,256]{2,1,0:T(8,128)S(1)}, f32[1,128,256]{2,1,0:T(8,128)S(1)}, u32[]{:S(2)}, u32[]{:S(2)}) collective-permute-start(f32[1,128,256]{2,1,0:T(8,128)S(1)} %slice_add_fusion.34), channel_id=1, source_target_pairs={{0,8},{1,9},{2,10},{3,11},{4,12},{5,13},{6,14},{7,15},{8,0},{9,1},... | collective-permute-start | bytes 393224 | tf_op jit(solution)/shard_map/ppermute | solution.py:430
  146.8 11.4 %collective-permute-start.21 = (f32[1,128,256]{2,1,0:T(8,128)S(1)}, f32[1,128,256]{2,1,0:T(8,128)S(1)}, u32[]{:S(2)}, u32[]{:S(2)}) collective-permute-start(f32[1,128,256]{2,1,0:T(8,128)S(1)} %slice_add_fusion.30), channel_id=1, source_target_pairs={{0,2},{1,3},{2,0},{3,1},{4,6},{5,7},{6,4},{7,5},{8,10},{9,11},{10,... | collective-permute-start | bytes 393224 | tf_op jit(solution)/shard_map/ppermute | solution.py:430
  149.4 10.3 %collective-permute-start.25 = (f32[1,128,256]{2,1,0:T(8,128)S(1)}, f32[1,128,256]{2,1,0:T(8,128)S(1)}, u32[]{:S(2)}, u32[]{:S(2)}) collective-permute-start(f32[1,128,256]{2,1,0:T(8,128)S(1)} %slice_add_fusion.26), channel_id=1, source_target_pairs={{0,2},{1,3},{2,0},{3,1},{4,6},{5,7},{6,4},{7,5},{8,10},{9,11},{10,... | collective-permute-start | bytes 393224 | tf_op jit(solution)/shard_map/ppermute | solution.py:430
  153.4 17.9 %copy-start.7 = (f32[256,1536]{1,0:T(8,128)S(1)}, f32[256,1536]{1,0:T(8,128)}, u32[]{:S(2)}) copy-start(f32[256,1536]{1,0:T(8,128)} %copy-done.6) | copy-start | bytes 4718596
  153.4 10.1 %collective-permute-start.26 = (f32[256,256]{1,0:T(8,128)S(1)}, f32[256,256]{1,0:T(8,128)S(1)}, u32[]{:S(2)}, u32[]{:S(2)}) collective-permute-start(f32[256,256]{1,0:T(8,128)S(1)} %shard_map.83.refs_0_), channel_id=1, source_target_pairs={{0,4},{1,5},{2,6},{3,7},{4,0},{5,1},{6,2},{7,3},{8,12},{9,13},{10,... | collective-permute-start | bytes 786440 | tf_op jit(solution)/shard_map/ppermute | solution.py:430
  153.5 10.6 %collective-permute-start.28 = (f32[256,256]{1,0:T(8,128)S(1)}, f32[256,256]{1,0:T(8,128)S(1)}, u32[]{:S(2)}, u32[]{:S(2)}) collective-permute-start(f32[256,256]{1,0:T(8,128)S(1)} %shard_map.83.refs_0_), channel_id=1, source_target_pairs={{0,8},{1,9},{2,10},{3,11},{4,12},{5,13},{6,14},{7,15},{8,0},{9,1},... | collective-permute-start | bytes 786440 | tf_op jit(solution)/shard_map/ppermute | solution.py:430
  160.8 8.8 %collective-permute-start.31 = (f32[256,256]{1,0:T(8,128)S(1)}, f32[256,256]{1,0:T(8,128)S(1)}, u32[]{:S(2)}, u32[]{:S(2)}) collective-permute-start(f32[256,256]{1,0:T(8,128)S(1)} %shard_map.86.refs_1_), channel_id=1, source_target_pairs={{0,16},{1,17},{2,18},{3,19},{4,20},{5,21},{6,22},{7,23},{8,24},{9,... | collective-permute-start | bytes 786440 | tf_op jit(solution)/shard_map/ppermute | solution.py:430
  162.2 10.8 %collective-permute-start.27 = (f32[256,256]{1,0:T(8,128)S(1)}, f32[256,256]{1,0:T(8,128)}, u32[]{:S(2)}, u32[]{:S(2)}) collective-permute-start(f32[256,256]{1,0:T(8,128)S(1)} %shard_map.86.refs_1_), channel_id=1, source_target_pairs={{0,4},{1,5},{2,6},{3,7},{4,0},{5,1},{6,2},{7,3},{8,12},{9,13},{10,... | collective-permute-start | bytes 786440 | tf_op jit(solution)/shard_map/ppermute | solution.py:430
  162.2 15.4 %collective-permute-start.29 = (f32[256,256]{1,0:T(8,128)S(1)}, f32[256,256]{1,0:T(8,128)S(1)}, u32[]{:S(2)}, u32[]{:S(2)}) collective-permute-start(f32[256,256]{1,0:T(8,128)S(1)} %shard_map.86.refs_1_), channel_id=1, source_target_pairs={{0,8},{1,9},{2,10},{3,11},{4,12},{5,13},{6,14},{7,15},{8,0},{9,1},... | collective-permute-start | bytes 786440 | tf_op jit(solution)/shard_map/ppermute | solution.py:430
  163.5 14.1 %collective-permute-start.30 = (f32[256,256]{1,0:T(8,128)S(1)}, f32[256,256]{1,0:T(8,128)S(1)}, u32[]{:S(2)}, u32[]{:S(2)}) collective-permute-start(f32[256,256]{1,0:T(8,128)S(1)} %shard_map.83.refs_0_), channel_id=1, source_target_pairs={{0,16},{1,17},{2,18},{3,19},{4,20},{5,21},{6,22},{7,23},{8,24},{9,... | collective-permute-start | bytes 786440 | tf_op jit(solution)/shard_map/ppermute | solution.py:430
  164.1 18.2 %collective-permute-start.32 = (f32[256,256]{1,0:T(8,128)S(1)}, f32[256,256]{1,0:T(8,128)}, u32[]{:S(2)}, u32[]{:S(2)}) collective-permute-start(f32[256,256]{1,0:T(8,128)S(1)} %collective-permute-done.28.refs_0_), channel_id=1, source_target_pairs={{0,16},{1,17},{2,18},{3,19},{4,20},{5,21},{6,22},{7,23},{8,24},{9,... | collective-permute-start | bytes 786440 | tf_op jit(solution)/shard_map/ppermute | solution.py:430
  169.7 12.7 %collective-permute-start.33 = (f32[256,256]{1,0:T(8,128)S(1)}, f32[256,256]{1,0:T(8,128)}, u32[]{:S(2)}, u32[]{:S(2)}) collective-permute-start(f32[256,256]{1,0:T(8,128)S(1)} %collective-permute-done.31.refs_3_), channel_id=1, source_target_pairs={{0,8},{1,9},{2,10},{3,11},{4,12},{5,13},{6,14},{7,15},{8,0},{9,1},... | collective-permute-start | bytes 786440 | tf_op jit(solution)/shard_map/ppermute | solution.py:430
  186.1 8.1 %collective-permute-start.38 = (f32[1,512,256]{2,1,0:T(8,128)S(1)}, f32[1,512,256]{2,1,0:T(8,128)S(1)}, u32[]{:S(2)}, u32[]{:S(2)}) collective-permute-start(f32[1,512,256]{2,1,0:T(8,128)S(1)} %get-tuple-element.28), channel_id=1, source_target_pairs={{0,4},{1,5},{2,6},{3,7},{4,0},{5,1},{6,2},{7,3},{8,12},{9,13},{10,... | collective-permute-start | bytes 1572872 | tf_op jit(solution)/shard_map/ppermute | solution.py:430
  186.1 2.3 %collective-permute-start.34 = (f32[256,256]{1,0:T(8,128)S(1)}, f32[256,256]{1,0:T(8,128)S(1)}, u32[]{:S(2)}, u32[]{:S(2)}) collective-permute-start(f32[256,256]{1,0:T(8,128)S(1)} %collective-permute-done.28.refs_0_), channel_id=1, source_target_pairs={{0,4},{1,5},{2,6},{3,7},{4,0},{5,1},{6,2},{7,3},{8,12},{9,13},{10,... | collective-permute-start | bytes 786440 | tf_op jit(solution)/shard_map/ppermute | solution.py:430
  186.6 2.1 %collective-permute-start.35 = (f32[256,256]{1,0:T(8,128)S(1)}, f32[256,256]{1,0:T(8,128)S(1)}, u32[]{:S(2)}, u32[]{:S(2)}) collective-permute-start(f32[256,256]{1,0:T(8,128)S(1)} %collective-permute-done.29.refs_1_), channel_id=1, source_target_pairs={{0,4},{1,5},{2,6},{3,7},{4,0},{5,1},{6,2},{7,3},{8,12},{9,13},{10,... | collective-permute-start | bytes 786440 | tf_op jit(solution)/shard_map/ppermute | solution.py:430
  186.6 2.5 %collective-permute-start.36 = (f32[256,256]{1,0:T(8,128)S(1)}, f32[256,256]{1,0:T(8,128)S(1)}, u32[]{:S(2)}, u32[]{:S(2)}) collective-permute-start(f32[256,256]{1,0:T(8,128)S(1)} %collective-permute-done.30.refs_2_), channel_id=1, source_target_pairs={{0,4},{1,5},{2,6},{3,7},{4,0},{5,1},{6,2},{7,3},{8,12},{9,13},{10,... | collective-permute-start | bytes 786440 | tf_op jit(solution)/shard_map/ppermute | solution.py:430
  187.1 2.4 %collective-permute-start.37 = (f32[256,256]{1,0:T(8,128)S(1)}, f32[256,256]{1,0:T(8,128)S(1)}, u32[]{:S(2)}, u32[]{:S(2)}) collective-permute-start(f32[256,256]{1,0:T(8,128)S(1)} %collective-permute-done.31.refs_3_), channel_id=1, source_target_pairs={{0,4},{1,5},{2,6},{3,7},{4,0},{5,1},{6,2},{7,3},{8,12},{9,13},{10,... | collective-permute-start | bytes 786440 | tf_op jit(solution)/shard_map/ppermute | solution.py:430

commit v2 on v1

--- a/solution.py
+++ b/solution.py
@@ -86,29 +86,38 @@
     return place
 
 
-def first_kernel(seeds_ref, inverse_ref, first_ref, half_ref):
-    width = inverse_ref.shape[1]
-    tile = tile_of(width)
-    seeds = split(seeds_ref[0].T)
-    inverse = split(inverse_ref[0])
-    for start in range(0, width, tile):
-        stop = start + tile
-        first = dot3(
-            [part[:, :stop] for part in seeds], [part[:stop, start:stop] for part in inverse]
-        )
-        first_ref[:, start:stop] = first
-        half_ref[:, start:stop] = first.astype(BF16)
+def upper_tiles(count):
+    return [(i, j) for i in range(count) for j in range(i, count)]
+
+
+def first_kernel(parts, *refs):
+    seeds_refs, inverse_refs, (first_ref, half_ref) = refs[:parts], refs[parts:-2], refs[-2:]
+    tile = seeds_refs[0].shape[1]
+    seeds = [split(ref[0].T) for ref in seeds_refs]
+    firsts = [None] * parts
+    for (i, j), ref in zip(upper_tiles(parts), inverse_refs):
+        term = dot3(seeds[i], split(ref[0]))
+        firsts[j] = term if i == 0 else firsts[j] + term
+    for j, first in enumerate(firsts):
+        first_ref[:, j * tile : (j + 1) * tile] = first
+        half_ref[:, j * tile : (j + 1) * tile] = first.astype(BF16)
 
 
 def first_of(seeds, inverse):
     blocks, width, count = seeds.shape
+    tile = tile_of(width)
+    parts = width // tile
     across = pl.BlockSpec((count, width), lambda b: (0, b))
     return call(
-        first_kernel,
+        functools.partial(first_kernel, parts),
         (blocks,),
         [
-            pl.BlockSpec((1, width, count), lambda b: (b, 0, 0)),
-            pl.BlockSpec((1, width, width), lambda b: (b, 0, 0)),
+            pl.BlockSpec((1, tile, count), functools.partial(lambda i, b: (b, i, 0), i))
+            for i in range(parts)
+        ]
+        + [
+            pl.BlockSpec((1, tile, tile), functools.partial(lambda i, j, b: (b, i, j), i, j))
+            for i, j in upper_tiles(parts)
         ],
         [across, across],
         [
@@ -118,11 +127,17 @@
         6 * blocks * width * width * count,
         4 * blocks * width * (width + 3 * count),
         prefetch=0,
-    )(seeds, inverse)
-
-
-def seed_kernel(me_ref, coupling_ref, half_ref, *sum_refs):
-    total = dot(half_ref[...], coupling_ref[...])
+        room=58 * MIB,
+    )(*([seeds] * parts), *([inverse] * len(upper_tiles(parts))))
+
+
+def seed_kernel(strips, me_ref, *refs):
+    coupling_refs, half_ref, sum_refs = refs[:strips], refs[strips], refs[strips + 1 :]
+    depth = coupling_refs[0].shape[0]
+    total = sum(
+        dot(half_ref[:, at * depth : (at + 1) * depth], ref[...])
+        for at, ref in enumerate(coupling_refs)
+    )
     cols = total.shape[1] // len(sum_refs)
     for chunk, ref in enumerate(sum_refs):
         ref[0] = total[:, chunk * cols : (chunk + 1) * cols]
@@ -137,13 +152,19 @@
     def unit_of(f):
         return spread(orders[0], f) | base
 
+    def place(strip, f, me_ref):
+        return strip, ((unit_of(f) ^ me_ref[0]) * sub + offset) // wide
+
+    strip = strip_of(depth)
+    strips = depth // strip
     return call(
-        seed_kernel,
+        functools.partial(seed_kernel, strips),
         (units,),
         [
-            pl.BlockSpec(
-                (depth, wide), lambda f, me_ref: (0, ((unit_of(f) ^ me_ref[0]) * sub + offset) // wide)
-            ),
+            pl.BlockSpec((strip, wide), functools.partial(place, number))
+            for number in range(strips)
+        ]
+        + [
             pl.BlockSpec((count, depth), lambda f, me_ref: (0, 0)),
         ],
         [
@@ -158,7 +179,12 @@
         [jax.ShapeDtypeStruct((units, count, cols), F32)] * len(orders),
         2 * units * depth * wide * count,
         units * wide * (2 * depth + 4 * count),
-    )(me, coupling, half)
+        room=52 * MIB,
+    )(me, *([coupling] * strips), half)
+
+
+def strip_of(depth):
+    return 256 if depth % 256 == 0 else depth
 
 
 def seed_cols(sub):
@@ -187,7 +213,6 @@
         0,
         16 * seed.size,
         prefetch=0,
-        room=40 * MIB,
     )(seed, *flat)
 
 
@@ -245,10 +270,12 @@
     )(*flat)
 
 
-def shared_kernel(group, rows, pieces, arrived, me_ref, *refs):
-    tiles, refs = refs[:group], refs[group:]
+def shared_kernel(group, strips, pieces, arrived, me_ref, *refs):
+    tiles, refs = refs[: group * strips], refs[group * strips :]
     seed_ref, *received, out_ref, parts_ref, seed_parts_ref = refs
     depth = seed_ref.shape[0]
+    rows = parts_ref.shape[0] // group
+    strip = rows // strips
 
     @pl.when(pl.program_id(0) == 0)
     def _():
@@ -257,9 +284,9 @@
         seed_parts_ref[depth : 2 * depth] = high
         seed_parts_ref[2 * depth :] = low
 
-    for g in range(group):
-        place = pl.ds(g * rows, rows)
-        high, low = split(rows_of(tiles[g], rows, pieces))
+    for at, ref in enumerate(tiles):
+        place = pl.ds(at * strip, strip)
+        high, low = split(rows_of(ref, strip, pieces))
         parts_ref[place, :depth] = high
         parts_ref[place, depth : 2 * depth] = low
         parts_ref[place, 2 * depth :] = high
@@ -275,20 +302,24 @@
     pieces = depth // lanes
     units = 1 << len(bits)
     group = min(units, 4)
-
-    def place(g, f, me_ref):
-        return (spread(bits, f * group + g) | base) ^ me_ref[0], offset // rows, 0
+    strips = next(n for n in (4, 2, 1) if rows % (n * 16) == 0 or n == 1)
+
+    def place(g, strip, f, me_ref):
+        unit = (spread(bits, f * group + g) | base) ^ me_ref[0]
+        return unit, offset // rows * strips + strip, 0
 
     in_specs = [
-        pl.BlockSpec((1, rows * pieces, lanes), functools.partial(place, g)) for g in range(group)
+        pl.BlockSpec((1, rows // strips * pieces, lanes), functools.partial(place, g, strip))
+        for g in range(group)
+        for strip in range(strips)
     ] + [pl.BlockSpec((depth, count), lambda f, me_ref: (0, 0))]
-    operands = [tiles] * group + [seed]
+    operands = [tiles] * (group * strips) + [seed]
     if received is not None:
         skip = received.shape[0] // group - units // group
         in_specs.append(pl.BlockSpec((group, rows, count), lambda f, me_ref: (skip + f, 0, 0)))
         operands.append(received)
     return call(
-        functools.partial(shared_kernel, group, rows, pieces, received is not None),
+        functools.partial(shared_kernel, group, strips, pieces, received is not None),
         (units // group,),
         in_specs,
         pl.BlockSpec((group, rows, count), lambda f, me_ref: (f, 0, 0)),
@@ -301,20 +332,33 @@
     )(me, *operands)
 
 
-def coupled_kernel(units, halves, aliased, last, me_ref, coupling_ref, start_ref, *refs):
+def coupled_kernel(units, halves, strips, aliased, last, me_ref, *refs):
+    coupling_refs, start_ref, refs = refs[:strips], refs[strips], refs[strips + 1 :]
     pieces, refs = refs[: units * halves], refs[units * halves :]
     refs = refs[1:] if aliased else refs
     u = pl.program_id(0)
     if last:
-        inverse_ref, out_ref, adjoint_ref, second_ref, held_ref, sem = refs
-        fetch = pltpu.make_async_copy(inverse_ref, held_ref, sem)
+        inverse_ref, out_ref, adjoint_ref, second_ref, held_ref, sems = refs
+        blocks, width, _ = inverse_ref.shape
+        tile = held_ref.shape[2]
+        parts = width // tile
+        places = [(block, i, j) for block in range(blocks) for i, j in upper_tiles(parts)]
+        fetches = [
+            pltpu.make_async_copy(
+                inverse_ref.at[block, pl.ds(i * tile, tile), pl.ds(j * tile, tile)],
+                held_ref.at[at],
+                sems.at[at],
+            )
+            for at, (block, i, j) in enumerate(places)
+        ]
     else:
         second_ref, adjoint_ref, packed_ref = refs
 
     @pl.when(u == 0)
     def _():
         if last:
-            fetch.start()
+            for fetch in fetches:
+                fetch.start()
         second_ref[...] = start_ref[...]
 
     for g in range(units):
@@ -327,22 +371,25 @@
             adjoint_ref[...] = block
             if not last:
                 packed_ref[0] = block
-            second_ref[...] -= dot(coupling_ref[...], block.astype(BF16))
+            half = block.astype(BF16)
+            for at, ref in enumerate(coupling_refs):
+                place = pl.ds(at * ref.shape[0], ref.shape[0])
+                second_ref[place] -= dot(ref[...], half)
 
     if last:
 
         @pl.when(u == units - 1)
         def _():
-            fetch.wait()
-            blocks, width, _ = held_ref.shape
-            tile = tile_of(width)
-            for block in range(blocks):
-                second = split(second_ref[block * width : (block + 1) * width])
-                for start in range(0, width, tile):
-                    out_ref[block, start : start + tile] = dot3(
-                        split(held_ref[block, start : start + tile, start:]),
-                        [part[start:] for part in second],
-                    )
+            second = [
+                split(second_ref[at * tile : (at + 1) * tile]) for at in range(blocks * parts)
+            ]
+            totals = {}
+            for at, (block, i, j) in enumerate(places):
+                fetches[at].wait()
+                term = dot3(split(held_ref[at]), second[block * parts + j])
+                totals[block, i] = term if i == j else totals[block, i] + term
+            for (block, i), total in totals.items():
+                out_ref[block, i * tile : (i + 1) * tile] = total
 
 
 def coupled_step(me, coupling, start, pieces, numbers, adjoint, inverse=None):
@@ -358,11 +405,15 @@
         return unit
 
     whole = pl.BlockSpec((depth, count), lambda u, me_ref: (0, 0))
+    strip = strip_of(depth)
+    strips = depth // strip
     in_specs = [
-        pl.BlockSpec((depth, sub), lambda u, me_ref: (0, unit_of(u) ^ me_ref[0])),
-        whole,
-    ]
-    operands = [coupling, start]
+        pl.BlockSpec(
+            (strip, sub), functools.partial(lambda at, u, me_ref: (at, unit_of(u) ^ me_ref[0]), at)
+        )
+        for at in range(strips)
+    ] + [whole]
+    operands = [coupling] * strips + [start]
     for group in pieces:
         for piece in group:
             in_specs.append(pl.BlockSpec(piece.shape, lambda u, me_ref: (0, 0)))
@@ -386,20 +437,21 @@
         scratch = ()
     else:
         blocks, width, _ = inverse.shape
+        tiles = blocks * len(upper_tiles(width // tile_of(width)))
         in_specs.append(pl.BlockSpec(memory_space=pl.ANY))
         operands.append(inverse)
         out_specs = [pl.BlockSpec((blocks, width, count), lambda u, me_ref: (0, 0, 0)), place]
         out_shape = [jax.ShapeDtypeStruct((blocks, width, count), F32), adjoint_shape]
         scratch = (
             pltpu.VMEM((depth, count), F32),
-            pltpu.VMEM(inverse.shape, F32),
-            pltpu.SemaphoreType.DMA(()),
+            pltpu.VMEM((tiles, tile_of(width), tile_of(width)), F32),
+            pltpu.SemaphoreType.DMA((tiles,)),
         )
         flops += 6 * inverse.size * count
         moved += 4 * inverse.size
     return call(
         functools.partial(
-            coupled_kernel, units, halves, adjoint is not None, inverse is not None
+            coupled_kernel, units, halves, strips, adjoint is not None, inverse is not None
         ),
         (units,),
         in_specs,
@@ -454,8 +506,11 @@
     reduced = reduced_of(
         shared_seed[0],
         [
-            halved(sum(term[term.shape[0] // 2 :] for term in pair), list(pair), order)
-            for *pair, order in zip(own, arrived, orders)
+            [sum(term[:1] for term in terms[:-1]), terms[-1]]
+            for terms in (
+                halved(sum(term[term.shape[0] // 2 :] for term in pair), list(pair), order)
+                for *pair, order in zip(own, arrived, orders)
+            )
         ],
     )
 

time: 203 us -> 206 us (1.015)
  Pallas kernels: 81.7 us -> 98.9 us
  local copies, waits for them, and re-layouts: 15.5 us -> 4.2 us
  starting transfers between devices: 41.2 us -> 39.1 us
    pallas_call x24, Pallas kernels: 81.7 us -> 98.9 us  [run(): pl.pallas_call(body, grid_spec=pltpu.PrefetchScalarGridSpec(num_scalar_pr...]
    unnamed x34 -> x6, local copies, waits for them, and re-layouts: 13.9 us -> 1.14 us
    ppermute x39, starting transfers between devices: 41.2 us -> 39.1 us  [exchange(): lax.ppermute(array, AXES, [(w, w ^ 1 << bit) for w in range(devices)])]
  transfers between devices with their start and end apart: 39 -> 39, of which waited for: 17 -> 16; matrix products, arithmetic and copies ran while one was open for 8% -> 9% of each run, Pallas kernels for 30% -> 36%
where the time goes in v2:
time: 206 us; the launch traced here: 204 us
  Pallas kernels  98.9 us (48%)
  waiting for transfers between devices  45.9 us (22%)
  starting transfers between devices  39.1 us (19%)
  other arithmetic  15 us (7%)
  local copies, waits for them, and re-layouts  4.2 us (2%)
    pallas_call x24, Pallas kernels, run(): pl.pallas_call(body, grid_spec=pltpu.PrefetchScalarGridSpec(num_scalar_pr...  98.9 us
    ppermute x39, waiting for transfers between devices, exchange(): lax.ppermute(array, AXES, [(w, w ^ 1 << bit) for w in range(devices)])  45.9 us
    ppermute x39, starting transfers between devices, exchange(): lax.ppermute(array, AXES, [(w, w ^ 1 << bit) for w in range(devices)])  39.1 us
    add x14, other arithmetic, halved(): away = sum((term[half:2 * half] for term in terms))  13.8 us
  transfers between devices with their start and end apart: 39, of which 16 were waited for; matrix products, arithmetic and copies ran while one was open for 9% of the time, Pallas kernels for 36%

profile of v2, /device:TPU:0, one launch (start us, length us, event | category | flops | bytes accessed | tf_op | source)
XLA Modules:
  0.0 204.1 jit_solution(12352675966538216253)
XLA Ops:
  0.6 4.3 %shard_map.68 = (f32[256,1536]{1,0:T(8,128)}, bf16[256,1536]{1,0:T(8,128)(2,1)}) custom-call(f32[2,768,256]{2,1,0:T(8,128)} %bitcast.261, f32[2,768,256]{2,1,0:T(8,128)} %bitcast.262, f32[2,768,256]{2,1,0:T(8,128)} %bitcast.263, f32[2,768,768]{2,1,0:T(8,128)} %bitcast.253, f32[2,768,768]{2,1,0:T(8,128)} %bitcast.254, f32[2,768,768]{2,1,0:T(8,128)} %bitcast.255, ...), custom_call_target="tpu_custom_call" | custom-call | flops 1811939328 | bytes 9437184 | tf_op jit(solution)/shard_map/pallas_call | solution.py:55
  5.0 1.1 copy-done
  6.1 3.7 %shard_map.70 = f32[4,256,256]{2,1,0:T(8,128)S(1)} custom-call(s32[1]{0:T(128)} %bitcast.me_ref, bf16[1536,4096]{1,0:T(8,128)(2,1)} %bitcast.205, bf16[1536,4096]{1,0:T(8,128)(2,1)} %bitcast.206, bf16[1536,4096]{1,0:T(8,128)(2,1)} %bitcast.207, bf16[1536,4096]{1,0:T(8,128)(2,1)} %bitcast.208, bf16[1536,4096]{1,0:T(8,128)(2,1)} %bitcast.209, ...), custom_call_target="tpu_custom_call" | custom-call | flops 805306368 | bytes 4194304 | tf_op jit(solution)/shard_map/pallas_call | solution.py:55
  10.4 3.7 %shard_map.71 = f32[4,256,256]{2,1,0:T(8,128)S(1)} custom-call(s32[1]{0:T(128)} %bitcast.me_ref, bf16[1536,4096]{1,0:T(8,128)(2,1)} %bitcast.211, bf16[1536,4096]{1,0:T(8,128)(2,1)} %bitcast.212, bf16[1536,4096]{1,0:T(8,128)(2,1)} %bitcast.213, bf16[1536,4096]{1,0:T(8,128)(2,1)} %bitcast.214, bf16[1536,4096]{1,0:T(8,128)(2,1)} %bitcast.215, ...), custom_call_target="tpu_custom_call" | custom-call | flops 805306368 | bytes 4194304 | tf_op jit(solution)/shard_map/pallas_call | solution.py:55
  14.3 5.5 %shard_map.69 = (f32[4,256,256]{2,1,0:T(8,128)S(1)}, f32[4,256,256]{2,1,0:T(8,128)}) custom-call(s32[1]{0:T(128)} %bitcast.me_ref, bf16[1536,4096]{1,0:T(8,128)(2,1)} %bitcast.217, bf16[1536,4096]{1,0:T(8,128)(2,1)} %bitcast.218, bf16[1536,4096]{1,0:T(8,128)(2,1)} %bitcast.219, bf16[1536,4096]{1,0:T(8,128)(2,1)} %bitcast.220, bf16[1536,4096]{1,0:T(8,128)(2,1)} %bitcast.221, ...), custom_call_target="tpu_custom_call" | custom-call | flops 1610612736 | bytes 8388608 | tf_op jit(solution)/shard_map/pallas_call | solution.py:55
  19.9 3.0 %collective-permute-start.1 = (f32[2,256,256]{2,1,0:T(8,128)S(1)}, f32[2,256,256]{2,1,0:T(8,128)S(1)}, u32[]{:S(2)}, u32[]{:S(2)}) collective-permute-start(f32[2,256,256]{2,1,0:T(8,128)S(1)} %slice_add_fusion.9), channel_id=1, source_target_pairs={{0,8},{1,9},{2,10},{3,11},{4,12},{5,13},{6,14},{7,15},{8,0},{9,1},... | collective-permute-start | bytes 1572872 | tf_op jit(solution)/shard_map/ppermute | solution.py:482
  22.8 1.1 slice_add_fusion.8
  24.0 1.6 collective-permute-start.4
  25.5 9.5 %collective-permute-done.1 = f32[2,256,256]{2,1,0:T(8,128)S(1)} collective-permute-done((f32[2,256,256]{2,1,0:T(8,128)S(1)}, f32[2,256,256]{2,1,0:T(8,128)S(1)}, u32[]{:S(2)}, u32[]{:S(2)}) %collective-permute-start.1) | collective-permute-done | bytes 524320 | tf_op jit(solution)/shard_map/ppermute | solution.py:482
  35.1 1.8 collective-permute-start.2
  38.6 4.7 %collective-permute-done.2.refs_1_ = f32[1,256,256]{2,1,0:T(8,128)S(1)} collective-permute-done((f32[1,256,256]{2,1,0:T(8,128)S(1)}, f32[1,256,256]{2,1,0:T(8,128)S(1)}, u32[]{:S(2)}, u32[]{:S(2)}) %collective-permute-start.2) | collective-permute-done | bytes 262176 | tf_op jit(solution)/shard_map/ppermute | solution.py:482
  43.3 1.7 collective-permute-done.5.refs_3_
  45.2 5.9 %shard_map.73 = f32[16,128,256]{2,1,0:T(8,128)} custom-call(s32[1]{0:T(128)} %bitcast.5.me_ref.refs_0_, f32[32,2048,128]{2,1,0:T(8,128)} %bitcast.28, f32[32,2048,128]{2,1,0:T(8,128)} %bitcast.14, f32[32,2048,128]{2,1,0:T(8,128)} %bitcast.15, f32[32,2048,128]{2,1,0:T(8,128)} %bitcast.16, f32[32,2048,128]{2,1,0:T(8,128)} %bitcast.17, ...), custom_call_target="tpu_custom_call" | custom-call | flops 1610612736 | bytes 6291456 | tf_op jit(solution)/shard_map/pallas_call | solution.py:55
  51.2 5.9 %shard_map.75 = f32[16,128,256]{2,1,0:T(8,128)} custom-call(s32[1]{0:T(128)} %bitcast.5.me_ref.refs_0_, f32[32,2048,128]{2,1,0:T(8,128)} %bitcast.29, f32[32,2048,128]{2,1,0:T(8,128)} %bitcast.30, f32[32,2048,128]{2,1,0:T(8,128)} %bitcast.31, f32[32,2048,128]{2,1,0:T(8,128)} %bitcast.32, f32[32,2048,128]{2,1,0:T(8,128)} %bitcast.33, ...), custom_call_target="tpu_custom_call" | custom-call | flops 1610612736 | bytes 6291456 | tf_op jit(solution)/shard_map/pallas_call | solution.py:55
  57.6 5.9 %shard_map.77 = f32[16,128,256]{2,1,0:T(8,128)} custom-call(s32[1]{0:T(128)} %bitcast.5.me_ref.refs_0_, f32[32,2048,128]{2,1,0:T(8,128)} %bitcast.52, f32[32,2048,128]{2,1,0:T(8,128)} %bitcast.46, f32[32,2048,128]{2,1,0:T(8,128)} %bitcast.47, f32[32,2048,128]{2,1,0:T(8,128)} %bitcast.48, f32[32,2048,128]{2,1,0:T(8,128)} %bitcast.49, ...), custom_call_target="tpu_custom_call" | custom-call | flops 1610612736 | bytes 6291456 | tf_op jit(solution)/shard_map/pallas_call | solution.py:55
  63.6 5.9 %shard_map.79 = f32[16,128,256]{2,1,0:T(8,128)} custom-call(s32[1]{0:T(128)} %bitcast.5.me_ref.refs_0_, f32[32,2048,128]{2,1,0:T(8,128)} %bitcast.69, f32[32,2048,128]{2,1,0:T(8,128)} %bitcast.62, f32[32,2048,128]{2,1,0:T(8,128)} %bitcast.63, f32[32,2048,128]{2,1,0:T(8,128)} %bitcast.64, f32[32,2048,128]{2,1,0:T(8,128)} %bitcast.65, ...), custom_call_target="tpu_custom_call" | custom-call | flops 1610612736 | bytes 6291456 | tf_op jit(solution)/shard_map/pallas_call | solution.py:55
  70.0 4.1 %shard_map.74.refs_18_ = f32[8,128,256]{2,1,0:T(8,128)} custom-call(s32[1]{0:T(128)} %bitcast.5.me_ref.refs_0_, f32[32,2048,128]{2,1,0:T(8,128)} %bitcast.77, f32[32,2048,128]{2,1,0:T(8,128)} %bitcast.78, f32[32,2048,128]{2,1,0:T(8,128)} %bitcast.79, f32[32,2048,128]{2,1,0:T(8,128)} %bitcast.80, f32[32,2048,128]{2,1,0:T(8,128)} %bitcast.81, ...), custom_call_target="tpu_custom_call" | custom-call | flops 805306368 | bytes 3145728 | tf_op jit(solution)/shard_map/pallas_call | solution.py:55
  75.0 4.1 %shard_map.76.refs_19_ = f32[8,128,256]{2,1,0:T(8,128)} custom-call(s32[1]{0:T(128)} %bitcast.5.me_ref.refs_0_, f32[32,2048,128]{2,1,0:T(8,128)} %bitcast.108, f32[32,2048,128]{2,1,0:T(8,128)} %bitcast.94, f32[32,2048,128]{2,1,0:T(8,128)} %bitcast.95, f32[32,2048,128]{2,1,0:T(8,128)} %bitcast.96, f32[32,2048,128]{2,1,0:T(8,128)} %bitcast.97, ...), custom_call_target="tpu_custom_call" | custom-call | flops 805306368 | bytes 3145728 | tf_op jit(solution)/shard_map/pallas_call | solution.py:55
  79.1 1.3 collective-permute-start.14
  80.4 4.1 %shard_map.78.refs_20_ = f32[8,128,256]{2,1,0:T(8,128)} custom-call(s32[1]{0:T(128)} %bitcast.5.me_ref.refs_0_, f32[32,2048,128]{2,1,0:T(8,128)} %bitcast.117, f32[32,2048,128]{2,1,0:T(8,128)} %bitcast.110, f32[32,2048,128]{2,1,0:T(8,128)} %bitcast.111, f32[32,2048,128]{2,1,0:T(8,128)} %bitcast.112, f32[32,2048,128]{2,1,0:T(8,128)} %bitcast.113, ...), custom_call_target="tpu_custom_call" | custom-call | flops 805306368 | bytes 3145728 | tf_op jit(solution)/shard_map/pallas_call | solution.py:55
  84.4 1.6 collective-permute-start.18
  86.1 4.1 %shard_map.80.refs_21_ = f32[8,128,256]{2,1,0:T(8,128)} custom-call(s32[1]{0:T(128)} %bitcast.5.me_ref.refs_0_, f32[32,2048,128]{2,1,0:T(8,128)} %bitcast.125, f32[32,2048,128]{2,1,0:T(8,128)} %bitcast.126, f32[32,2048,128]{2,1,0:T(8,128)} %bitcast.127, f32[32,2048,128]{2,1,0:T(8,128)} %bitcast.128, f32[32,2048,128]{2,1,0:T(8,128)} %bitcast.129, ...), custom_call_target="tpu_custom_call" | custom-call | flops 805306368 | bytes 3145728 | tf_op jit(solution)/shard_map/pallas_call | solution.py:55
  90.1 1.6 collective-permute-start.22
  91.7 3.3 %shard_map.81.refs_0_ = f32[8,128,256]{2,1,0:T(8,128)S(1)} custom-call(s32[1]{0:T(128)} %bitcast.5.me_ref.refs_0_, f32[32,2048,128]{2,1,0:T(8,128)} %bitcast.149, f32[32,2048,128]{2,1,0:T(8,128)} %bitcast.142, f32[32,2048,128]{2,1,0:T(8,128)} %bitcast.143, f32[32,2048,128]{2,1,0:T(8,128)} %bitcast.144, f32[32,2048,128]{2,1,0:T(8,128)} %bitcast.145, ...), custom_call_target="tpu_custom_call" | custom-call | flops 805306368 | bytes 3145728 | tf_op jit(solution)/shard_map/pallas_call | solution.py:55
  95.0 3.2 %shard_map.82.refs_6_ = f32[8,128,256]{2,1,0:T(8,128)S(1)} custom-call(s32[1]{0:T(128)} %bitcast.5.me_ref.refs_0_, f32[32,2048,128]{2,1,0:T(8,128)} %bitcast.157, f32[32,2048,128]{2,1,0:T(8,128)} %bitcast.158, f32[32,2048,128]{2,1,0:T(8,128)} %bitcast.159, f32[32,2048,128]{2,1,0:T(8,128)} %bitcast.160, f32[32,2048,128]{2,1,0:T(8,128)} %bitcast.161, ...), custom_call_target="tpu_custom_call" | custom-call | flops 805306368 | bytes 3145728 | tf_op jit(solution)/shard_map/pallas_call | solution.py:55
  98.2 3.2 %shard_map.84.refs_0_ = f32[8,128,256]{2,1,0:T(8,128)S(1)} custom-call(s32[1]{0:T(128)} %bitcast.5.me_ref.refs_0_, f32[32,2048,128]{2,1,0:T(8,128)} %bitcast.173, f32[32,2048,128]{2,1,0:T(8,128)} %bitcast.174, f32[32,2048,128]{2,1,0:T(8,128)} %bitcast.175, f32[32,2048,128]{2,1,0:T(8,128)} %bitcast.176, f32[32,2048,128]{2,1,0:T(8,128)} %bitcast.177, ...), custom_call_target="tpu_custom_call" | custom-call | flops 805306368 | bytes 3145728 | tf_op jit(solution)/shard_map/pallas_call | solution.py:55
  101.4 3.2 %shard_map.85.refs_6_ = f32[8,128,256]{2,1,0:T(8,128)S(1)} custom-call(s32[1]{0:T(128)} %bitcast.5.me_ref.refs_0_, f32[32,2048,128]{2,1,0:T(8,128)} %bitcast.189, f32[32,2048,128]{2,1,0:T(8,128)} %bitcast.190, f32[32,2048,128]{2,1,0:T(8,128)} %bitcast.191, f32[32,2048,128]{2,1,0:T(8,128)} %bitcast.192, f32[32,2048,128]{2,1,0:T(8,128)} %bitcast.193, ...), custom_call_target="tpu_custom_call" | custom-call | flops 805306368 | bytes 3145728 | tf_op jit(solution)/shard_map/pallas_call | solution.py:55
  104.6 1.3 slice_add_fusion.6
  106.5 1.3 slice_add_fusion.4
  108.3 1.4 collective-permute-done.18.refs_2_
  109.7 1.3 slice_add_fusion.2
  111.0 2.0 collective-permute-start.19
  113.0 10.0 %collective-permute-done.22.refs_8_ = f32[8,128,256]{2,1,0:T(8,128)} collective-permute-done((f32[8,128,256]{2,1,0:T(8,128)}, f32[8,128,256]{2,1,0:T(8,128)}, u32[]{:S(2)}, u32[]{:S(2)}) %collective-permute-start.22) | collective-permute-done | bytes 1048608 | tf_op jit(solution)/shard_map/ppermute | solution.py:482
  123.0 1.3 slice_add_fusion
  124.3 1.6 collective-permute-start.23
  125.9 1.1 slice_add_fusion.19
  127.0 1.7 collective-permute-start.12
  128.6 1.1 slice_add_fusion.16
  129.7 2.6 %collective-permute-start.16 = (f32[2,128,256]{2,1,0:T(8,128)S(1)}, f32[2,128,256]{2,1,0:T(8,128)S(1)}, u32[]{:S(2)}, u32[]{:S(2)}) collective-permute-start(f32[2,128,256]{2,1,0:T(8,128)S(1)} %slice_add_fusion.16), channel_id=1, source_target_pairs={{0,2},{1,3},{2,0},{3,1},{4,6},{5,7},{6,4},{7,5},{8,10},{9,11},{10,... | collective-permute-start | bytes 786440 | tf_op jit(solution)/shard_map/ppermute | solution.py:482
  133.2 1.1 slice_add_fusion.13
  134.3 1.6 collective-permute-start.20
  136.7 1.1 slice_add_fusion.10
  137.8 1.6 collective-permute-start.24
  139.4 1.0 slice_add_fusion.42
  140.5 2.7 %collective-permute-start.13 = (f32[1,128,256]{2,1,0:T(8,128)S(1)}, f32[1,128,256]{2,1,0:T(8,128)S(1)}, u32[]{:S(2)}, u32[]{:S(2)}) collective-permute-start(f32[1,128,256]{2,1,0:T(8,128)S(1)} %slice_add_fusion.42), channel_id=1, source_target_pairs={{0,2},{1,3},{2,0},{3,1},{4,6},{5,7},{6,4},{7,5},{8,10},{9,11},{10,... | collective-permute-start | bytes 393224 | tf_op jit(solution)/shard_map/ppermute | solution.py:482
  143.1 1.0 slice_add_fusion.38
  145.0 1.0 slice_add_fusion.34
  146.4 2.5 %collective-permute-done.24.refs_10_ = f32[2,128,256]{2,1,0:T(8,128)S(1)} collective-permute-done((f32[2,128,256]{2,1,0:T(8,128)S(1)}, f32[2,128,256]{2,1,0:T(8,128)S(1)}, u32[]{:S(2)}, u32[]{:S(2)}) %collective-permute-start.24) | collective-permute-done | bytes 262176 | tf_op jit(solution)/shard_map/ppermute | solution.py:482
  148.9 1.0 slice_add_fusion.30
  150.0 2.3 %collective-permute-start.25 = (f32[1,128,256]{2,1,0:T(8,128)S(1)}, f32[1,128,256]{2,1,0:T(8,128)S(1)}, u32[]{:S(2)}, u32[]{:S(2)}) collective-permute-start(f32[1,128,256]{2,1,0:T(8,128)S(1)} %slice_add_fusion.30), channel_id=1, source_target_pairs={{0,2},{1,3},{2,0},{3,1},{4,6},{5,7},{6,4},{7,5},{8,10},{9,11},{10,... | collective-permute-start | bytes 393224 | tf_op jit(solution)/shard_map/ppermute | solution.py:482
  152.2 1.3 shard_map.83.refs_7_
  154.3 3.6 %collective-permute-done.21.refs_5_ = f32[1,128,256]{2,1,0:T(8,128)S(1)} collective-permute-done((f32[1,128,256]{2,1,0:T(8,128)S(1)}, f32[1,128,256]{2,1,0:T(8,128)S(1)}, u32[]{:S(2)}, u32[]{:S(2)}) %collective-permute-start.21) | collective-permute-done | bytes 131104 | tf_op jit(solution)/shard_map/ppermute | solution.py:482
  157.9 2.0 collective-permute-done.25.refs_11_
  159.9 1.3 shard_map.86.refs_8_
  161.9 1.0 collective-permute-start.29
  162.9 1.1 collective-permute-start.30
  165.0 5.5 %collective-permute-done.31.refs_10_ = f32[256,256]{1,0:T(8,128)S(1)} collective-permute-done((f32[256,256]{1,0:T(8,128)S(1)}, f32[256,256]{1,0:T(8,128)S(1)}, u32[]{:S(2)}, u32[]{:S(2)}) %collective-permute-start.31) | collective-permute-done | bytes 262176 | tf_op jit(solution)/shard_map/ppermute | solution.py:482
  171.3 3.1 %copy.11 = f32[256,1536]{0,1:T(8,128)} copy(f32[256,1536]{1,0:T(8,128)} %get-tuple-element.17) | data formatting | bytes 3145728 | tf_op jit(solution)/shard_map/pallas_call | solution.py:55
  174.3 4.9 %shard_map.87 = (f32[1536,256]{1,0:T(8,128)}, f32[4096,256]{1,0:T(8,128)}, f32[2,512,256]{2,1,0:T(8,128)}) custom-call(s32[1]{0:T(128)} %bitcast.me_ref, bf16[1536,4096]{1,0:T(8,128)(2,1)} %bitcast.228, bf16[1536,4096]{1,0:T(8,128)(2,1)} %bitcast.224, bf16[1536,4096]{1,0:T(8,128)(2,1)} %bitcast.225, bf16[1536,4096]{1,0:T(8,128)(2,1)} %bitcast.226, ...), custom_call_target="tpu_custom_call" | custom-call | flops 805306368 | bytes 8388608 | tf_op jit(solution)/shard_map/pallas_call | solution.py:55
  179.2 4.9 %shard_map.88 = (f32[1536,256]{1,0:T(8,128)}, f32[4096,256]{1,0:T(8,128)}, f32[2,512,256]{2,1,0:T(8,128)}) custom-call(s32[1]{0:T(128)} %bitcast.me_ref, bf16[1536,4096]{1,0:T(8,128)(2,1)} %bitcast.229, bf16[1536,4096]{1,0:T(8,128)(2,1)} %bitcast.230, bf16[1536,4096]{1,0:T(8,128)(2,1)} %bitcast.231, ...), custom_call_target="tpu_custom_call", output_to_operand_aliasing={{1}: (12, {})} | custom-call | flops 805306368 | bytes 8388608 | tf_op jit(solution)/shard_map/pallas_call | solution.py:55
  184.2 3.7 %shard_map.89 = (f32[1536,256]{1,0:T(8,128)}, f32[4096,256]{1,0:T(8,128)}, f32[1,512,256]{2,1,0:T(8,128)S(1)}) custom-call(s32[1]{0:T(128)} %bitcast.me_ref, bf16[1536,4096]{1,0:T(8,128)(2,1)} %bitcast.238, bf16[1536,4096]{1,0:T(8,128)(2,1)} %bitcast.236, bf16[1536,4096]{1,0:T(8,128)(2,1)} %bitcast.237, ...), custom_call_target="tpu_custom_call", output_to_operand_aliasing={{1}: (10, {})} | custom-call | flops 402653184 | bytes 5767168 | tf_op jit(solution)/shard_map/pallas_call | solution.py:55
  188.9 1.3 collective-permute-done.34.refs_7_
  191.2 4.9 %shard_map.90 = (f32[1536,256]{1,0:T(8,128)}, f32[4096,256]{1,0:T(8,128)}, f32[2,512,256]{2,1,0:T(8,128)}) custom-call(s32[1]{0:T(128)} %bitcast.me_ref, bf16[1536,4096]{1,0:T(8,128)(2,1)} %bitcast.241, bf16[1536,4096]{1,0:T(8,128)(2,1)} %bitcast.242, bf16[1536,4096]{1,0:T(8,128)(2,1)} %bitcast.243, ...), custom_call_target="tpu_custom_call", output_to_operand_aliasing={{1}: (12, {})} | custom-call | flops 805306368 | bytes 8388608 | tf_op jit(solution)/shard_map/pallas_call | solution.py:55
  196.2 7.8 %shard_map.91 = (f32[2,768,256]{2,1,0:T(8,128)}, f32[4096,256]{1,0:T(8,128)}) custom-call(s32[1]{0:T(128)} %bitcast.me_ref, bf16[1536,4096]{1,0:T(8,128)(2,1)} %bitcast.247, bf16[1536,4096]{1,0:T(8,128)(2,1)} %bitcast.248, bf16[1536,4096]{1,0:T(8,128)(2,1)} %bitcast.249, bf16[1536,4096]{1,0:T(8,128)(2,1)} %bitcast.250, ...), custom_call_target="tpu_custom_call", output_to_operand_aliasing={{1}: (9, {})} | custom-call | flops 2214592512 | bytes 10485760 | tf_op jit(solution)/shard_map/pallas_call | solution.py:55
  (61 shorter events, 14.4 us)
Async XLA Ops:
  5.0 1.1 copy-start
  9.9 9.9 %collective-permute-start = (f32[4,256,256]{2,1,0:T(8,128)S(1)}, f32[4,256,256]{2,1,0:T(8,128)S(1)}, u32[]{:S(2)}, u32[]{:S(2)}) collective-permute-start(f32[4,256,256]{2,1,0:T(8,128)S(1)} %shard_map.70), channel_id=1, source_target_pairs={{0,4},{1,5},{2,6},{3,7},{4,0},{5,1},{6,2},{7,3},{8,12},{9,13},{10,... | collective-permute-start | bytes 3145736 | tf_op jit(solution)/shard_map/ppermute | solution.py:482
  14.2 8.7 %collective-permute-start.3 = (f32[4,256,256]{2,1,0:T(8,128)S(1)}, f32[4,256,256]{2,1,0:T(8,128)S(1)}, u32[]{:S(2)}, u32[]{:S(2)}) collective-permute-start(f32[4,256,256]{2,1,0:T(8,128)S(1)} %shard_map.71), channel_id=1, source_target_pairs={{0,4},{1,5},{2,6},{3,7},{4,0},{5,1},{6,2},{7,3},{8,12},{9,13},{10,... | collective-permute-start | bytes 3145736 | tf_op jit(solution)/shard_map/ppermute | solution.py:482
  19.9 18.1 %copy-start.2 = (f32[4,256,256]{2,1,0:T(8,128)S(1)}, f32[4,256,256]{2,1,0:T(8,128)}, u32[]{:S(2)}) copy-start(f32[4,256,256]{2,1,0:T(8,128)} %get-tuple-element.20) | copy-start | bytes 3145732
  19.9 15.2 %collective-permute-start.1 = (f32[2,256,256]{2,1,0:T(8,128)S(1)}, f32[2,256,256]{2,1,0:T(8,128)S(1)}, u32[]{:S(2)}, u32[]{:S(2)}) collective-permute-start(f32[2,256,256]{2,1,0:T(8,128)S(1)} %slice_add_fusion.9), channel_id=1, source_target_pairs={{0,8},{1,9},{2,10},{3,11},{4,12},{5,13},{6,14},{7,15},{8,0},{9,1},... | collective-permute-start | bytes 1572872 | tf_op jit(solution)/shard_map/ppermute | solution.py:482
  24.0 21.0 %copy-start.1 = (f32[1,512,256]{2,1,0:T(8,128)S(1)}, f32[1,512,256]{2,1,0:T(8,128)}, u32[]{:S(2)}) copy-start(f32[1,512,256]{2,1,0:T(8,128)} %param.8) | copy-start | bytes 1572868
  24.0 13.9 %collective-permute-start.4 = (f32[2,256,256]{2,1,0:T(8,128)S(1)}, f32[2,256,256]{2,1,0:T(8,128)S(1)}, u32[]{:S(2)}, u32[]{:S(2)}) collective-permute-start(f32[2,256,256]{2,1,0:T(8,128)S(1)} %slice_add_fusion.8), channel_id=1, source_target_pairs={{0,16},{1,17},{2,18},{3,19},{4,20},{5,21},{6,22},{7,23},{8,24},{9,... | collective-permute-start | bytes 1572872 | tf_op jit(solution)/shard_map/ppermute | solution.py:482
  35.1 8.2 %collective-permute-start.2 = (f32[1,256,256]{2,1,0:T(8,128)S(1)}, f32[1,256,256]{2,1,0:T(8,128)S(1)}, u32[]{:S(2)}, u32[]{:S(2)}) collective-permute-start(f32[1,256,256]{2,1,0:T(8,128)S(1)} %get-tuple-element.34), channel_id=1, source_target_pairs={{0,16},{1,17},{2,18},{3,19},{4,20},{5,21},{6,22},{7,23},{8,24},{9,... | collective-permute-start | bytes 786440 | tf_op jit(solution)/shard_map/ppermute | solution.py:482
  38.0 7.0 %collective-permute-start.5 = (f32[1,256,256]{2,1,0:T(8,128)S(1)}, f32[1,256,256]{2,1,0:T(8,128)S(1)}, u32[]{:S(2)}, u32[]{:S(2)}) collective-permute-start(f32[1,256,256]{2,1,0:T(8,128)S(1)} %get-tuple-element.32), channel_id=1, source_target_pairs={{0,8},{1,9},{2,10},{3,11},{4,12},{5,13},{6,14},{7,15},{8,0},{9,1},... | collective-permute-start | bytes 786440 | tf_op jit(solution)/shard_map/ppermute | solution.py:482
  51.1 18.9 %collective-permute-start.6 = (f32[16,128,256]{2,1,0:T(8,128)}, f32[16,128,256]{2,1,0:T(8,128)}, u32[]{:S(2)}, u32[]{:S(2)}) collective-permute-start(f32[16,128,256]{2,1,0:T(8,128)} %shard_map.73), channel_id=1, source_target_pairs={{0,4},{1,5},{2,6},{3,7},{4,0},{5,1},{6,2},{7,3},{8,12},{9,13},{10,... | collective-permute-start | bytes 6291464 | tf_op jit(solution)/shard_map/ppermute | solution.py:482
  57.1 17.9 %collective-permute-start.7 = (f32[16,128,256]{2,1,0:T(8,128)}, f32[16,128,256]{2,1,0:T(8,128)}, u32[]{:S(2)}, u32[]{:S(2)}) collective-permute-start(f32[16,128,256]{2,1,0:T(8,128)} %shard_map.75), channel_id=1, source_target_pairs={{0,4},{1,5},{2,6},{3,7},{4,0},{5,1},{6,2},{7,3},{8,12},{9,13},{10,... | collective-permute-start | bytes 6291464 | tf_op jit(solution)/shard_map/ppermute | solution.py:482
  63.5 16.8 %collective-permute-start.8 = (f32[16,128,256]{2,1,0:T(8,128)}, f32[16,128,256]{2,1,0:T(8,128)}, u32[]{:S(2)}, u32[]{:S(2)}) collective-permute-start(f32[16,128,256]{2,1,0:T(8,128)} %shard_map.77), channel_id=1, source_target_pairs={{0,4},{1,5},{2,6},{3,7},{4,0},{5,1},{6,2},{7,3},{8,12},{9,13},{10,... | collective-permute-start | bytes 6291464 | tf_op jit(solution)/shard_map/ppermute | solution.py:482
  69.5 16.6 %collective-permute-start.9 = (f32[16,128,256]{2,1,0:T(8,128)}, f32[16,128,256]{2,1,0:T(8,128)}, u32[]{:S(2)}, u32[]{:S(2)}) collective-permute-start(f32[16,128,256]{2,1,0:T(8,128)} %shard_map.79), channel_id=1, source_target_pairs={{0,4},{1,5},{2,6},{3,7},{4,0},{5,1},{6,2},{7,3},{8,12},{9,13},{10,... | collective-permute-start | bytes 6291464 | tf_op jit(solution)/shard_map/ppermute | solution.py:482
  74.1 30.5 %collective-permute-start.10 = (f32[8,128,256]{2,1,0:T(8,128)}, f32[8,128,256]{2,1,0:T(8,128)}, u32[]{:S(2)}, u32[]{:S(2)}) collective-permute-start(f32[8,128,256]{2,1,0:T(8,128)} %shard_map.74.refs_18_), channel_id=1, source_target_pairs={{0,8},{1,9},{2,10},{3,11},{4,12},{5,13},{6,14},{7,15},{8,0},{9,1},... | collective-permute-start | bytes 3145736 | tf_op jit(solution)/shard_map/ppermute | solution.py:482
  79.1 27.4 %collective-permute-start.14 = (f32[8,128,256]{2,1,0:T(8,128)}, f32[8,128,256]{2,1,0:T(8,128)}, u32[]{:S(2)}, u32[]{:S(2)}) collective-permute-start(f32[8,128,256]{2,1,0:T(8,128)} %shard_map.76.refs_19_), channel_id=1, source_target_pairs={{0,16},{1,17},{2,18},{3,19},{4,20},{5,21},{6,22},{7,23},{8,24},{9,... | collective-permute-start | bytes 3145736 | tf_op jit(solution)/shard_map/ppermute | solution.py:482
  84.4 25.3 %collective-permute-start.18 = (f32[8,128,256]{2,1,0:T(8,128)}, f32[8,128,256]{2,1,0:T(8,128)}, u32[]{:S(2)}, u32[]{:S(2)}) collective-permute-start(f32[8,128,256]{2,1,0:T(8,128)} %shard_map.78.refs_20_), channel_id=1, source_target_pairs={{0,1},{1,0},{2,3},{3,2},{4,5},{5,4},{6,7},{7,6},{8,9},{9,8},{10,11... | collective-permute-start | bytes 3145736 | tf_op jit(solution)/shard_map/ppermute | solution.py:482
  90.1 32.8 %collective-permute-start.22 = (f32[8,128,256]{2,1,0:T(8,128)}, f32[8,128,256]{2,1,0:T(8,128)}, u32[]{:S(2)}, u32[]{:S(2)}) collective-permute-start(f32[8,128,256]{2,1,0:T(8,128)} %shard_map.80.refs_21_), channel_id=1, source_target_pairs={{0,8},{1,9},{2,10},{3,11},{4,12},{5,13},{6,14},{7,15},{8,0},{9,1},... | collective-permute-start | bytes 3145736 | tf_op jit(solution)/shard_map/ppermute | solution.py:482
  105.9 20.0 %collective-permute-start.11 = (f32[4,128,256]{2,1,0:T(8,128)S(1)}, f32[4,128,256]{2,1,0:T(8,128)S(1)}, u32[]{:S(2)}, u32[]{:S(2)}) collective-permute-start(f32[4,128,256]{2,1,0:T(8,128)S(1)} %slice_add_fusion.6), channel_id=1, source_target_pairs={{0,16},{1,17},{2,18},{3,19},{4,20},{5,21},{6,22},{7,23},{8,24},{9,... | collective-permute-start | bytes 1572872 | tf_op jit(solution)/shard_map/ppermute | solution.py:482
  107.8 20.8 %collective-permute-start.15 = (f32[4,128,256]{2,1,0:T(8,128)S(1)}, f32[4,128,256]{2,1,0:T(8,128)S(1)}, u32[]{:S(2)}, u32[]{:S(2)}) collective-permute-start(f32[4,128,256]{2,1,0:T(8,128)S(1)} %slice_add_fusion.4), channel_id=1, source_target_pairs={{0,1},{1,0},{2,3},{3,2},{4,5},{5,4},{6,7},{7,6},{8,9},{9,8},{10,11... | collective-permute-start | bytes 1572872 | tf_op jit(solution)/shard_map/ppermute | solution.py:482
  111.0 22.2 %collective-permute-start.19 = (f32[4,128,256]{2,1,0:T(8,128)S(1)}, f32[4,128,256]{2,1,0:T(8,128)S(1)}, u32[]{:S(2)}, u32[]{:S(2)}) collective-permute-start(f32[4,128,256]{2,1,0:T(8,128)S(1)} %slice_add_fusion.2), channel_id=1, source_target_pairs={{0,8},{1,9},{2,10},{3,11},{4,12},{5,13},{6,14},{7,15},{8,0},{9,1},... | collective-permute-start | bytes 1572872 | tf_op jit(solution)/shard_map/ppermute | solution.py:482
  124.3 12.4 %collective-permute-start.23 = (f32[4,128,256]{2,1,0:T(8,128)S(1)}, f32[4,128,256]{2,1,0:T(8,128)S(1)}, u32[]{:S(2)}, u32[]{:S(2)}) collective-permute-start(f32[4,128,256]{2,1,0:T(8,128)S(1)} %slice_add_fusion), channel_id=1, source_target_pairs={{0,16},{1,17},{2,18},{3,19},{4,20},{5,21},{6,22},{7,23},{8,24},{9,... | collective-permute-start | bytes 1572872 | tf_op jit(solution)/shard_map/ppermute | solution.py:482
  127.0 12.5 %collective-permute-start.12 = (f32[2,128,256]{2,1,0:T(8,128)S(1)}, f32[2,128,256]{2,1,0:T(8,128)S(1)}, u32[]{:S(2)}, u32[]{:S(2)}) collective-permute-start(f32[2,128,256]{2,1,0:T(8,128)S(1)} %slice_add_fusion.19), channel_id=1, source_target_pairs={{0,1},{1,0},{2,3},{3,2},{4,5},{5,4},{6,7},{7,6},{8,9},{9,8},{10,11... | collective-permute-start | bytes 786440 | tf_op jit(solution)/shard_map/ppermute | solution.py:482
  129.7 13.4 %collective-permute-start.16 = (f32[2,128,256]{2,1,0:T(8,128)S(1)}, f32[2,128,256]{2,1,0:T(8,128)S(1)}, u32[]{:S(2)}, u32[]{:S(2)}) collective-permute-start(f32[2,128,256]{2,1,0:T(8,128)S(1)} %slice_add_fusion.16), channel_id=1, source_target_pairs={{0,2},{1,3},{2,0},{3,1},{4,6},{5,7},{6,4},{7,5},{8,10},{9,11},{10,... | collective-permute-start | bytes 786440 | tf_op jit(solution)/shard_map/ppermute | solution.py:482
  134.3 10.7 %collective-permute-start.20 = (f32[2,128,256]{2,1,0:T(8,128)S(1)}, f32[2,128,256]{2,1,0:T(8,128)S(1)}, u32[]{:S(2)}, u32[]{:S(2)}) collective-permute-start(f32[2,128,256]{2,1,0:T(8,128)S(1)} %slice_add_fusion.13), channel_id=1, source_target_pairs={{0,16},{1,17},{2,18},{3,19},{4,20},{5,21},{6,22},{7,23},{8,24},{9,... | collective-permute-start | bytes 786440 | tf_op jit(solution)/shard_map/ppermute | solution.py:482
  137.8 11.1 %collective-permute-start.24 = (f32[2,128,256]{2,1,0:T(8,128)S(1)}, f32[2,128,256]{2,1,0:T(8,128)S(1)}, u32[]{:S(2)}, u32[]{:S(2)}) collective-permute-start(f32[2,128,256]{2,1,0:T(8,128)S(1)} %slice_add_fusion.10), channel_id=1, source_target_pairs={{0,1},{1,0},{2,3},{3,2},{4,5},{5,4},{6,7},{7,6},{8,9},{9,8},{10,11... | collective-permute-start | bytes 786440 | tf_op jit(solution)/shard_map/ppermute | solution.py:482
  140.5 11.8 %collective-permute-start.13 = (f32[1,128,256]{2,1,0:T(8,128)S(1)}, f32[1,128,256]{2,1,0:T(8,128)S(1)}, u32[]{:S(2)}, u32[]{:S(2)}) collective-permute-start(f32[1,128,256]{2,1,0:T(8,128)S(1)} %slice_add_fusion.42), channel_id=1, source_target_pairs={{0,2},{1,3},{2,0},{3,1},{4,6},{5,7},{6,4},{7,5},{8,10},{9,11},{10,... | collective-permute-start | bytes 393224 | tf_op jit(solution)/shard_map/ppermute | solution.py:482
  144.1 8.1 %collective-permute-start.17 = (f32[1,128,256]{2,1,0:T(8,128)S(1)}, f32[1,128,256]{2,1,0:T(8,128)S(1)}, u32[]{:S(2)}, u32[]{:S(2)}) collective-permute-start(f32[1,128,256]{2,1,0:T(8,128)S(1)} %slice_add_fusion.38), channel_id=1, source_target_pairs={{0,8},{1,9},{2,10},{3,11},{4,12},{5,13},{6,14},{7,15},{8,0},{9,1},... | collective-permute-start | bytes 393224 | tf_op jit(solution)/shard_map/ppermute | solution.py:482
  146.0 11.9 %collective-permute-start.21 = (f32[1,128,256]{2,1,0:T(8,128)S(1)}, f32[1,128,256]{2,1,0:T(8,128)S(1)}, u32[]{:S(2)}, u32[]{:S(2)}) collective-permute-start(f32[1,128,256]{2,1,0:T(8,128)S(1)} %slice_add_fusion.34), channel_id=1, source_target_pairs={{0,2},{1,3},{2,0},{3,1},{4,6},{5,7},{6,4},{7,5},{8,10},{9,11},{10,... | collective-permute-start | bytes 393224 | tf_op jit(solution)/shard_map/ppermute | solution.py:482
  150.0 9.9 %collective-permute-start.25 = (f32[1,128,256]{2,1,0:T(8,128)S(1)}, f32[1,128,256]{2,1,0:T(8,128)S(1)}, u32[]{:S(2)}, u32[]{:S(2)}) collective-permute-start(f32[1,128,256]{2,1,0:T(8,128)S(1)} %slice_add_fusion.30), channel_id=1, source_target_pairs={{0,2},{1,3},{2,0},{3,1},{4,6},{5,7},{6,4},{7,5},{8,10},{9,11},{10,... | collective-permute-start | bytes 393224 | tf_op jit(solution)/shard_map/ppermute | solution.py:482
  153.5 9.4 %collective-permute-start.26 = (f32[256,256]{1,0:T(8,128)S(1)}, f32[256,256]{1,0:T(8,128)S(1)}, u32[]{:S(2)}, u32[]{:S(2)}) collective-permute-start(f32[256,256]{1,0:T(8,128)S(1)} %shard_map.83.refs_7_), channel_id=1, source_target_pairs={{0,4},{1,5},{2,6},{3,7},{4,0},{5,1},{6,2},{7,3},{8,12},{9,13},{10,... | collective-permute-start | bytes 786440 | tf_op jit(solution)/shard_map/ppermute | solution.py:482
  153.6 10.4 %collective-permute-start.28 = (f32[256,256]{1,0:T(8,128)S(1)}, f32[256,256]{1,0:T(8,128)S(1)}, u32[]{:S(2)}, u32[]{:S(2)}) collective-permute-start(f32[256,256]{1,0:T(8,128)S(1)} %shard_map.83.refs_7_), channel_id=1, source_target_pairs={{0,8},{1,9},{2,10},{3,11},{4,12},{5,13},{6,14},{7,15},{8,0},{9,1},... | collective-permute-start | bytes 786440 | tf_op jit(solution)/shard_map/ppermute | solution.py:482
  161.2 9.3 %collective-permute-start.31 = (f32[256,256]{1,0:T(8,128)S(1)}, f32[256,256]{1,0:T(8,128)S(1)}, u32[]{:S(2)}, u32[]{:S(2)}) collective-permute-start(f32[256,256]{1,0:T(8,128)S(1)} %shard_map.86.refs_8_), channel_id=1, source_target_pairs={{0,16},{1,17},{2,18},{3,19},{4,20},{5,21},{6,22},{7,23},{8,24},{9,... | collective-permute-start | bytes 786440 | tf_op jit(solution)/shard_map/ppermute | solution.py:482
  161.9 12.4 %collective-permute-start.27 = (f32[256,256]{1,0:T(8,128)S(1)}, f32[256,256]{1,0:T(8,128)S(1)}, u32[]{:S(2)}, u32[]{:S(2)}) collective-permute-start(f32[256,256]{1,0:T(8,128)S(1)} %shard_map.86.refs_8_), channel_id=1, source_target_pairs={{0,4},{1,5},{2,6},{3,7},{4,0},{5,1},{6,2},{7,3},{8,12},{9,13},{10,... | collective-permute-start | bytes 786440 | tf_op jit(solution)/shard_map/ppermute | solution.py:482
  161.9 17.3 %collective-permute-start.29 = (f32[256,256]{1,0:T(8,128)S(1)}, f32[256,256]{1,0:T(8,128)S(1)}, u32[]{:S(2)}, u32[]{:S(2)}) collective-permute-start(f32[256,256]{1,0:T(8,128)S(1)} %shard_map.86.refs_8_), channel_id=1, source_target_pairs={{0,8},{1,9},{2,10},{3,11},{4,12},{5,13},{6,14},{7,15},{8,0},{9,1},... | collective-permute-start | bytes 786440 | tf_op jit(solution)/shard_map/ppermute | solution.py:482
  162.9 16.3 %collective-permute-start.30 = (f32[256,256]{1,0:T(8,128)S(1)}, f32[256,256]{1,0:T(8,128)S(1)}, u32[]{:S(2)}, u32[]{:S(2)}) collective-permute-start(f32[256,256]{1,0:T(8,128)S(1)} %shard_map.83.refs_7_), channel_id=1, source_target_pairs={{0,16},{1,17},{2,18},{3,19},{4,20},{5,21},{6,22},{7,23},{8,24},{9,... | collective-permute-start | bytes 786440 | tf_op jit(solution)/shard_map/ppermute | solution.py:482
  164.0 20.1 %collective-permute-start.32 = (f32[256,256]{1,0:T(8,128)S(1)}, f32[256,256]{1,0:T(8,128)S(1)}, u32[]{:S(2)}, u32[]{:S(2)}) collective-permute-start(f32[256,256]{1,0:T(8,128)S(1)} %collective-permute-done.28.refs_7_), channel_id=1, source_target_pairs={{0,16},{1,17},{2,18},{3,19},{4,20},{5,21},{6,22},{7,23},{8,24},{9,... | collective-permute-start | bytes 786440 | tf_op jit(solution)/shard_map/ppermute | solution.py:482
  170.5 13.7 %collective-permute-start.33 = (f32[256,256]{1,0:T(8,128)S(1)}, f32[256,256]{1,0:T(8,128)S(1)}, u32[]{:S(2)}, u32[]{:S(2)}) collective-permute-start(f32[256,256]{1,0:T(8,128)S(1)} %collective-permute-done.31.refs_10_), channel_id=1, source_target_pairs={{0,8},{1,9},{2,10},{3,11},{4,12},{5,13},{6,14},{7,15},{8,0},{9,1},... | collective-permute-start | bytes 786440 | tf_op jit(solution)/shard_map/ppermute | solution.py:482
  187.8 8.3 %collective-permute-start.38 = (f32[1,512,256]{2,1,0:T(8,128)S(1)}, f32[1,512,256]{2,1,0:T(8,128)S(1)}, u32[]{:S(2)}, u32[]{:S(2)}) collective-permute-start(f32[1,512,256]{2,1,0:T(8,128)S(1)} %get-tuple-element.28), channel_id=1, source_target_pairs={{0,4},{1,5},{2,6},{3,7},{4,0},{5,1},{6,2},{7,3},{8,12},{9,13},{10,... | collective-permute-start | bytes 1572872 | tf_op jit(solution)/shard_map/ppermute | solution.py:482
  187.8 2.3 %collective-permute-start.34 = (f32[256,256]{1,0:T(8,128)S(1)}, f32[256,256]{1,0:T(8,128)S(1)}, u32[]{:S(2)}, u32[]{:S(2)}) collective-permute-start(f32[256,256]{1,0:T(8,128)S(1)} %collective-permute-done.28.refs_7_), channel_id=1, source_target_pairs={{0,4},{1,5},{2,6},{3,7},{4,0},{5,1},{6,2},{7,3},{8,12},{9,13},{10,... | collective-permute-start | bytes 786440 | tf_op jit(solution)/shard_map/ppermute | solution.py:482
  188.3 2.1 %collective-permute-start.35 = (f32[256,256]{1,0:T(8,128)S(1)}, f32[256,256]{1,0:T(8,128)S(1)}, u32[]{:S(2)}, u32[]{:S(2)}) collective-permute-start(f32[256,256]{1,0:T(8,128)S(1)} %collective-permute-done.29.refs_8_), channel_id=1, source_target_pairs={{0,4},{1,5},{2,6},{3,7},{4,0},{5,1},{6,2},{7,3},{8,12},{9,13},{10,... | collective-permute-start | bytes 786440 | tf_op jit(solution)/shard_map/ppermute | solution.py:482
  188.4 2.5 %collective-permute-start.36 = (f32[256,256]{1,0:T(8,128)S(1)}, f32[256,256]{1,0:T(8,128)S(1)}, u32[]{:S(2)}, u32[]{:S(2)}) collective-permute-start(f32[256,256]{1,0:T(8,128)S(1)} %collective-permute-done.30.refs_9_), channel_id=1, source_target_pairs={{0,4},{1,5},{2,6},{3,7},{4,0},{5,1},{6,2},{7,3},{8,12},{9,13},{10,... | collective-permute-start | bytes 786440 | tf_op jit(solution)/shard_map/ppermute | solution.py:482
  188.9 2.4 %collective-permute-start.37 = (f32[256,256]{1,0:T(8,128)S(1)}, f32[256,256]{1,0:T(8,128)S(1)}, u32[]{:S(2)}, u32[]{:S(2)}) collective-permute-start(f32[256,256]{1,0:T(8,128)S(1)} %collective-permute-done.31.refs_10_), channel_id=1, source_target_pairs={{0,4},{1,5},{2,6},{3,7},{4,0},{5,1},{6,2},{7,3},{8,12},{9,13},{10,... | collective-permute-start | bytes 786440 | tf_op jit(solution)/shard_map/ppermute | solution.py:482

commit v3 on v2

--- a/solution.py
+++ b/solution.py
@@ -216,49 +216,22 @@
     )(seed, *flat)
 
 
-def rows_of(tile_ref, rows, pieces):
-    if pieces == 1:
-        return tile_ref[0]
-    lanes = tile_ref.shape[2]
-    parts = tile_ref[0].reshape(rows // 8, pieces, 8, lanes)
-    parts = [parts[:, j] for j in range(pieces)]
-    at = lax.broadcasted_iota(jnp.int32, (rows // 8, 8, lanes), 1)
-    step = 1
-    while step < pieces:
-        upper = (at & step) != 0
-        for j in range(pieces):
-            if j & step == 0:
-                low, high = parts[j], parts[j + step]
-                parts[j] = jnp.where(upper, pltpu.roll(high, step, 1), low)
-                parts[j + step] = jnp.where(upper, high, pltpu.roll(low, 8 - step, 1))
-        step *= 2
-    return jnp.concatenate([part.reshape(rows, lanes) for part in parts], axis=1)
-
-
-def share_kernel(chunks, pieces, *refs):
-    terms, out_ref, held_ref, order_ref = refs[:-3], *refs[-3:]
+def share_kernel(chunks, *refs):
+    *terms, out_ref = refs
     each = len(terms) // chunks
     rows = terms[0].shape[1]
-    run = 8 // pieces
-    total = jnp.concatenate(
-        [sum(ref[0] for ref in terms[at : at + each]) for at in range(0, len(terms), each)], axis=0
-    )
-    for lane in range(0, total.shape[1], 128):
-        held_ref[...] = total[:, lane : lane + 128]
-        for place in range(8):
-            j, b = place // run, place % run
-            order_ref[pl.ds(place, chunks * rows // 8, stride=8), :] = held_ref[
-                pl.ds(b * pieces + j, chunks * rows // 8, stride=8), :
-            ]
-        out_ref[:, lane : lane + 128] = order_ref[...]
-
-
-def share_of(terms, pieces):
+    for chunk in range(chunks):
+        out_ref[chunk * rows : (chunk + 1) * rows] = sum(
+            ref[0] for ref in terms[chunk * each : (chunk + 1) * each]
+        )
+
+
+def share_of(terms):
     _, rows, count = terms[0][0].shape
     flat = [term for chunk in terms for term in chunk]
     shape = (len(terms) * rows, count)
     return call(
-        functools.partial(share_kernel, len(terms), pieces),
+        functools.partial(share_kernel, len(terms)),
         (1,),
         [pl.BlockSpec((1, rows, count), lambda i: (0, 0, 0)) for _ in flat],
         pl.BlockSpec(shape, lambda i: (0, 0)),
@@ -266,63 +239,72 @@
         0,
         4 * rows * count * (len(flat) + len(terms)),
         prefetch=0,
-        scratch=[pltpu.VMEM((shape[0], 128), F32)] * 2,
     )(*flat)
 
 
-def shared_kernel(group, strips, pieces, arrived, me_ref, *refs):
-    tiles, refs = refs[: group * strips], refs[group * strips :]
+def shared_kernel(bits, inner, base, col_bits, pieces, me_ref, *refs):
+    tiles, refs = refs[:pieces], refs[pieces:]
     seed_ref, *received, out_ref, parts_ref, seed_parts_ref = refs
     depth = seed_ref.shape[0]
+    group = 1 << len(inner)
     rows = parts_ref.shape[0] // group
-    strip = rows // strips
-
-    @pl.when(pl.program_id(0) == 0)
+    lanes = depth // pieces
+    step = pl.program_id(0)
+
+    @pl.when(step == 0)
     def _():
         high, low = split(seed_ref[...])
         seed_parts_ref[:depth] = high
         seed_parts_ref[depth : 2 * depth] = high
         seed_parts_ref[2 * depth :] = low
 
-    for at, ref in enumerate(tiles):
-        place = pl.ds(at * strip, strip)
-        high, low = split(rows_of(ref, strip, pieces))
-        parts_ref[place, :depth] = high
-        parts_ref[place, depth : 2 * depth] = low
-        parts_ref[place, 2 * depth :] = high
+    for piece, ref in enumerate(tiles):
+        high, low = split(ref.reshape(group * rows, lanes)[...])
+        at = piece * lanes
+        parts_ref[:, at : at + lanes] = high
+        parts_ref[:, depth + at : depth + at + lanes] = low
+        parts_ref[:, 2 * depth + at : 2 * depth + at + lanes] = high
     total = dot(parts_ref[...], seed_parts_ref[...])
+    outer_bits = [bit for bit in bits if bit not in inner]
     for g in range(group):
+        unit = spread(outer_bits, step) | (spread(inner, g) ^ (me_ref[0] & spread(inner, group - 1)))
+        place = place_of(bits, unit)
         term = total[g * rows : (g + 1) * rows]
-        out_ref[g] = term + received[0][g] if arrived else term
+        if received:
+            term = term + received[0][place]
+        out_ref[place] = term
 
 
 def shared_products(me, tiles, seed, bits, base, offset, rows, received=None, earlier=()):
     depth, count = seed.shape
-    lanes = tiles.shape[2]
+    lanes = min(depth, 128)
     pieces = depth // lanes
+    col_bits = tiles.ndim - 4
     units = 1 << len(bits)
-    group = min(units, 4)
-    strips = next(n for n in (4, 2, 1) if rows % (n * 16) == 0 or n == 1)
-
-    def place(g, strip, f, me_ref):
-        unit = (spread(bits, f * group + g) | base) ^ me_ref[0]
-        return unit, offset // rows * strips + strip, 0
-
+    inner = sorted([bit for bit in bits if bit < col_bits], reverse=True)
+    outer_bits = [bit for bit in bits if bit >= col_bits]
+    group = 1 << len(inner)
+
+    def place(piece, f, me_ref):
+        unit = (spread(outer_bits, f) | base) ^ me_ref[0]
+        cols = [0 if bit in inner else (unit >> bit) & 1 for bit in reversed(range(col_bits))]
+        return (unit >> col_bits, *cols, offset // rows, 0, piece)
+
+    block = [2 if bit in inner else 1 for bit in reversed(range(col_bits))]
     in_specs = [
-        pl.BlockSpec((1, rows // strips * pieces, lanes), functools.partial(place, g, strip))
-        for g in range(group)
-        for strip in range(strips)
+        pl.BlockSpec((1, *block, rows, 1, lanes), functools.partial(place, piece))
+        for piece in range(pieces)
     ] + [pl.BlockSpec((depth, count), lambda f, me_ref: (0, 0))]
-    operands = [tiles] * (group * strips) + [seed]
+    operands = [tiles] * pieces + [seed]
     if received is not None:
-        skip = received.shape[0] // group - units // group
-        in_specs.append(pl.BlockSpec((group, rows, count), lambda f, me_ref: (skip + f, 0, 0)))
+        half = received.shape[0] // units - 1
+        in_specs.append(pl.BlockSpec((units, rows, count), lambda f, me_ref: (half, 0, 0)))
         operands.append(received)
     return call(
-        functools.partial(shared_kernel, group, strips, pieces, received is not None),
+        functools.partial(shared_kernel, bits, inner, base, col_bits, pieces),
         (units // group,),
         in_specs,
-        pl.BlockSpec((group, rows, count), lambda f, me_ref: (f, 0, 0)),
+        pl.BlockSpec((units, rows, count), lambda f, me_ref: (0, 0, 0)),
         jax.ShapeDtypeStruct((units, rows, count), F32),
         6 * units * rows * depth * count,
         4 * units * rows * (depth + count),
@@ -332,9 +314,10 @@
     )(me, *operands)
 
 
-def coupled_kernel(units, halves, strips, aliased, last, me_ref, *refs):
+def coupled_kernel(counts, strips, aliased, packs, last, me_ref, *refs):
     coupling_refs, start_ref, refs = refs[:strips], refs[strips], refs[strips + 1 :]
-    pieces, refs = refs[: units * halves], refs[units * halves :]
+    units, given = len(counts), sum(counts)
+    pieces, refs = refs[:given], refs[given:]
     refs = refs[1:] if aliased else refs
     u = pl.program_id(0)
     if last:
@@ -352,25 +335,25 @@
             for at, (block, i, j) in enumerate(places)
         ]
     else:
-        second_ref, adjoint_ref, packed_ref = refs
+        second_ref, adjoint_ref = refs[:2]
 
     @pl.when(u == 0)
     def _():
         if last:
             for fetch in fetches:
                 fetch.start()
-        second_ref[...] = start_ref[...]
+        second_ref[...] = start_ref[...] if aliased else start_ref[...].T
 
     for g in range(units):
 
         @pl.when(u == g)
         def _():
-            block = jnp.concatenate(
-                [ref[...] for ref in pieces[g * halves : (g + 1) * halves]], axis=0
-            )
+            begin = sum(counts[:g])
+            block = [ref[...] for ref in pieces[begin : begin + counts[g]]]
+            block = block[0] if len(block) == 1 else jnp.concatenate(block, axis=0)
             adjoint_ref[...] = block
-            if not last:
-                packed_ref[0] = block
+            if packs:
+                refs[2][0] = block
             half = block.astype(BF16)
             for at, ref in enumerate(coupling_refs):
                 place = pl.ds(at * ref.shape[0], ref.shape[0])
@@ -392,9 +375,8 @@
                 out_ref[block, i * tile : (i + 1) * tile] = total
 
 
-def coupled_step(me, coupling, start, pieces, numbers, adjoint, inverse=None):
-    depth, count = start.shape
-    halves = len(pieces[0])
+def coupled_step(me, coupling, start, pieces, numbers, adjoint, packs=False, inverse=None):
+    depth, count = coupling.shape[0], pieces[0][0].shape[1]
     sub = sum(piece.shape[0] for piece in pieces[0])
     units = len(numbers)
 
@@ -412,7 +394,7 @@
             (strip, sub), functools.partial(lambda at, u, me_ref: (at, unit_of(u) ^ me_ref[0]), at)
         )
         for at in range(strips)
-    ] + [whole]
+    ] + [pl.BlockSpec(start.shape, lambda u, me_ref: (0, 0))]
     operands = [coupling] * strips + [start]
     for group in pieces:
         for piece in group:
@@ -428,12 +410,11 @@
     place = pl.BlockSpec((sub, count), lambda u, me_ref: (unit_of(u) ^ me_ref[0], 0))
     adjoint_shape = jax.ShapeDtypeStruct((coupling.shape[1], count), F32)
     if inverse is None:
-        out_specs = [whole, place, pl.BlockSpec((1, sub, count), lambda u, me_ref: (u, 0, 0))]
-        out_shape = [
-            jax.ShapeDtypeStruct((depth, count), F32),
-            adjoint_shape,
-            jax.ShapeDtypeStruct((units, sub, count), F32),
-        ]
+        out_specs = [whole, place]
+        out_shape = [jax.ShapeDtypeStruct((depth, count), F32), adjoint_shape]
+        if packs:
+            out_specs.append(pl.BlockSpec((1, sub, count), lambda u, me_ref: (u, 0, 0)))
+            out_shape.append(jax.ShapeDtypeStruct((units, sub, count), F32))
         scratch = ()
     else:
         blocks, width, _ = inverse.shape
@@ -451,7 +432,12 @@
         moved += 4 * inverse.size
     return call(
         functools.partial(
-            coupled_kernel, units, halves, strips, adjoint is not None, inverse is not None
+            coupled_kernel,
+            tuple(len(group) for group in pieces),
+            strips,
+            adjoint is not None,
+            packs,
+            inverse is not None,
         ),
         (units,),
         in_specs,
@@ -514,15 +500,13 @@
         ],
     )
 
-    lanes = min(depth, 128)
-    tiles = shared_inverse.reshape(devices, sub * depth // lanes, lanes)
+    tiles = shared_inverse.reshape(scen_count, *([2] * col_bits), sub, 1, depth)
     orders = [
         outer + col_order,
         outer[1:] + col_order + outer[:1],
         col_order[:1] + outer + col_order[1:],
         outer + col_order,
     ]
-    pieces = depth // lanes
     rows = sub // len(orders)
 
     def products(chunk, base, received=None, earlier=()):
@@ -542,27 +526,38 @@
 
     near = []
     for part, way in enumerate((outer, outer[::-1])):
-        held = {0: share_of(shares[2 * part : 2 * part + 2], pieces)}
+        held = {0: share_of(shares[2 * part : 2 * part + 2])}
         for bit in way:
             for number, piece in list(held.items()):
                 held[number | (1 << (bit - core))] = exchange(piece, bit)
         near.append(held)
-    second, adjoint = first.T, None
     inverse = private_inverse[0, 0]
     numbers = sorted(near[0])
     middle, last = numbers[1:-1], numbers[-1]
-
-    def take(numbers, pieces, inverse=None):
-        return coupled_step(me_scen, flat_coupling, second, pieces, numbers, adjoint, inverse)
-
     own = [held[0] for held in near]
-    second, adjoint, _ = take([0, 1], [own, [exchange(piece, core) for piece in own]])
+    across = [exchange(piece, core) for piece in own]
     far = [[exchange(held[number], core) for held in near] for number in middle]
-    second, adjoint, _ = take(middle, [[held[number] for held in near] for number in middle])
-    second, adjoint, packed = take([last], [[held[last] for held in near]])
-    far_last = exchange(packed, core)
-    second, adjoint, _ = take([number | 1 for number in middle], far)
-    second, adjoint = take([last | 1], [[far_last[0]]], inverse)
+    second, adjoint = coupled_step(
+        me_scen,
+        flat_coupling,
+        first,
+        [own, across] + [[held[number] for held in near] for number in middle],
+        [0, 1] + middle,
+        None,
+    )
+    second, adjoint, packed = coupled_step(
+        me_scen, flat_coupling, second, [[held[last] for held in near]], [last], adjoint, packs=True
+    )
+    packed = exchange(packed, core).reshape(sub, count)
+    second, adjoint = coupled_step(
+        me_scen,
+        flat_coupling,
+        second,
+        far + [[packed]],
+        [number | 1 for number in middle + [last]],
+        adjoint,
+        inverse=inverse,
+    )
     return second[None, None], adjoint[None]
 
 

time: 206 us -> 197 us (0.956)
  Pallas kernels: 98.9 us -> 86.5 us
  waiting for transfers between devices: 45.9 us -> 53.9 us
  local copies, waits for them, and re-layouts: 4.2 us -> 1.16 us
    pallas_call x24 -> x22, Pallas kernels: 98.9 us -> 86.5 us  [run(): pl.pallas_call(body, grid_spec=pltpu.PrefetchScalarGridSpec(num_scalar_pr...]
    ppermute x39, waiting for transfers between devices: 45.9 us -> 53.9 us  [exchange(): lax.ppermute(array, AXES, [(w, w ^ 1 << bit) for w in range(devices)])]
    pallas_call x1 -> x0, local copies, waits for them, and re-layouts: 3.06 us -> none  [run(): pl.pallas_call(body, grid_spec=pltpu.PrefetchScalarGridSpec(num_scalar_pr...]
  transfers between devices with their start and end apart: 39 -> 39, of which waited for: 16 -> 19; matrix products, arithmetic and copies ran while one was open for 9% -> 7% of each run, Pallas kernels for 36% -> 30%
where the time goes in v3:
time: 197 us; the launch traced here: 195 us
  Pallas kernels  86.5 us (44%)
  waiting for transfers between devices  53.9 us (27%)
  starting transfers between devices  38.7 us (20%)
  other arithmetic  14 us (7%)
    pallas_call x22, Pallas kernels, run(): pl.pallas_call(body, grid_spec=pltpu.PrefetchScalarGridSpec(num_scalar_pr...  86.5 us
    ppermute x39, waiting for transfers between devices, exchange(): lax.ppermute(array, AXES, [(w, w ^ 1 << bit) for w in range(devices)])  53.9 us
    ppermute x39, starting transfers between devices, exchange(): lax.ppermute(array, AXES, [(w, w ^ 1 << bit) for w in range(devices)])  38.7 us
    add x14, other arithmetic, halved(): away = sum((term[half:2 * half] for term in terms))  12.8 us
  transfers between devices with their start and end apart: 39, of which 19 were waited for; matrix products, arithmetic and copies ran while one was open for 7% of the time, Pallas kernels for 30%

profile of v3, /device:TPU:0, one launch (start us, length us, event | category | flops | bytes accessed | tf_op | source)
XLA Modules:
  0.0 195.3 jit_solution(3478404512088511056)
XLA Ops:
  0.6 4.3 %shard_map.68 = (f32[256,1536]{1,0:T(8,128)}, bf16[256,1536]{1,0:T(8,128)(2,1)}) custom-call(f32[2,768,256]{2,1,0:T(8,128)} %bitcast.104, f32[2,768,256]{2,1,0:T(8,128)} %bitcast.105, f32[2,768,256]{2,1,0:T(8,128)} %bitcast.106, f32[2,768,768]{2,1,0:T(8,128)} %bitcast.96, f32[2,768,768]{2,1,0:T(8,128)} %bitcast.97, f32[2,768,768]{2,1,0:T(8,128)} %bitcast.98, ...), custom_call_target="tpu_custom_call" | custom-call | flops 1811939328 | bytes 9437184 | tf_op jit(solution)/shard_map/pallas_call | solution.py:55
  5.0 1.1 copy-done.2
  6.1 3.7 %shard_map.70 = f32[4,256,256]{2,1,0:T(8,128)S(1)} custom-call(s32[1]{0:T(128)} %bitcast.me_ref, bf16[1536,4096]{1,0:T(8,128)(2,1)} %bitcast.60, bf16[1536,4096]{1,0:T(8,128)(2,1)} %bitcast.61, bf16[1536,4096]{1,0:T(8,128)(2,1)} %bitcast.62, bf16[1536,4096]{1,0:T(8,128)(2,1)} %bitcast.63, bf16[1536,4096]{1,0:T(8,128)(2,1)} %bitcast.64, ...), custom_call_target="tpu_custom_call" | custom-call | flops 805306368 | bytes 4194304 | tf_op jit(solution)/shard_map/pallas_call | solution.py:55
  10.4 3.7 %shard_map.71 = f32[4,256,256]{2,1,0:T(8,128)S(1)} custom-call(s32[1]{0:T(128)} %bitcast.me_ref, bf16[1536,4096]{1,0:T(8,128)(2,1)} %bitcast.66, bf16[1536,4096]{1,0:T(8,128)(2,1)} %bitcast.67, bf16[1536,4096]{1,0:T(8,128)(2,1)} %bitcast.68, bf16[1536,4096]{1,0:T(8,128)(2,1)} %bitcast.69, bf16[1536,4096]{1,0:T(8,128)(2,1)} %bitcast.70, ...), custom_call_target="tpu_custom_call" | custom-call | flops 805306368 | bytes 4194304 | tf_op jit(solution)/shard_map/pallas_call | solution.py:55
  14.3 5.5 %shard_map.69 = (f32[4,256,256]{2,1,0:T(8,128)S(1)}, f32[4,256,256]{2,1,0:T(8,128)}) custom-call(s32[1]{0:T(128)} %bitcast.me_ref, bf16[1536,4096]{1,0:T(8,128)(2,1)} %bitcast.77, bf16[1536,4096]{1,0:T(8,128)(2,1)} %bitcast.73, bf16[1536,4096]{1,0:T(8,128)(2,1)} %bitcast.74, bf16[1536,4096]{1,0:T(8,128)(2,1)} %bitcast.75, bf16[1536,4096]{1,0:T(8,128)(2,1)} %bitcast.76, ...), custom_call_target="tpu_custom_call" | custom-call | flops 1610612736 | bytes 8388608 | tf_op jit(solution)/shard_map/pallas_call | solution.py:55
  19.9 3.0 %collective-permute-start.1 = (f32[2,256,256]{2,1,0:T(8,128)S(1)}, f32[2,256,256]{2,1,0:T(8,128)S(1)}, u32[]{:S(2)}, u32[]{:S(2)}) collective-permute-start(f32[2,256,256]{2,1,0:T(8,128)S(1)} %slice_add_fusion.9), channel_id=1, source_target_pairs={{0,8},{1,9},{2,10},{3,11},{4,12},{5,13},{6,14},{7,15},{8,0},{9,1},... | collective-permute-start | bytes 1572872 | tf_op jit(solution)/shard_map/ppermute | solution.py:468
  22.8 1.1 slice_add_fusion.8
  24.0 1.6 collective-permute-start.4
  25.5 9.5 %collective-permute-done.1 = f32[2,256,256]{2,1,0:T(8,128)S(1)} collective-permute-done((f32[2,256,256]{2,1,0:T(8,128)S(1)}, f32[2,256,256]{2,1,0:T(8,128)S(1)}, u32[]{:S(2)}, u32[]{:S(2)}) %collective-permute-start.1) | collective-permute-done | bytes 524320 | tf_op jit(solution)/shard_map/ppermute | solution.py:468
  35.1 1.8 collective-permute-start.2
  36.9 1.0 collective-permute-done.4
  38.6 4.7 %collective-permute-done.2.refs_1_ = f32[1,256,256]{2,1,0:T(8,128)S(1)} collective-permute-done((f32[1,256,256]{2,1,0:T(8,128)S(1)}, f32[1,256,256]{2,1,0:T(8,128)S(1)}, u32[]{:S(2)}, u32[]{:S(2)}) %collective-permute-start.2) | collective-permute-done | bytes 262176 | tf_op jit(solution)/shard_map/ppermute | solution.py:468
  43.3 1.7 collective-permute-done.5.refs_3_
  45.2 4.5 %shard_map.73 = f32[16,128,256]{2,1,0:T(8,128)S(1)} custom-call(s32[1]{0:T(128)} %bitcast.4.me_ref.refs_0_, f32[8,2,2,512,1,512]{5,4,3,2,1,0:T(1,128)} %bitcast.12, f32[8,2,2,512,1,512]{5,4,3,2,1,0:T(1,128)} %bitcast.13, f32[8,2,2,512,1,512]{5,4,3,2,1,0:T(1,128)} %bitcast.14, f32[8,2,2,512,1,512]{5,4,3,2,1,0:T(1,128)} %bitcast.15, ...), custom_call_target="tpu_custom_call" | custom-call | flops 1610612736 | bytes 6291456 | tf_op jit(solution)/shard_map/pallas_call | solution.py:55
  49.8 4.5 %shard_map.75 = f32[16,128,256]{2,1,0:T(8,128)S(1)} custom-call(s32[1]{0:T(128)} %bitcast.4.me_ref.refs_0_, f32[8,2,2,512,1,512]{5,4,3,2,1,0:T(1,128)} %bitcast.16, f32[8,2,2,512,1,512]{5,4,3,2,1,0:T(1,128)} %bitcast.17, f32[8,2,2,512,1,512]{5,4,3,2,1,0:T(1,128)} %bitcast.18, f32[8,2,2,512,1,512]{5,4,3,2,1,0:T(1,128)} %bitcast.19, ...), custom_call_target="tpu_custom_call" | custom-call | flops 1610612736 | bytes 6291456 | tf_op jit(solution)/shard_map/pallas_call | solution.py:55
  54.9 4.5 %shard_map.77 = f32[16,128,256]{2,1,0:T(8,128)S(1)} custom-call(s32[1]{0:T(128)} %bitcast.4.me_ref.refs_0_, f32[8,2,2,512,1,512]{5,4,3,2,1,0:T(1,128)} %bitcast.20, f32[8,2,2,512,1,512]{5,4,3,2,1,0:T(1,128)} %bitcast.21, f32[8,2,2,512,1,512]{5,4,3,2,1,0:T(1,128)} %bitcast.22, f32[8,2,2,512,1,512]{5,4,3,2,1,0:T(1,128)} %bitcast.23, ...), custom_call_target="tpu_custom_call" | custom-call | flops 1610612736 | bytes 6291456 | tf_op jit(solution)/shard_map/pallas_call | solution.py:55
  59.5 4.5 %shard_map.79 = f32[16,128,256]{2,1,0:T(8,128)S(1)} custom-call(s32[1]{0:T(128)} %bitcast.4.me_ref.refs_0_, f32[8,2,2,512,1,512]{5,4,3,2,1,0:T(1,128)} %bitcast.24, f32[8,2,2,512,1,512]{5,4,3,2,1,0:T(1,128)} %bitcast.25, f32[8,2,2,512,1,512]{5,4,3,2,1,0:T(1,128)} %bitcast.26, f32[8,2,2,512,1,512]{5,4,3,2,1,0:T(1,128)} %bitcast.27, ...), custom_call_target="tpu_custom_call" | custom-call | flops 1610612736 | bytes 6291456 | tf_op jit(solution)/shard_map/pallas_call | solution.py:55
  64.5 3.5 %shard_map.74.refs_6_ = f32[8,128,256]{2,1,0:T(8,128)} custom-call(s32[1]{0:T(128)} %bitcast.4.me_ref.refs_0_, f32[8,2,2,512,1,512]{5,4,3,2,1,0:T(1,128)} %bitcast.28, f32[8,2,2,512,1,512]{5,4,3,2,1,0:T(1,128)} %bitcast.29, f32[8,2,2,512,1,512]{5,4,3,2,1,0:T(1,128)} %bitcast.30, f32[8,2,2,512,1,512]{5,4,3,2,1,0:T(1,128)} %bitcast.31, ...), custom_call_target="tpu_custom_call" | custom-call | flops 805306368 | bytes 3145728 | tf_op jit(solution)/shard_map/pallas_call | solution.py:55
  68.8 3.5 %shard_map.76.refs_7_ = f32[8,128,256]{2,1,0:T(8,128)} custom-call(s32[1]{0:T(128)} %bitcast.4.me_ref.refs_0_, f32[8,2,2,512,1,512]{5,4,3,2,1,0:T(1,128)} %bitcast.35, f32[8,2,2,512,1,512]{5,4,3,2,1,0:T(1,128)} %bitcast.33, f32[8,2,2,512,1,512]{5,4,3,2,1,0:T(1,128)} %bitcast.34, f32[8,2,2,512,1,512]{5,4,3,2,1,0:T(1,128)} %bitcast.32, ...), custom_call_target="tpu_custom_call" | custom-call | flops 805306368 | bytes 3145728 | tf_op jit(solution)/shard_map/pallas_call | solution.py:55
  72.4 1.2 collective-permute-start.14
  73.6 5.2 %shard_map.78.refs_8_ = f32[8,128,256]{2,1,0:T(8,128)} custom-call(s32[1]{0:T(128)} %bitcast.4.me_ref.refs_0_, f32[8,2,2,512,1,512]{5,4,3,2,1,0:T(1,128)} %bitcast.36, f32[8,2,2,512,1,512]{5,4,3,2,1,0:T(1,128)} %bitcast.37, f32[8,2,2,512,1,512]{5,4,3,2,1,0:T(1,128)} %bitcast.38, f32[8,2,2,512,1,512]{5,4,3,2,1,0:T(1,128)} %bitcast.39, ...), custom_call_target="tpu_custom_call" | custom-call | flops 805306368 | bytes 3145728 | tf_op jit(solution)/shard_map/pallas_call | solution.py:55
  78.8 1.6 collective-permute-start.18
  80.4 3.6 %shard_map.80.refs_9_ = f32[8,128,256]{2,1,0:T(8,128)} custom-call(s32[1]{0:T(128)} %bitcast.4.me_ref.refs_0_, f32[8,2,2,512,1,512]{5,4,3,2,1,0:T(1,128)} %bitcast.40, f32[8,2,2,512,1,512]{5,4,3,2,1,0:T(1,128)} %bitcast.41, f32[8,2,2,512,1,512]{5,4,3,2,1,0:T(1,128)} %bitcast.42, f32[8,2,2,512,1,512]{5,4,3,2,1,0:T(1,128)} %bitcast.43, ...), custom_call_target="tpu_custom_call" | custom-call | flops 805306368 | bytes 3145728 | tf_op jit(solution)/shard_map/pallas_call | solution.py:55
  84.0 1.5 collective-permute-start.22
  85.5 2.6 %shard_map.81.refs_0_ = f32[8,128,256]{2,1,0:T(8,128)S(1)} custom-call(s32[1]{0:T(128)} %bitcast.4.me_ref.refs_0_, f32[8,2,2,512,1,512]{5,4,3,2,1,0:T(1,128)} %bitcast.46, f32[8,2,2,512,1,512]{5,4,3,2,1,0:T(1,128)} %bitcast.45, f32[8,2,2,512,1,512]{5,4,3,2,1,0:T(1,128)} %bitcast.44, f32[8,2,2,512,1,512]{5,4,3,2,1,0:T(1,128)} %bitcast.47, ...), custom_call_target="tpu_custom_call" | custom-call | flops 805306368 | bytes 3145728 | tf_op jit(solution)/shard_map/pallas_call | solution.py:55
  88.1 2.6 %shard_map.82.refs_6_ = f32[8,128,256]{2,1,0:T(8,128)S(1)} custom-call(s32[1]{0:T(128)} %bitcast.4.me_ref.refs_0_, f32[8,2,2,512,1,512]{5,4,3,2,1,0:T(1,128)} %bitcast.48, f32[8,2,2,512,1,512]{5,4,3,2,1,0:T(1,128)} %bitcast.49, f32[8,2,2,512,1,512]{5,4,3,2,1,0:T(1,128)} %bitcast.50, f32[8,2,2,512,1,512]{5,4,3,2,1,0:T(1,128)} %bitcast.51, ...), custom_call_target="tpu_custom_call" | custom-call | flops 805306368 | bytes 3145728 | tf_op jit(solution)/shard_map/pallas_call | solution.py:55
  90.7 3.7 %shard_map.84.refs_0_ = f32[8,128,256]{2,1,0:T(8,128)S(1)} custom-call(s32[1]{0:T(128)} %bitcast.4.me_ref.refs_0_, f32[8,2,2,512,1,512]{5,4,3,2,1,0:T(1,128)} %bitcast.52, f32[8,2,2,512,1,512]{5,4,3,2,1,0:T(1,128)} %bitcast.53, f32[8,2,2,512,1,512]{5,4,3,2,1,0:T(1,128)} %bitcast.54, f32[8,2,2,512,1,512]{5,4,3,2,1,0:T(1,128)} %bitcast.55, ...), custom_call_target="tpu_custom_call" | custom-call | flops 805306368 | bytes 3145728 | tf_op jit(solution)/shard_map/pallas_call | solution.py:55
  94.4 2.8 %shard_map.85.refs_6_ = f32[8,128,256]{2,1,0:T(8,128)S(1)} custom-call(s32[1]{0:T(128)} %bitcast.4.me_ref.refs_0_, f32[8,2,2,512,1,512]{5,4,3,2,1,0:T(1,128)} %bitcast.56, f32[8,2,2,512,1,512]{5,4,3,2,1,0:T(1,128)} %bitcast.57, f32[8,2,2,512,1,512]{5,4,3,2,1,0:T(1,128)} %bitcast.58, f32[8,2,2,512,1,512]{5,4,3,2,1,0:T(1,128)} %bitcast.59, ...), custom_call_target="tpu_custom_call" | custom-call | flops 805306368 | bytes 3145728 | tf_op jit(solution)/shard_map/pallas_call | solution.py:55
  97.2 1.3 slice_add_fusion.6
  99.0 1.1 slice_add_fusion.4
  100.7 4.5 %collective-permute-done.18.refs_2_ = f32[8,128,256]{2,1,0:T(8,128)} collective-permute-done((f32[8,128,256]{2,1,0:T(8,128)}, f32[8,128,256]{2,1,0:T(8,128)}, u32[]{:S(2)}, u32[]{:S(2)}) %collective-permute-start.18) | collective-permute-done | bytes 1048608 | tf_op jit(solution)/shard_map/ppermute | solution.py:468
  105.2 1.1 slice_add_fusion.2
  106.4 1.6 collective-permute-start.19
  107.9 8.9 %collective-permute-done.22.refs_8_ = f32[8,128,256]{2,1,0:T(8,128)} collective-permute-done((f32[8,128,256]{2,1,0:T(8,128)}, f32[8,128,256]{2,1,0:T(8,128)}, u32[]{:S(2)}, u32[]{:S(2)}) %collective-permute-start.22) | collective-permute-done | bytes 1048608 | tf_op jit(solution)/shard_map/ppermute | solution.py:468
  116.8 1.1 slice_add_fusion
  118.0 1.6 collective-permute-start.23
  119.6 1.0 slice_add_fusion.19
  120.6 1.7 collective-permute-start.12
  122.2 1.0 slice_add_fusion.16
  123.3 2.6 %collective-permute-start.16 = (f32[2,128,256]{2,1,0:T(8,128)S(1)}, f32[2,128,256]{2,1,0:T(8,128)S(1)}, u32[]{:S(2)}, u32[]{:S(2)}) collective-permute-start(f32[2,128,256]{2,1,0:T(8,128)S(1)} %slice_add_fusion.16), channel_id=1, source_target_pairs={{0,2},{1,3},{2,0},{3,1},{4,6},{5,7},{6,4},{7,5},{8,10},{9,11},{10,... | collective-permute-start | bytes 786440 | tf_op jit(solution)/shard_map/ppermute | solution.py:468
  125.9 1.2 collective-permute-done.19.refs_3_
  127.1 1.0 slice_add_fusion.13
  128.1 1.6 collective-permute-start.20
  130.4 1.0 slice_add_fusion.10
  131.4 1.6 collective-permute-start.24
  133.1 1.0 slice_add_fusion.42
  134.0 2.7 %collective-permute-start.13 = (f32[1,128,256]{2,1,0:T(8,128)S(1)}, f32[1,128,256]{2,1,0:T(8,128)S(1)}, u32[]{:S(2)}, u32[]{:S(2)}) collective-permute-start(f32[1,128,256]{2,1,0:T(8,128)S(1)} %slice_add_fusion.42), channel_id=1, source_target_pairs={{0,2},{1,3},{2,0},{3,1},{4,6},{5,7},{6,4},{7,5},{8,10},{9,11},{10,... | collective-permute-start | bytes 393224 | tf_op jit(solution)/shard_map/ppermute | solution.py:468
  136.7 1.0 slice_add_fusion.38
  137.6 0.9 collective-permute-start.17
  138.5 0.9 slice_add_fusion.34
  139.9 2.6 %collective-permute-done.13.refs_5_ = f32[1,128,256]{2,1,0:T(8,128)S(1)} collective-permute-done((f32[1,128,256]{2,1,0:T(8,128)S(1)}, f32[1,128,256]{2,1,0:T(8,128)S(1)}, u32[]{:S(2)}, u32[]{:S(2)}) %collective-permute-start.13) | collective-permute-done | bytes 131104 | tf_op jit(solution)/shard_map/ppermute | solution.py:468
  142.7 1.0 shard_map.83.refs_7_
  143.8 1.0 slice_add_fusion.30
  144.7 2.5 %collective-permute-start.25 = (f32[1,128,256]{2,1,0:T(8,128)S(1)}, f32[1,128,256]{2,1,0:T(8,128)S(1)}, u32[]{:S(2)}, u32[]{:S(2)}) collective-permute-start(f32[1,128,256]{2,1,0:T(8,128)S(1)} %slice_add_fusion.30), channel_id=1, source_target_pairs={{0,2},{1,3},{2,0},{3,1},{4,6},{5,7},{6,4},{7,5},{8,10},{9,11},{10,... | collective-permute-start | bytes 393224 | tf_op jit(solution)/shard_map/ppermute | solution.py:468
  147.9 6.5 %collective-permute-done.25.refs_11_ = f32[1,128,256]{2,1,0:T(8,128)S(1)} collective-permute-done((f32[1,128,256]{2,1,0:T(8,128)S(1)}, f32[1,128,256]{2,1,0:T(8,128)S(1)}, u32[]{:S(2)}, u32[]{:S(2)}) %collective-permute-start.25) | collective-permute-done | bytes 131104 | tf_op jit(solution)/shard_map/ppermute | solution.py:468
  154.4 1.1 shard_map.86.refs_8_
  155.5 1.6 collective-permute-start.31
  158.4 1.2 collective-permute-start.32
  159.6 5.1 %collective-permute-done.31.refs_14_ = f32[256,256]{1,0:T(8,128)S(1)} collective-permute-done((f32[256,256]{1,0:T(8,128)S(1)}, f32[256,256]{1,0:T(8,128)S(1)}, u32[]{:S(2)}, u32[]{:S(2)}) %collective-permute-start.31) | collective-permute-done | bytes 262176 | tf_op jit(solution)/shard_map/ppermute | solution.py:468
  166.1 4.2 %collective-permute-done.30.refs_13_ = f32[256,256]{1,0:T(8,128)S(1)} collective-permute-done((f32[256,256]{1,0:T(8,128)S(1)}, f32[256,256]{1,0:T(8,128)S(1)}, u32[]{:S(2)}, u32[]{:S(2)}) %collective-permute-start.30) | collective-permute-done | bytes 262176 | tf_op jit(solution)/shard_map/ppermute | solution.py:468
  170.4 7.0 %shard_map.87 = (f32[1536,256]{1,0:T(8,128)}, f32[4096,256]{1,0:T(8,128)}) custom-call(s32[1]{0:T(128)} %bitcast.me_ref, bf16[1536,4096]{1,0:T(8,128)(2,1)} %bitcast.78, bf16[1536,4096]{1,0:T(8,128)(2,1)} %bitcast.79, bf16[1536,4096]{1,0:T(8,128)(2,1)} %bitcast.80, bf16[1536,4096]{1,0:T(8,128)(2,1)} %bitcast.81, bf16[1536,4096]{1,0:T(8,128)(2,1)} %bitcast.82, ...), custom_call_target="tpu_custom_call" | custom-call | flops 1610612736 | bytes 13631488 | tf_op jit(solution)/shard_map/pallas_call | solution.py:55
  177.4 3.7 %shard_map.88 = (f32[1536,256]{1,0:T(8,128)}, f32[4096,256]{1,0:T(8,128)}, f32[1,512,256]{2,1,0:T(8,128)S(1)}) custom-call(s32[1]{0:T(128)} %bitcast.me_ref, bf16[1536,4096]{1,0:T(8,128)(2,1)} %bitcast.84, bf16[1536,4096]{1,0:T(8,128)(2,1)} %bitcast.85, bf16[1536,4096]{1,0:T(8,128)(2,1)} %bitcast.86, ...), custom_call_target="tpu_custom_call", output_to_operand_aliasing={{1}: (10, {})} | custom-call | flops 402653184 | bytes 5767168 | tf_op jit(solution)/shard_map/pallas_call | solution.py:55
  182.1 1.3 collective-permute-done.34.refs_7_
  184.5 10.6 %shard_map.89 = (f32[2,768,256]{2,1,0:T(8,128)}, f32[4096,256]{1,0:T(8,128)}) custom-call(s32[1]{0:T(128)} %bitcast.me_ref, bf16[1536,4096]{1,0:T(8,128)(2,1)} %bitcast.90, bf16[1536,4096]{1,0:T(8,128)(2,1)} %bitcast.91, bf16[1536,4096]{1,0:T(8,128)(2,1)} %bitcast.92, bf16[1536,4096]{1,0:T(8,128)(2,1)} %bitcast.93, ...), custom_call_target="tpu_custom_call", output_to_operand_aliasing={{1}: (13, {})} | custom-call | flops 3019898880 | bytes 15728640 | tf_op jit(solution)/shard_map/pallas_call | solution.py:55
  (66 shorter events, 12.0 us)
Async XLA Ops:
  5.0 1.1 copy-start.2
  9.9 9.9 %collective-permute-start = (f32[4,256,256]{2,1,0:T(8,128)S(1)}, f32[4,256,256]{2,1,0:T(8,128)S(1)}, u32[]{:S(2)}, u32[]{:S(2)}) collective-permute-start(f32[4,256,256]{2,1,0:T(8,128)S(1)} %shard_map.70), channel_id=1, source_target_pairs={{0,4},{1,5},{2,6},{3,7},{4,0},{5,1},{6,2},{7,3},{8,12},{9,13},{10,... | collective-permute-start | bytes 3145736 | tf_op jit(solution)/shard_map/ppermute | solution.py:468
  14.2 8.7 %collective-permute-start.3 = (f32[4,256,256]{2,1,0:T(8,128)S(1)}, f32[4,256,256]{2,1,0:T(8,128)S(1)}, u32[]{:S(2)}, u32[]{:S(2)}) collective-permute-start(f32[4,256,256]{2,1,0:T(8,128)S(1)} %shard_map.71), channel_id=1, source_target_pairs={{0,4},{1,5},{2,6},{3,7},{4,0},{5,1},{6,2},{7,3},{8,12},{9,13},{10,... | collective-permute-start | bytes 3145736 | tf_op jit(solution)/shard_map/ppermute | solution.py:468
  19.8 18.1 %copy-start.4 = (f32[4,256,256]{2,1,0:T(8,128)S(1)}, f32[4,256,256]{2,1,0:T(8,128)}, u32[]{:S(2)}) copy-start(f32[4,256,256]{2,1,0:T(8,128)} %get-tuple-element.16) | copy-start | bytes 3145732
  19.9 15.2 %collective-permute-start.1 = (f32[2,256,256]{2,1,0:T(8,128)S(1)}, f32[2,256,256]{2,1,0:T(8,128)S(1)}, u32[]{:S(2)}, u32[]{:S(2)}) collective-permute-start(f32[2,256,256]{2,1,0:T(8,128)S(1)} %slice_add_fusion.9), channel_id=1, source_target_pairs={{0,8},{1,9},{2,10},{3,11},{4,12},{5,13},{6,14},{7,15},{8,0},{9,1},... | collective-permute-start | bytes 1572872 | tf_op jit(solution)/shard_map/ppermute | solution.py:468
  23.9 21.0 %copy-start.3 = (f32[1,512,256]{2,1,0:T(8,128)S(1)}, f32[1,512,256]{2,1,0:T(8,128)}, u32[]{:S(2)}) copy-start(f32[1,512,256]{2,1,0:T(8,128)} %param.8) | copy-start | bytes 1572868
  24.0 14.0 %collective-permute-start.4 = (f32[2,256,256]{2,1,0:T(8,128)S(1)}, f32[2,256,256]{2,1,0:T(8,128)S(1)}, u32[]{:S(2)}, u32[]{:S(2)}) collective-permute-start(f32[2,256,256]{2,1,0:T(8,128)S(1)} %slice_add_fusion.8), channel_id=1, source_target_pairs={{0,16},{1,17},{2,18},{3,19},{4,20},{5,21},{6,22},{7,23},{8,24},{9,... | collective-permute-start | bytes 1572872 | tf_op jit(solution)/shard_map/ppermute | solution.py:468
  35.1 8.2 %collective-permute-start.2 = (f32[1,256,256]{2,1,0:T(8,128)S(1)}, f32[1,256,256]{2,1,0:T(8,128)S(1)}, u32[]{:S(2)}, u32[]{:S(2)}) collective-permute-start(f32[1,256,256]{2,1,0:T(8,128)S(1)} %get-tuple-element.26), channel_id=1, source_target_pairs={{0,16},{1,17},{2,18},{3,19},{4,20},{5,21},{6,22},{7,23},{8,24},{9,... | collective-permute-start | bytes 786440 | tf_op jit(solution)/shard_map/ppermute | solution.py:468
  38.0 7.0 %collective-permute-start.5 = (f32[1,256,256]{2,1,0:T(8,128)S(1)}, f32[1,256,256]{2,1,0:T(8,128)S(1)}, u32[]{:S(2)}, u32[]{:S(2)}) collective-permute-start(f32[1,256,256]{2,1,0:T(8,128)S(1)} %get-tuple-element.24), channel_id=1, source_target_pairs={{0,8},{1,9},{2,10},{3,11},{4,12},{5,13},{6,14},{7,15},{8,0},{9,1},... | collective-permute-start | bytes 786440 | tf_op jit(solution)/shard_map/ppermute | solution.py:468
  49.7 14.8 %collective-permute-start.6 = (f32[16,128,256]{2,1,0:T(8,128)S(1)}, f32[16,128,256]{2,1,0:T(8,128)S(1)}, u32[]{:S(2)}, u32[]{:S(2)}) collective-permute-start(f32[16,128,256]{2,1,0:T(8,128)S(1)} %shard_map.73), channel_id=1, source_target_pairs={{0,4},{1,5},{2,6},{3,7},{4,0},{5,1},{6,2},{7,3},{8,12},{9,13},{10,... | collective-permute-start | bytes 6291464 | tf_op jit(solution)/shard_map/ppermute | solution.py:468
  54.4 14.5 %collective-permute-start.7 = (f32[16,128,256]{2,1,0:T(8,128)S(1)}, f32[16,128,256]{2,1,0:T(8,128)S(1)}, u32[]{:S(2)}, u32[]{:S(2)}) collective-permute-start(f32[16,128,256]{2,1,0:T(8,128)S(1)} %shard_map.75), channel_id=1, source_target_pairs={{0,4},{1,5},{2,6},{3,7},{4,0},{5,1},{6,2},{7,3},{8,12},{9,13},{10,... | collective-permute-start | bytes 6291464 | tf_op jit(solution)/shard_map/ppermute | solution.py:468
  59.4 14.2 %collective-permute-start.8 = (f32[16,128,256]{2,1,0:T(8,128)S(1)}, f32[16,128,256]{2,1,0:T(8,128)S(1)}, u32[]{:S(2)}, u32[]{:S(2)}) collective-permute-start(f32[16,128,256]{2,1,0:T(8,128)S(1)} %shard_map.77), channel_id=1, source_target_pairs={{0,4},{1,5},{2,6},{3,7},{4,0},{5,1},{6,2},{7,3},{8,12},{9,13},{10,... | collective-permute-start | bytes 6291464 | tf_op jit(solution)/shard_map/ppermute | solution.py:468
  64.0 16.4 %collective-permute-start.9 = (f32[16,128,256]{2,1,0:T(8,128)S(1)}, f32[16,128,256]{2,1,0:T(8,128)S(1)}, u32[]{:S(2)}, u32[]{:S(2)}) collective-permute-start(f32[16,128,256]{2,1,0:T(8,128)S(1)} %shard_map.79), channel_id=1, source_target_pairs={{0,4},{1,5},{2,6},{3,7},{4,0},{5,1},{6,2},{7,3},{8,12},{9,13},{10,... | collective-permute-start | bytes 6291464 | tf_op jit(solution)/shard_map/ppermute | solution.py:468
  68.0 29.1 %collective-permute-start.10 = (f32[8,128,256]{2,1,0:T(8,128)}, f32[8,128,256]{2,1,0:T(8,128)}, u32[]{:S(2)}, u32[]{:S(2)}) collective-permute-start(f32[8,128,256]{2,1,0:T(8,128)} %shard_map.74.refs_6_), channel_id=1, source_target_pairs={{0,8},{1,9},{2,10},{3,11},{4,12},{5,13},{6,14},{7,15},{8,0},{9,1},... | collective-permute-start | bytes 3145736 | tf_op jit(solution)/shard_map/ppermute | solution.py:468
  72.4 26.7 %collective-permute-start.14 = (f32[8,128,256]{2,1,0:T(8,128)}, f32[8,128,256]{2,1,0:T(8,128)}, u32[]{:S(2)}, u32[]{:S(2)}) collective-permute-start(f32[8,128,256]{2,1,0:T(8,128)} %shard_map.76.refs_7_), channel_id=1, source_target_pairs={{0,16},{1,17},{2,18},{3,19},{4,20},{5,21},{6,22},{7,23},{8,24},{9,... | collective-permute-start | bytes 3145736 | tf_op jit(solution)/shard_map/ppermute | solution.py:468
  73.6 5.2 %copy-start = (f32[16,128,256]{2,1,0:T(8,128)}, f32[16,128,256]{2,1,0:T(8,128)S(1)}, u32[]{:S(2)}) copy-start(f32[16,128,256]{2,1,0:T(8,128)S(1)} %collective-permute-done.8.refs_5_.refs_1_) | copy-start | bytes 6291460
  78.8 26.4 %collective-permute-start.18 = (f32[8,128,256]{2,1,0:T(8,128)}, f32[8,128,256]{2,1,0:T(8,128)}, u32[]{:S(2)}, u32[]{:S(2)}) collective-permute-start(f32[8,128,256]{2,1,0:T(8,128)} %shard_map.78.refs_8_), channel_id=1, source_target_pairs={{0,1},{1,0},{2,3},{3,2},{4,5},{5,4},{6,7},{7,6},{8,9},{9,8},{10,11... | collective-permute-start | bytes 3145736 | tf_op jit(solution)/shard_map/ppermute | solution.py:468
  84.0 32.8 %collective-permute-start.22 = (f32[8,128,256]{2,1,0:T(8,128)}, f32[8,128,256]{2,1,0:T(8,128)}, u32[]{:S(2)}, u32[]{:S(2)}) collective-permute-start(f32[8,128,256]{2,1,0:T(8,128)} %shard_map.80.refs_9_), channel_id=1, source_target_pairs={{0,8},{1,9},{2,10},{3,11},{4,12},{5,13},{6,14},{7,15},{8,0},{9,1},... | collective-permute-start | bytes 3145736 | tf_op jit(solution)/shard_map/ppermute | solution.py:468
  97.1 8.1 %copy-start.1 = (f32[16,128,256]{2,1,0:T(8,128)S(1)}, f32[16,128,256]{2,1,0:T(8,128)}, u32[]{:S(2)}) copy-start(f32[16,128,256]{2,1,0:T(8,128)} %copy-done) | copy-start | bytes 6291460
  98.5 21.1 %collective-permute-start.11 = (f32[4,128,256]{2,1,0:T(8,128)S(1)}, f32[4,128,256]{2,1,0:T(8,128)S(1)}, u32[]{:S(2)}, u32[]{:S(2)}) collective-permute-start(f32[4,128,256]{2,1,0:T(8,128)S(1)} %slice_add_fusion.6), channel_id=1, source_target_pairs={{0,16},{1,17},{2,18},{3,19},{4,20},{5,21},{6,22},{7,23},{8,24},{9,... | collective-permute-start | bytes 1572872 | tf_op jit(solution)/shard_map/ppermute | solution.py:468
  100.2 22.0 %collective-permute-start.15 = (f32[4,128,256]{2,1,0:T(8,128)S(1)}, f32[4,128,256]{2,1,0:T(8,128)S(1)}, u32[]{:S(2)}, u32[]{:S(2)}) collective-permute-start(f32[4,128,256]{2,1,0:T(8,128)S(1)} %slice_add_fusion.4), channel_id=1, source_target_pairs={{0,1},{1,0},{2,3},{3,2},{4,5},{5,4},{6,7},{7,6},{8,9},{9,8},{10,11... | collective-permute-start | bytes 1572872 | tf_op jit(solution)/shard_map/ppermute | solution.py:468
  106.4 20.7 %collective-permute-start.19 = (f32[4,128,256]{2,1,0:T(8,128)S(1)}, f32[4,128,256]{2,1,0:T(8,128)S(1)}, u32[]{:S(2)}, u32[]{:S(2)}) collective-permute-start(f32[4,128,256]{2,1,0:T(8,128)S(1)} %slice_add_fusion.2), channel_id=1, source_target_pairs={{0,8},{1,9},{2,10},{3,11},{4,12},{5,13},{6,14},{7,15},{8,0},{9,1},... | collective-permute-start | bytes 1572872 | tf_op jit(solution)/shard_map/ppermute | solution.py:468
  118.0 12.4 %collective-permute-start.23 = (f32[4,128,256]{2,1,0:T(8,128)S(1)}, f32[4,128,256]{2,1,0:T(8,128)S(1)}, u32[]{:S(2)}, u32[]{:S(2)}) collective-permute-start(f32[4,128,256]{2,1,0:T(8,128)S(1)} %slice_add_fusion), channel_id=1, source_target_pairs={{0,16},{1,17},{2,18},{3,19},{4,20},{5,21},{6,22},{7,23},{8,24},{9,... | collective-permute-start | bytes 1572872 | tf_op jit(solution)/shard_map/ppermute | solution.py:468
  120.6 12.5 %collective-permute-start.12 = (f32[2,128,256]{2,1,0:T(8,128)S(1)}, f32[2,128,256]{2,1,0:T(8,128)S(1)}, u32[]{:S(2)}, u32[]{:S(2)}) collective-permute-start(f32[2,128,256]{2,1,0:T(8,128)S(1)} %slice_add_fusion.19), channel_id=1, source_target_pairs={{0,1},{1,0},{2,3},{3,2},{4,5},{5,4},{6,7},{7,6},{8,9},{9,8},{10,11... | collective-permute-start | bytes 786440 | tf_op jit(solution)/shard_map/ppermute | solution.py:468
  123.3 13.4 %collective-permute-start.16 = (f32[2,128,256]{2,1,0:T(8,128)S(1)}, f32[2,128,256]{2,1,0:T(8,128)S(1)}, u32[]{:S(2)}, u32[]{:S(2)}) collective-permute-start(f32[2,128,256]{2,1,0:T(8,128)S(1)} %slice_add_fusion.16), channel_id=1, source_target_pairs={{0,2},{1,3},{2,0},{3,1},{4,6},{5,7},{6,4},{7,5},{8,10},{9,11},{10,... | collective-permute-start | bytes 786440 | tf_op jit(solution)/shard_map/ppermute | solution.py:468
  128.1 10.4 %collective-permute-start.20 = (f32[2,128,256]{2,1,0:T(8,128)S(1)}, f32[2,128,256]{2,1,0:T(8,128)S(1)}, u32[]{:S(2)}, u32[]{:S(2)}) collective-permute-start(f32[2,128,256]{2,1,0:T(8,128)S(1)} %slice_add_fusion.13), channel_id=1, source_target_pairs={{0,16},{1,17},{2,18},{3,19},{4,20},{5,21},{6,22},{7,23},{8,24},{9,... | collective-permute-start | bytes 786440 | tf_op jit(solution)/shard_map/ppermute | solution.py:468
  131.4 12.4 %collective-permute-start.24 = (f32[2,128,256]{2,1,0:T(8,128)S(1)}, f32[2,128,256]{2,1,0:T(8,128)S(1)}, u32[]{:S(2)}, u32[]{:S(2)}) collective-permute-start(f32[2,128,256]{2,1,0:T(8,128)S(1)} %slice_add_fusion.10), channel_id=1, source_target_pairs={{0,1},{1,0},{2,3},{3,2},{4,5},{5,4},{6,7},{7,6},{8,9},{9,8},{10,11... | collective-permute-start | bytes 786440 | tf_op jit(solution)/shard_map/ppermute | solution.py:468
  134.0 8.4 %collective-permute-start.13 = (f32[1,128,256]{2,1,0:T(8,128)S(1)}, f32[1,128,256]{2,1,0:T(8,128)S(1)}, u32[]{:S(2)}, u32[]{:S(2)}) collective-permute-start(f32[1,128,256]{2,1,0:T(8,128)S(1)} %slice_add_fusion.42), channel_id=1, source_target_pairs={{0,2},{1,3},{2,0},{3,1},{4,6},{5,7},{6,4},{7,5},{8,10},{9,11},{10,... | collective-permute-start | bytes 393224 | tf_op jit(solution)/shard_map/ppermute | solution.py:468
  137.6 5.0 %collective-permute-start.17 = (f32[1,128,256]{2,1,0:T(8,128)S(1)}, f32[1,128,256]{2,1,0:T(8,128)S(1)}, u32[]{:S(2)}, u32[]{:S(2)}) collective-permute-start(f32[1,128,256]{2,1,0:T(8,128)S(1)} %slice_add_fusion.38), channel_id=1, source_target_pairs={{0,8},{1,9},{2,10},{3,11},{4,12},{5,13},{6,14},{7,15},{8,0},{9,1},... | collective-permute-start | bytes 393224 | tf_op jit(solution)/shard_map/ppermute | solution.py:468
  139.5 8.5 %collective-permute-start.21 = (f32[1,128,256]{2,1,0:T(8,128)S(1)}, f32[1,128,256]{2,1,0:T(8,128)S(1)}, u32[]{:S(2)}, u32[]{:S(2)}) collective-permute-start(f32[1,128,256]{2,1,0:T(8,128)S(1)} %slice_add_fusion.34), channel_id=1, source_target_pairs={{0,2},{1,3},{2,0},{3,1},{4,6},{5,7},{6,4},{7,5},{8,10},{9,11},{10,... | collective-permute-start | bytes 393224 | tf_op jit(solution)/shard_map/ppermute | solution.py:468
  143.7 13.9 %collective-permute-start.26 = (f32[256,256]{1,0:T(8,128)S(1)}, f32[256,256]{1,0:T(8,128)S(1)}, u32[]{:S(2)}, u32[]{:S(2)}) collective-permute-start(f32[256,256]{1,0:T(8,128)S(1)} %shard_map.83.refs_7_), channel_id=1, source_target_pairs={{0,4},{1,5},{2,6},{3,7},{4,0},{5,1},{6,2},{7,3},{8,12},{9,13},{10,... | collective-permute-start | bytes 786440 | tf_op jit(solution)/shard_map/ppermute | solution.py:468
  144.7 9.7 %collective-permute-start.25 = (f32[1,128,256]{2,1,0:T(8,128)S(1)}, f32[1,128,256]{2,1,0:T(8,128)S(1)}, u32[]{:S(2)}, u32[]{:S(2)}) collective-permute-start(f32[1,128,256]{2,1,0:T(8,128)S(1)} %slice_add_fusion.30), channel_id=1, source_target_pairs={{0,2},{1,3},{2,0},{3,1},{4,6},{5,7},{6,4},{7,5},{8,10},{9,11},{10,... | collective-permute-start | bytes 393224 | tf_op jit(solution)/shard_map/ppermute | solution.py:468
  147.2 11.2 %collective-permute-start.28 = (f32[256,256]{1,0:T(8,128)S(1)}, f32[256,256]{1,0:T(8,128)S(1)}, u32[]{:S(2)}, u32[]{:S(2)}) collective-permute-start(f32[256,256]{1,0:T(8,128)S(1)} %shard_map.83.refs_7_), channel_id=1, source_target_pairs={{0,8},{1,9},{2,10},{3,11},{4,12},{5,13},{6,14},{7,15},{8,0},{9,1},... | collective-permute-start | bytes 786440 | tf_op jit(solution)/shard_map/ppermute | solution.py:468
  155.5 9.3 %collective-permute-start.31 = (f32[256,256]{1,0:T(8,128)S(1)}, f32[256,256]{1,0:T(8,128)S(1)}, u32[]{:S(2)}, u32[]{:S(2)}) collective-permute-start(f32[256,256]{1,0:T(8,128)S(1)} %shard_map.86.refs_8_), channel_id=1, source_target_pairs={{0,16},{1,17},{2,18},{3,19},{4,20},{5,21},{6,22},{7,23},{8,24},{9,... | collective-permute-start | bytes 786440 | tf_op jit(solution)/shard_map/ppermute | solution.py:468
  157.0 8.5 %collective-permute-start.27 = (f32[256,256]{1,0:T(8,128)S(1)}, f32[256,256]{1,0:T(8,128)S(1)}, u32[]{:S(2)}, u32[]{:S(2)}) collective-permute-start(f32[256,256]{1,0:T(8,128)S(1)} %shard_map.86.refs_8_), channel_id=1, source_target_pairs={{0,4},{1,5},{2,6},{3,7},{4,0},{5,1},{6,2},{7,3},{8,12},{9,13},{10,... | collective-permute-start | bytes 786440 | tf_op jit(solution)/shard_map/ppermute | solution.py:468
  157.0 9.1 %collective-permute-start.29 = (f32[256,256]{1,0:T(8,128)S(1)}, f32[256,256]{1,0:T(8,128)S(1)}, u32[]{:S(2)}, u32[]{:S(2)}) collective-permute-start(f32[256,256]{1,0:T(8,128)S(1)} %shard_map.86.refs_8_), channel_id=1, source_target_pairs={{0,8},{1,9},{2,10},{3,11},{4,12},{5,13},{6,14},{7,15},{8,0},{9,1},... | collective-permute-start | bytes 786440 | tf_op jit(solution)/shard_map/ppermute | solution.py:468
  157.6 12.8 %collective-permute-start.30 = (f32[256,256]{1,0:T(8,128)S(1)}, f32[256,256]{1,0:T(8,128)S(1)}, u32[]{:S(2)}, u32[]{:S(2)}) collective-permute-start(f32[256,256]{1,0:T(8,128)S(1)} %shard_map.83.refs_7_), channel_id=1, source_target_pairs={{0,16},{1,17},{2,18},{3,19},{4,20},{5,21},{6,22},{7,23},{8,24},{9,... | collective-permute-start | bytes 786440 | tf_op jit(solution)/shard_map/ppermute | solution.py:468
  158.4 19.0 %collective-permute-start.32 = (f32[256,256]{1,0:T(8,128)S(1)}, f32[256,256]{1,0:T(8,128)S(1)}, u32[]{:S(2)}, u32[]{:S(2)}) collective-permute-start(f32[256,256]{1,0:T(8,128)S(1)} %collective-permute-done.28.refs_11_), channel_id=1, source_target_pairs={{0,16},{1,17},{2,18},{3,19},{4,20},{5,21},{6,22},{7,23},{8,24},{9,... | collective-permute-start | bytes 786440 | tf_op jit(solution)/shard_map/ppermute | solution.py:468
  164.7 5.6 %copy-start.5 = (f32[256,256]{1,0:T(8,128)}, f32[256,256]{1,0:T(8,128)S(1)}, u32[]{:S(2)}) copy-start(f32[256,256]{1,0:T(8,128)S(1)} %collective-permute-done.31.refs_14_) | copy-start | bytes 786436
  164.7 12.6 %collective-permute-start.33 = (f32[256,256]{1,0:T(8,128)S(1)}, f32[256,256]{1,0:T(8,128)S(1)}, u32[]{:S(2)}, u32[]{:S(2)}) collective-permute-start(f32[256,256]{1,0:T(8,128)S(1)} %collective-permute-done.31.refs_14_), channel_id=1, source_target_pairs={{0,8},{1,9},{2,10},{3,11},{4,12},{5,13},{6,14},{7,15},{8,0},{9,1},... | collective-permute-start | bytes 786440 | tf_op jit(solution)/shard_map/ppermute | solution.py:468
  177.4 4.8 %copy-start.6 = (f32[256,256]{1,0:T(8,128)S(1)}, f32[256,256]{1,0:T(8,128)}, u32[]{:S(2)}) copy-start(f32[256,256]{1,0:T(8,128)} %copy-done.5) | copy-start | bytes 786436
  181.1 3.4 %collective-permute-start.38 = (f32[1,512,256]{2,1,0:T(8,128)S(1)}, f32[1,512,256]{2,1,0:T(8,128)S(1)}, u32[]{:S(2)}, u32[]{:S(2)}) collective-permute-start(f32[1,512,256]{2,1,0:T(8,128)S(1)} %get-tuple-element.20), channel_id=1, source_target_pairs={{0,4},{1,5},{2,6},{3,7},{4,0},{5,1},{6,2},{7,3},{8,12},{9,13},{10,... | collective-permute-start | bytes 1572872 | tf_op jit(solution)/shard_map/ppermute | solution.py:468
  181.1 2.3 %collective-permute-start.34 = (f32[256,256]{1,0:T(8,128)S(1)}, f32[256,256]{1,0:T(8,128)S(1)}, u32[]{:S(2)}, u32[]{:S(2)}) collective-permute-start(f32[256,256]{1,0:T(8,128)S(1)} %collective-permute-done.28.refs_11_), channel_id=1, source_target_pairs={{0,4},{1,5},{2,6},{3,7},{4,0},{5,1},{6,2},{7,3},{8,12},{9,13},{10,... | collective-permute-start | bytes 786440 | tf_op jit(solution)/shard_map/ppermute | solution.py:468
  181.6 2.1 %collective-permute-start.35 = (f32[256,256]{1,0:T(8,128)S(1)}, f32[256,256]{1,0:T(8,128)S(1)}, u32[]{:S(2)}, u32[]{:S(2)}) collective-permute-start(f32[256,256]{1,0:T(8,128)S(1)} %collective-permute-done.29.refs_12_), channel_id=1, source_target_pairs={{0,4},{1,5},{2,6},{3,7},{4,0},{5,1},{6,2},{7,3},{8,12},{9,13},{10,... | collective-permute-start | bytes 786440 | tf_op jit(solution)/shard_map/ppermute | solution.py:468
  181.6 2.5 %collective-permute-start.36 = (f32[256,256]{1,0:T(8,128)S(1)}, f32[256,256]{1,0:T(8,128)S(1)}, u32[]{:S(2)}, u32[]{:S(2)}) collective-permute-start(f32[256,256]{1,0:T(8,128)S(1)} %collective-permute-done.30.refs_13_), channel_id=1, source_target_pairs={{0,4},{1,5},{2,6},{3,7},{4,0},{5,1},{6,2},{7,3},{8,12},{9,13},{10,... | collective-permute-start | bytes 786440 | tf_op jit(solution)/shard_map/ppermute | solution.py:468
  182.1 2.4 %collective-permute-start.37 = (f32[256,256]{1,0:T(8,128)S(1)}, f32[256,256]{1,0:T(8,128)S(1)}, u32[]{:S(2)}, u32[]{:S(2)}) collective-permute-start(f32[256,256]{1,0:T(8,128)S(1)} %copy-done.6), channel_id=1, source_target_pairs={{0,4},{1,5},{2,6},{3,7},{4,0},{5,1},{6,2},{7,3},{8,12},{9,13},{10,... | collective-permute-start | bytes 786440 | tf_op jit(solution)/shard_map/ppermute | solution.py:468

commit v4 on v3

--- a/solution.py
+++ b/solution.py
@@ -131,16 +131,19 @@
     )(*([seeds] * parts), *([inverse] * len(upper_tiles(parts))))
 
 
-def seed_kernel(strips, me_ref, *refs):
-    coupling_refs, half_ref, sum_refs = refs[:strips], refs[strips], refs[strips + 1 :]
+def seed_kernel(pair, strips, orders, base, me_ref, *refs):
+    coupling_refs, half_ref = refs[: pair * strips], refs[pair * strips]
+    sum_refs = refs[pair * strips + 1 :]
     depth = coupling_refs[0].shape[0]
-    total = sum(
-        dot(half_ref[:, at * depth : (at + 1) * depth], ref[...])
-        for at, ref in enumerate(coupling_refs)
-    )
-    cols = total.shape[1] // len(sum_refs)
-    for chunk, ref in enumerate(sum_refs):
-        ref[0] = total[:, chunk * cols : (chunk + 1) * cols]
+    cols = sum_refs[0].shape[2]
+    for g in range(pair):
+        unit = spread(orders[0], pl.program_id(0) * pair + g)
+        total = sum(
+            dot(half_ref[:, at * depth : (at + 1) * depth], coupling_refs[g * strips + at][...])
+            for at in range(strips)
+        )
+        for chunk, (order, ref) in enumerate(zip(orders, sum_refs)):
+            ref[place_of(order, unit)] = total[:, chunk * cols : (chunk + 1) * cols]
 
 
 def seed_products(me, coupling, half, sub, orders, base, offset):
@@ -148,39 +151,29 @@
     cols = seed_cols(sub)
     wide = cols * len(orders)
     units = 1 << len(orders[0])
-
-    def unit_of(f):
-        return spread(orders[0], f) | base
-
-    def place(strip, f, me_ref):
-        return strip, ((unit_of(f) ^ me_ref[0]) * sub + offset) // wide
-
+    pair = min(units, 2)
     strip = strip_of(depth)
     strips = depth // strip
+
+    def place(g, strip, f, me_ref):
+        unit = spread(orders[0], f * pair + g) | base
+        return strip, ((unit ^ me_ref[0]) * sub + offset) // wide
+
     return call(
-        functools.partial(seed_kernel, strips),
-        (units,),
+        functools.partial(seed_kernel, pair, strips, orders, base),
+        (units // pair,),
         [
-            pl.BlockSpec((strip, wide), functools.partial(place, number))
+            pl.BlockSpec((strip, wide), functools.partial(place, g, number))
+            for g in range(pair)
             for number in range(strips)
         ]
-        + [
-            pl.BlockSpec((count, depth), lambda f, me_ref: (0, 0)),
-        ],
-        [
-            pl.BlockSpec(
-                (1, count, cols),
-                functools.partial(
-                    lambda order, f, me_ref: (place_of(order, unit_of(f)), 0, 0), order
-                ),
-            )
-            for order in orders
-        ],
+        + [pl.BlockSpec((count, depth), lambda f, me_ref: (0, 0))],
+        [pl.BlockSpec((units, count, cols), lambda f, me_ref: (0, 0, 0))] * len(orders),
         [jax.ShapeDtypeStruct((units, count, cols), F32)] * len(orders),
         2 * units * depth * wide * count,
         units * wide * (2 * depth + 4 * count),
         room=52 * MIB,
-    )(me, *([coupling] * strips), half)
+    )(me, *([coupling] * (pair * strips)), half)
 
 
 def strip_of(depth):
@@ -242,12 +235,12 @@
     )(*flat)
 
 
-def shared_kernel(bits, inner, base, col_bits, pieces, me_ref, *refs):
-    tiles, refs = refs[:pieces], refs[pieces:]
+def shared_kernel(bits, inner, several, pieces, me_ref, *refs):
+    tiles, refs = refs[: several * pieces], refs[several * pieces :]
     seed_ref, *received, out_ref, parts_ref, seed_parts_ref = refs
     depth = seed_ref.shape[0]
     group = 1 << len(inner)
-    rows = parts_ref.shape[0] // group
+    rows = parts_ref.shape[0] // (group * several)
     lanes = depth // pieces
     step = pl.program_id(0)
 
@@ -258,16 +251,17 @@
         seed_parts_ref[depth : 2 * depth] = high
         seed_parts_ref[2 * depth :] = low
 
-    for piece, ref in enumerate(tiles):
+    for number, ref in enumerate(tiles):
         high, low = split(ref.reshape(group * rows, lanes)[...])
-        at = piece * lanes
-        parts_ref[:, at : at + lanes] = high
-        parts_ref[:, depth + at : depth + at + lanes] = low
-        parts_ref[:, 2 * depth + at : 2 * depth + at + lanes] = high
+        at, place = number % pieces * lanes, pl.ds(number // pieces * group * rows, group * rows)
+        parts_ref[place, at : at + lanes] = high
+        parts_ref[place, depth + at : depth + at + lanes] = low
+        parts_ref[place, 2 * depth + at : 2 * depth + at + lanes] = high
     total = dot(parts_ref[...], seed_parts_ref[...])
     outer_bits = [bit for bit in bits if bit not in inner]
-    for g in range(group):
-        unit = spread(outer_bits, step) | (spread(inner, g) ^ (me_ref[0] & spread(inner, group - 1)))
+    for g in range(several * group):
+        col = spread(inner, g % group) ^ (me_ref[0] & spread(inner, group - 1))
+        unit = spread(outer_bits, step * several + g // group) | col
         place = place_of(bits, unit)
         term = total[g * rows : (g + 1) * rows]
         if received:
@@ -284,31 +278,36 @@
     inner = sorted([bit for bit in bits if bit < col_bits], reverse=True)
     outer_bits = [bit for bit in bits if bit >= col_bits]
     group = 1 << len(inner)
-
-    def place(piece, f, me_ref):
-        unit = (spread(outer_bits, f) | base) ^ me_ref[0]
+    several = 1
+
+    def place(number, piece, f, me_ref):
+        unit = (spread(outer_bits, f * several + number) | base) ^ me_ref[0]
         cols = [0 if bit in inner else (unit >> bit) & 1 for bit in reversed(range(col_bits))]
         return (unit >> col_bits, *cols, offset // rows, 0, piece)
 
     block = [2 if bit in inner else 1 for bit in reversed(range(col_bits))]
     in_specs = [
-        pl.BlockSpec((1, *block, rows, 1, lanes), functools.partial(place, piece))
+        pl.BlockSpec((1, *block, rows, 1, lanes), functools.partial(place, number, piece))
+        for number in range(several)
         for piece in range(pieces)
     ] + [pl.BlockSpec((depth, count), lambda f, me_ref: (0, 0))]
-    operands = [tiles] * pieces + [seed]
+    operands = [tiles] * (several * pieces) + [seed]
     if received is not None:
         half = received.shape[0] // units - 1
         in_specs.append(pl.BlockSpec((units, rows, count), lambda f, me_ref: (half, 0, 0)))
         operands.append(received)
     return call(
-        functools.partial(shared_kernel, bits, inner, base, col_bits, pieces),
-        (units // group,),
+        functools.partial(shared_kernel, bits, inner, several, pieces),
+        (units // (group * several),),
         in_specs,
         pl.BlockSpec((units, rows, count), lambda f, me_ref: (0, 0, 0)),
         jax.ShapeDtypeStruct((units, rows, count), F32),
         6 * units * rows * depth * count,
         4 * units * rows * (depth + count),
-        scratch=[pltpu.VMEM((group * rows, 3 * depth), BF16), pltpu.VMEM((3 * depth, count), BF16)],
+        scratch=[
+            pltpu.VMEM((several * group * rows, 3 * depth), BF16),
+            pltpu.VMEM((3 * depth, count), BF16),
+        ],
         room=34 * MIB,
         earlier=earlier,
     )(me, *operands)
@@ -366,13 +365,20 @@
             second = [
                 split(second_ref[at * tile : (at + 1) * tile]) for at in range(blocks * parts)
             ]
-            totals = {}
-            for at, (block, i, j) in enumerate(places):
-                fetches[at].wait()
-                term = dot3(split(held_ref[at]), second[block * parts + j])
-                totals[block, i] = term if i == j else totals[block, i] + term
-            for (block, i), total in totals.items():
-                out_ref[block, i * tile : (i + 1) * tile] = total
+            for fetch in fetches:
+                fetch.wait()
+            for block in range(blocks):
+                for i in range(parts):
+                    held = [
+                        split(held_ref[at])
+                        for at, place in enumerate(places)
+                        if place[:2] == (block, i)
+                    ]
+                    right = second[block * parts + i : (block + 1) * parts]
+                    out_ref[block, i * tile : (i + 1) * tile] = dot(
+                        jnp.concatenate([half[part] for part in (0, 1, 0) for half in held], axis=1),
+                        jnp.concatenate([half[part] for part in (0, 0, 1) for half in right], axis=0),
+                    )
 
 
 def coupled_step(me, coupling, start, pieces, numbers, adjoint, packs=False, inverse=None):
@@ -446,7 +452,7 @@
         flops,
         moved,
         scratch=scratch,
-        room=52 * MIB,
+        room=48 * MIB,
         **more,
     )(me, *operands)
 

time: 197 us -> 189 us (0.959)
  Pallas kernels: 86.5 us -> 79.1 us
    pallas_call x22, Pallas kernels: 86.5 us -> 79.1 us  [run(): pl.pallas_call(body, grid_spec=pltpu.PrefetchScalarGridSpec(num_scalar_pr...]
where the time goes in v4:
time: 189 us; the launch traced here: 188 us
  Pallas kernels  79.1 us (42%)
  waiting for transfers between devices  54.2 us (29%)
  starting transfers between devices  38.7 us (20%)
  other arithmetic  14 us (7%)
    pallas_call x22, Pallas kernels, run(): pl.pallas_call(body, grid_spec=pltpu.PrefetchScalarGridSpec(num_scalar_pr...  79.1 us
    ppermute x39, waiting for transfers between devices, exchange(): lax.ppermute(array, AXES, [(w, w ^ 1 << bit) for w in range(devices)])  54.2 us
    ppermute x39, starting transfers between devices, exchange(): lax.ppermute(array, AXES, [(w, w ^ 1 << bit) for w in range(devices)])  38.7 us
    add x14, other arithmetic, halved(): away = sum((term[half:2 * half] for term in terms))  12.8 us
  transfers between devices with their start and end apart: 39, of which 19 were waited for; matrix products, arithmetic and copies ran while one was open for 7% of the time, Pallas kernels for 30%

profile of v4, /device:TPU:0, one launch (start us, length us, event | category | flops | bytes accessed | tf_op | source)
XLA Modules:
  0.0 188.2 jit_solution(18143862905696346170)
XLA Ops:
  0.6 4.3 %shard_map.68 = (f32[256,1536]{1,0:T(8,128)}, bf16[256,1536]{1,0:T(8,128)(2,1)}) custom-call(f32[2,768,256]{2,1,0:T(8,128)} %bitcast.122, f32[2,768,256]{2,1,0:T(8,128)} %bitcast.123, f32[2,768,256]{2,1,0:T(8,128)} %bitcast.124, f32[2,768,768]{2,1,0:T(8,128)} %bitcast.114, f32[2,768,768]{2,1,0:T(8,128)} %bitcast.115, f32[2,768,768]{2,1,0:T(8,128)} %bitcast.116, ...), custom_call_target="tpu_custom_call" | custom-call | flops 1811939328 | bytes 9437184 | tf_op jit(solution)/shard_map/pallas_call | solution.py:55
  5.0 1.1 copy-done.2
  6.1 3.0 %shard_map.70 = f32[4,256,256]{2,1,0:T(8,128)S(1)} custom-call(s32[1]{0:T(128)} %bitcast.me_ref, bf16[1536,4096]{1,0:T(8,128)(2,1)} %bitcast.71, bf16[1536,4096]{1,0:T(8,128)(2,1)} %bitcast.61, bf16[1536,4096]{1,0:T(8,128)(2,1)} %bitcast.62, bf16[1536,4096]{1,0:T(8,128)(2,1)} %bitcast.63, bf16[1536,4096]{1,0:T(8,128)(2,1)} %bitcast.64, ...), custom_call_target="tpu_custom_call" | custom-call | flops 805306368 | bytes 4194304 | tf_op jit(solution)/shard_map/pallas_call | solution.py:55
  9.6 3.0 %shard_map.71 = f32[4,256,256]{2,1,0:T(8,128)S(1)} custom-call(s32[1]{0:T(128)} %bitcast.me_ref, bf16[1536,4096]{1,0:T(8,128)(2,1)} %bitcast.72, bf16[1536,4096]{1,0:T(8,128)(2,1)} %bitcast.73, bf16[1536,4096]{1,0:T(8,128)(2,1)} %bitcast.74, bf16[1536,4096]{1,0:T(8,128)(2,1)} %bitcast.75, bf16[1536,4096]{1,0:T(8,128)(2,1)} %bitcast.76, ...), custom_call_target="tpu_custom_call" | custom-call | flops 805306368 | bytes 4194304 | tf_op jit(solution)/shard_map/pallas_call | solution.py:55
  12.8 5.1 %shard_map.69 = (f32[4,256,256]{2,1,0:T(8,128)S(1)}, f32[4,256,256]{2,1,0:T(8,128)}) custom-call(s32[1]{0:T(128)} %bitcast.me_ref, bf16[1536,4096]{1,0:T(8,128)(2,1)} %bitcast.86, bf16[1536,4096]{1,0:T(8,128)(2,1)} %bitcast.85, bf16[1536,4096]{1,0:T(8,128)(2,1)} %bitcast.84, bf16[1536,4096]{1,0:T(8,128)(2,1)} %bitcast.87, bf16[1536,4096]{1,0:T(8,128)(2,1)} %bitcast.88, ...), custom_call_target="tpu_custom_call" | custom-call | flops 1610612736 | bytes 8388608 | tf_op jit(solution)/shard_map/pallas_call | solution.py:55
  18.0 2.9 %collective-permute-start.1 = (f32[2,256,256]{2,1,0:T(8,128)S(1)}, f32[2,256,256]{2,1,0:T(8,128)S(1)}, u32[]{:S(2)}, u32[]{:S(2)}) collective-permute-start(f32[2,256,256]{2,1,0:T(8,128)S(1)} %slice_add_fusion.9), channel_id=1, source_target_pairs={{0,8},{1,9},{2,10},{3,11},{4,12},{5,13},{6,14},{7,15},{8,0},{9,1},... | collective-permute-start | bytes 1572872 | tf_op jit(solution)/shard_map/ppermute | solution.py:474
  20.9 1.1 slice_add_fusion.8
  22.0 1.6 collective-permute-start.4
  23.6 9.6 %collective-permute-done.1 = f32[2,256,256]{2,1,0:T(8,128)S(1)} collective-permute-done((f32[2,256,256]{2,1,0:T(8,128)S(1)}, f32[2,256,256]{2,1,0:T(8,128)S(1)}, u32[]{:S(2)}, u32[]{:S(2)}) %collective-permute-start.1) | collective-permute-done | bytes 524320 | tf_op jit(solution)/shard_map/ppermute | solution.py:474
  33.3 1.8 collective-permute-start.2
  35.1 0.9 collective-permute-done.4
  36.8 4.7 %collective-permute-done.2.refs_1_ = f32[1,256,256]{2,1,0:T(8,128)S(1)} collective-permute-done((f32[1,256,256]{2,1,0:T(8,128)S(1)}, f32[1,256,256]{2,1,0:T(8,128)S(1)}, u32[]{:S(2)}, u32[]{:S(2)}) %collective-permute-start.2) | collective-permute-done | bytes 262176 | tf_op jit(solution)/shard_map/ppermute | solution.py:474
  41.5 1.9 collective-permute-done.5.refs_3_
  43.6 4.5 %shard_map.73 = f32[16,128,256]{2,1,0:T(8,128)S(1)} custom-call(s32[1]{0:T(128)} %bitcast.4.me_ref.refs_0_, f32[8,2,2,512,1,512]{5,4,3,2,1,0:T(1,128)} %bitcast.12, f32[8,2,2,512,1,512]{5,4,3,2,1,0:T(1,128)} %bitcast.13, f32[8,2,2,512,1,512]{5,4,3,2,1,0:T(1,128)} %bitcast.14, f32[8,2,2,512,1,512]{5,4,3,2,1,0:T(1,128)} %bitcast.15, ...), custom_call_target="tpu_custom_call" | custom-call | flops 1610612736 | bytes 6291456 | tf_op jit(solution)/shard_map/pallas_call | solution.py:55
  48.2 4.5 %shard_map.75 = f32[16,128,256]{2,1,0:T(8,128)S(1)} custom-call(s32[1]{0:T(128)} %bitcast.4.me_ref.refs_0_, f32[8,2,2,512,1,512]{5,4,3,2,1,0:T(1,128)} %bitcast.16, f32[8,2,2,512,1,512]{5,4,3,2,1,0:T(1,128)} %bitcast.17, f32[8,2,2,512,1,512]{5,4,3,2,1,0:T(1,128)} %bitcast.18, f32[8,2,2,512,1,512]{5,4,3,2,1,0:T(1,128)} %bitcast.19, ...), custom_call_target="tpu_custom_call" | custom-call | flops 1610612736 | bytes 6291456 | tf_op jit(solution)/shard_map/pallas_call | solution.py:55
  53.3 4.5 %shard_map.77 = f32[16,128,256]{2,1,0:T(8,128)S(1)} custom-call(s32[1]{0:T(128)} %bitcast.4.me_ref.refs_0_, f32[8,2,2,512,1,512]{5,4,3,2,1,0:T(1,128)} %bitcast.20, f32[8,2,2,512,1,512]{5,4,3,2,1,0:T(1,128)} %bitcast.21, f32[8,2,2,512,1,512]{5,4,3,2,1,0:T(1,128)} %bitcast.22, f32[8,2,2,512,1,512]{5,4,3,2,1,0:T(1,128)} %bitcast.23, ...), custom_call_target="tpu_custom_call" | custom-call | flops 1610612736 | bytes 6291456 | tf_op jit(solution)/shard_map/pallas_call | solution.py:55
  57.9 4.5 %shard_map.79 = f32[16,128,256]{2,1,0:T(8,128)S(1)} custom-call(s32[1]{0:T(128)} %bitcast.4.me_ref.refs_0_, f32[8,2,2,512,1,512]{5,4,3,2,1,0:T(1,128)} %bitcast.24, f32[8,2,2,512,1,512]{5,4,3,2,1,0:T(1,128)} %bitcast.25, f32[8,2,2,512,1,512]{5,4,3,2,1,0:T(1,128)} %bitcast.26, f32[8,2,2,512,1,512]{5,4,3,2,1,0:T(1,128)} %bitcast.27, ...), custom_call_target="tpu_custom_call" | custom-call | flops 1610612736 | bytes 6291456 | tf_op jit(solution)/shard_map/pallas_call | solution.py:55
  62.9 3.5 %shard_map.74.refs_6_ = f32[8,128,256]{2,1,0:T(8,128)} custom-call(s32[1]{0:T(128)} %bitcast.4.me_ref.refs_0_, f32[8,2,2,512,1,512]{5,4,3,2,1,0:T(1,128)} %bitcast.28, f32[8,2,2,512,1,512]{5,4,3,2,1,0:T(1,128)} %bitcast.29, f32[8,2,2,512,1,512]{5,4,3,2,1,0:T(1,128)} %bitcast.30, f32[8,2,2,512,1,512]{5,4,3,2,1,0:T(1,128)} %bitcast.31, ...), custom_call_target="tpu_custom_call" | custom-call | flops 805306368 | bytes 3145728 | tf_op jit(solution)/shard_map/pallas_call | solution.py:55
  67.2 3.5 %shard_map.76.refs_7_ = f32[8,128,256]{2,1,0:T(8,128)} custom-call(s32[1]{0:T(128)} %bitcast.4.me_ref.refs_0_, f32[8,2,2,512,1,512]{5,4,3,2,1,0:T(1,128)} %bitcast.35, f32[8,2,2,512,1,512]{5,4,3,2,1,0:T(1,128)} %bitcast.33, f32[8,2,2,512,1,512]{5,4,3,2,1,0:T(1,128)} %bitcast.34, f32[8,2,2,512,1,512]{5,4,3,2,1,0:T(1,128)} %bitcast.32, ...), custom_call_target="tpu_custom_call" | custom-call | flops 805306368 | bytes 3145728 | tf_op jit(solution)/shard_map/pallas_call | solution.py:55
  70.7 1.2 collective-permute-start.14
  71.9 5.2 %shard_map.78.refs_8_ = f32[8,128,256]{2,1,0:T(8,128)} custom-call(s32[1]{0:T(128)} %bitcast.4.me_ref.refs_0_, f32[8,2,2,512,1,512]{5,4,3,2,1,0:T(1,128)} %bitcast.36, f32[8,2,2,512,1,512]{5,4,3,2,1,0:T(1,128)} %bitcast.37, f32[8,2,2,512,1,512]{5,4,3,2,1,0:T(1,128)} %bitcast.38, f32[8,2,2,512,1,512]{5,4,3,2,1,0:T(1,128)} %bitcast.39, ...), custom_call_target="tpu_custom_call" | custom-call | flops 805306368 | bytes 3145728 | tf_op jit(solution)/shard_map/pallas_call | solution.py:55
  77.2 1.6 collective-permute-start.18
  78.8 3.6 %shard_map.80.refs_9_ = f32[8,128,256]{2,1,0:T(8,128)} custom-call(s32[1]{0:T(128)} %bitcast.4.me_ref.refs_0_, f32[8,2,2,512,1,512]{5,4,3,2,1,0:T(1,128)} %bitcast.40, f32[8,2,2,512,1,512]{5,4,3,2,1,0:T(1,128)} %bitcast.41, f32[8,2,2,512,1,512]{5,4,3,2,1,0:T(1,128)} %bitcast.42, f32[8,2,2,512,1,512]{5,4,3,2,1,0:T(1,128)} %bitcast.43, ...), custom_call_target="tpu_custom_call" | custom-call | flops 805306368 | bytes 3145728 | tf_op jit(solution)/shard_map/pallas_call | solution.py:55
  82.3 1.5 collective-permute-start.22
  83.9 2.6 %shard_map.81.refs_0_ = f32[8,128,256]{2,1,0:T(8,128)S(1)} custom-call(s32[1]{0:T(128)} %bitcast.4.me_ref.refs_0_, f32[8,2,2,512,1,512]{5,4,3,2,1,0:T(1,128)} %bitcast.46, f32[8,2,2,512,1,512]{5,4,3,2,1,0:T(1,128)} %bitcast.45, f32[8,2,2,512,1,512]{5,4,3,2,1,0:T(1,128)} %bitcast.44, f32[8,2,2,512,1,512]{5,4,3,2,1,0:T(1,128)} %bitcast.47, ...), custom_call_target="tpu_custom_call" | custom-call | flops 805306368 | bytes 3145728 | tf_op jit(solution)/shard_map/pallas_call | solution.py:55
  86.4 2.6 %shard_map.82.refs_6_ = f32[8,128,256]{2,1,0:T(8,128)S(1)} custom-call(s32[1]{0:T(128)} %bitcast.4.me_ref.refs_0_, f32[8,2,2,512,1,512]{5,4,3,2,1,0:T(1,128)} %bitcast.48, f32[8,2,2,512,1,512]{5,4,3,2,1,0:T(1,128)} %bitcast.49, f32[8,2,2,512,1,512]{5,4,3,2,1,0:T(1,128)} %bitcast.50, f32[8,2,2,512,1,512]{5,4,3,2,1,0:T(1,128)} %bitcast.51, ...), custom_call_target="tpu_custom_call" | custom-call | flops 805306368 | bytes 3145728 | tf_op jit(solution)/shard_map/pallas_call | solution.py:55
  89.0 3.9 %shard_map.84.refs_0_ = f32[8,128,256]{2,1,0:T(8,128)S(1)} custom-call(s32[1]{0:T(128)} %bitcast.4.me_ref.refs_0_, f32[8,2,2,512,1,512]{5,4,3,2,1,0:T(1,128)} %bitcast.52, f32[8,2,2,512,1,512]{5,4,3,2,1,0:T(1,128)} %bitcast.53, f32[8,2,2,512,1,512]{5,4,3,2,1,0:T(1,128)} %bitcast.54, f32[8,2,2,512,1,512]{5,4,3,2,1,0:T(1,128)} %bitcast.55, ...), custom_call_target="tpu_custom_call" | custom-call | flops 805306368 | bytes 3145728 | tf_op jit(solution)/shard_map/pallas_call | solution.py:55
  92.9 2.6 %shard_map.85.refs_6_ = f32[8,128,256]{2,1,0:T(8,128)S(1)} custom-call(s32[1]{0:T(128)} %bitcast.4.me_ref.refs_0_, f32[8,2,2,512,1,512]{5,4,3,2,1,0:T(1,128)} %bitcast.56, f32[8,2,2,512,1,512]{5,4,3,2,1,0:T(1,128)} %bitcast.57, f32[8,2,2,512,1,512]{5,4,3,2,1,0:T(1,128)} %bitcast.58, f32[8,2,2,512,1,512]{5,4,3,2,1,0:T(1,128)} %bitcast.59, ...), custom_call_target="tpu_custom_call" | custom-call | flops 805306368 | bytes 3145728 | tf_op jit(solution)/shard_map/pallas_call | solution.py:55
  95.5 1.3 slice_add_fusion.6
  97.4 1.1 slice_add_fusion.4
  99.1 4.5 %collective-permute-done.18.refs_2_ = f32[8,128,256]{2,1,0:T(8,128)} collective-permute-done((f32[8,128,256]{2,1,0:T(8,128)}, f32[8,128,256]{2,1,0:T(8,128)}, u32[]{:S(2)}, u32[]{:S(2)}) %collective-permute-start.18) | collective-permute-done | bytes 1048608 | tf_op jit(solution)/shard_map/ppermute | solution.py:474
  103.6 1.1 slice_add_fusion.2
  104.7 1.6 collective-permute-start.19
  106.3 8.9 %collective-permute-done.22.refs_8_ = f32[8,128,256]{2,1,0:T(8,128)} collective-permute-done((f32[8,128,256]{2,1,0:T(8,128)}, f32[8,128,256]{2,1,0:T(8,128)}, u32[]{:S(2)}, u32[]{:S(2)}) %collective-permute-start.22) | collective-permute-done | bytes 1048608 | tf_op jit(solution)/shard_map/ppermute | solution.py:474
  115.2 1.1 slice_add_fusion
  116.4 1.6 collective-permute-start.23
  117.9 1.0 slice_add_fusion.19
  119.0 1.7 collective-permute-start.12
  120.6 1.0 slice_add_fusion.16
  121.6 2.6 %collective-permute-start.16 = (f32[2,128,256]{2,1,0:T(8,128)S(1)}, f32[2,128,256]{2,1,0:T(8,128)S(1)}, u32[]{:S(2)}, u32[]{:S(2)}) collective-permute-start(f32[2,128,256]{2,1,0:T(8,128)S(1)} %slice_add_fusion.16), channel_id=1, source_target_pairs={{0,2},{1,3},{2,0},{3,1},{4,6},{5,7},{6,4},{7,5},{8,10},{9,11},{10,... | collective-permute-start | bytes 786440 | tf_op jit(solution)/shard_map/ppermute | solution.py:474
  124.3 1.2 collective-permute-done.19.refs_3_
  125.5 1.0 slice_add_fusion.13
  126.5 1.6 collective-permute-start.20
  128.8 1.0 slice_add_fusion.10
  129.8 1.6 collective-permute-start.24
  131.4 1.0 slice_add_fusion.42
  132.4 2.7 %collective-permute-start.13 = (f32[1,128,256]{2,1,0:T(8,128)S(1)}, f32[1,128,256]{2,1,0:T(8,128)S(1)}, u32[]{:S(2)}, u32[]{:S(2)}) collective-permute-start(f32[1,128,256]{2,1,0:T(8,128)S(1)} %slice_add_fusion.42), channel_id=1, source_target_pairs={{0,2},{1,3},{2,0},{3,1},{4,6},{5,7},{6,4},{7,5},{8,10},{9,11},{10,... | collective-permute-start | bytes 393224 | tf_op jit(solution)/shard_map/ppermute | solution.py:474
  135.1 1.0 slice_add_fusion.38
  136.0 0.9 collective-permute-start.17
  136.9 0.9 slice_add_fusion.34
  138.2 2.6 %collective-permute-done.13.refs_5_ = f32[1,128,256]{2,1,0:T(8,128)S(1)} collective-permute-done((f32[1,128,256]{2,1,0:T(8,128)S(1)}, f32[1,128,256]{2,1,0:T(8,128)S(1)}, u32[]{:S(2)}, u32[]{:S(2)}) %collective-permute-start.13) | collective-permute-done | bytes 131104 | tf_op jit(solution)/shard_map/ppermute | solution.py:474
  141.0 1.0 shard_map.83.refs_7_
  142.2 1.0 slice_add_fusion.30
  143.1 2.5 %collective-permute-start.25 = (f32[1,128,256]{2,1,0:T(8,128)S(1)}, f32[1,128,256]{2,1,0:T(8,128)S(1)}, u32[]{:S(2)}, u32[]{:S(2)}) collective-permute-start(f32[1,128,256]{2,1,0:T(8,128)S(1)} %slice_add_fusion.30), channel_id=1, source_target_pairs={{0,2},{1,3},{2,0},{3,1},{4,6},{5,7},{6,4},{7,5},{8,10},{9,11},{10,... | collective-permute-start | bytes 393224 | tf_op jit(solution)/shard_map/ppermute | solution.py:474
  146.3 6.5 %collective-permute-done.25.refs_11_ = f32[1,128,256]{2,1,0:T(8,128)S(1)} collective-permute-done((f32[1,128,256]{2,1,0:T(8,128)S(1)}, f32[1,128,256]{2,1,0:T(8,128)S(1)}, u32[]{:S(2)}, u32[]{:S(2)}) %collective-permute-start.25) | collective-permute-done | bytes 131104 | tf_op jit(solution)/shard_map/ppermute | solution.py:474
  152.8 1.1 shard_map.86.refs_8_
  153.9 1.6 collective-permute-start.31
  156.8 1.2 collective-permute-start.32
  158.0 5.2 %collective-permute-done.31.refs_14_ = f32[256,256]{1,0:T(8,128)S(1)} collective-permute-done((f32[256,256]{1,0:T(8,128)S(1)}, f32[256,256]{1,0:T(8,128)S(1)}, u32[]{:S(2)}, u32[]{:S(2)}) %collective-permute-start.31) | collective-permute-done | bytes 262176 | tf_op jit(solution)/shard_map/ppermute | solution.py:474
  164.5 4.2 %collective-permute-done.30.refs_13_ = f32[256,256]{1,0:T(8,128)S(1)} collective-permute-done((f32[256,256]{1,0:T(8,128)S(1)}, f32[256,256]{1,0:T(8,128)S(1)}, u32[]{:S(2)}, u32[]{:S(2)}) %collective-permute-start.30) | collective-permute-done | bytes 262176 | tf_op jit(solution)/shard_map/ppermute | solution.py:474
  168.8 5.8 %shard_map.87 = (f32[1536,256]{1,0:T(8,128)S(1)}, f32[4096,256]{1,0:T(8,128)}) custom-call(s32[1]{0:T(128)} %bitcast.me_ref, bf16[1536,4096]{1,0:T(8,128)(2,1)} %bitcast.99, bf16[1536,4096]{1,0:T(8,128)(2,1)} %bitcast.97, bf16[1536,4096]{1,0:T(8,128)(2,1)} %bitcast.98, bf16[1536,4096]{1,0:T(8,128)(2,1)} %bitcast.96, bf16[1536,4096]{1,0:T(8,128)(2,1)} %bitcast.100, ...), custom_call_target="tpu_custom_call" | custom-call | flops 1610612736 | bytes 13631488 | tf_op jit(solution)/shard_map/pallas_call | solution.py:55
  174.5 2.2 %shard_map.88 = (f32[1536,256]{1,0:T(8,128)S(1)}, f32[4096,256]{1,0:T(8,128)}, f32[1,512,256]{2,1,0:T(8,128)S(1)}) custom-call(s32[1]{0:T(128)} %bitcast.me_ref, bf16[1536,4096]{1,0:T(8,128)(2,1)} %bitcast.102, bf16[1536,4096]{1,0:T(8,128)(2,1)} %bitcast.103, bf16[1536,4096]{1,0:T(8,128)(2,1)} %bitcast.104, ...), custom_call_target="tpu_custom_call", output_to_operand_aliasing={{1}: (10, {})} | custom-call | flops 402653184 | bytes 5767168 | tf_op jit(solution)/shard_map/pallas_call | solution.py:55
  177.8 1.3 collective-permute-done.34.refs_7_
  180.2 7.8 %shard_map.89 = (f32[2,768,256]{2,1,0:T(8,128)}, f32[4096,256]{1,0:T(8,128)}) custom-call(s32[1]{0:T(128)} %bitcast.me_ref, bf16[1536,4096]{1,0:T(8,128)(2,1)} %bitcast.108, bf16[1536,4096]{1,0:T(8,128)(2,1)} %bitcast.109, bf16[1536,4096]{1,0:T(8,128)(2,1)} %bitcast.110, bf16[1536,4096]{1,0:T(8,128)(2,1)} %bitcast.111, ...), custom_call_target="tpu_custom_call", output_to_operand_aliasing={{1}: (13, {})} | custom-call | flops 3019898880 | bytes 15728640 | tf_op jit(solution)/shard_map/pallas_call | solution.py:55
  (64 shorter events, 12.1 us)
Async XLA Ops:
  5.0 1.1 copy-start.2
  9.1 8.9 %collective-permute-start = (f32[4,256,256]{2,1,0:T(8,128)S(1)}, f32[4,256,256]{2,1,0:T(8,128)S(1)}, u32[]{:S(2)}, u32[]{:S(2)}) collective-permute-start(f32[4,256,256]{2,1,0:T(8,128)S(1)} %shard_map.70), channel_id=1, source_target_pairs={{0,4},{1,5},{2,6},{3,7},{4,0},{5,1},{6,2},{7,3},{8,12},{9,13},{10,... | collective-permute-start | bytes 3145736 | tf_op jit(solution)/shard_map/ppermute | solution.py:474
  12.6 8.3 %collective-permute-start.3 = (f32[4,256,256]{2,1,0:T(8,128)S(1)}, f32[4,256,256]{2,1,0:T(8,128)S(1)}, u32[]{:S(2)}, u32[]{:S(2)}) collective-permute-start(f32[4,256,256]{2,1,0:T(8,128)S(1)} %shard_map.71), channel_id=1, source_target_pairs={{0,4},{1,5},{2,6},{3,7},{4,0},{5,1},{6,2},{7,3},{8,12},{9,13},{10,... | collective-permute-start | bytes 3145736 | tf_op jit(solution)/shard_map/ppermute | solution.py:474
  18.0 18.0 %copy-start.5 = (f32[4,256,256]{2,1,0:T(8,128)S(1)}, f32[4,256,256]{2,1,0:T(8,128)}, u32[]{:S(2)}) copy-start(f32[4,256,256]{2,1,0:T(8,128)} %get-tuple-element.16) | copy-start | bytes 3145732
  18.0 15.2 %collective-permute-start.1 = (f32[2,256,256]{2,1,0:T(8,128)S(1)}, f32[2,256,256]{2,1,0:T(8,128)S(1)}, u32[]{:S(2)}, u32[]{:S(2)}) collective-permute-start(f32[2,256,256]{2,1,0:T(8,128)S(1)} %slice_add_fusion.9), channel_id=1, source_target_pairs={{0,8},{1,9},{2,10},{3,11},{4,12},{5,13},{6,14},{7,15},{8,0},{9,1},... | collective-permute-start | bytes 1572872 | tf_op jit(solution)/shard_map/ppermute | solution.py:474
  22.0 21.3 %copy-start.4 = (f32[1,512,256]{2,1,0:T(8,128)S(1)}, f32[1,512,256]{2,1,0:T(8,128)}, u32[]{:S(2)}) copy-start(f32[1,512,256]{2,1,0:T(8,128)} %param.8) | copy-start | bytes 1572868
  22.0 13.9 %collective-permute-start.4 = (f32[2,256,256]{2,1,0:T(8,128)S(1)}, f32[2,256,256]{2,1,0:T(8,128)S(1)}, u32[]{:S(2)}, u32[]{:S(2)}) collective-permute-start(f32[2,256,256]{2,1,0:T(8,128)S(1)} %slice_add_fusion.8), channel_id=1, source_target_pairs={{0,16},{1,17},{2,18},{3,19},{4,20},{5,21},{6,22},{7,23},{8,24},{9,... | collective-permute-start | bytes 1572872 | tf_op jit(solution)/shard_map/ppermute | solution.py:474
  33.3 8.2 %collective-permute-start.2 = (f32[1,256,256]{2,1,0:T(8,128)S(1)}, f32[1,256,256]{2,1,0:T(8,128)S(1)}, u32[]{:S(2)}, u32[]{:S(2)}) collective-permute-start(f32[1,256,256]{2,1,0:T(8,128)S(1)} %get-tuple-element.26), channel_id=1, source_target_pairs={{0,16},{1,17},{2,18},{3,19},{4,20},{5,21},{6,22},{7,23},{8,24},{9,... | collective-permute-start | bytes 786440 | tf_op jit(solution)/shard_map/ppermute | solution.py:474
  36.1 7.3 %collective-permute-start.5 = (f32[1,256,256]{2,1,0:T(8,128)S(1)}, f32[1,256,256]{2,1,0:T(8,128)S(1)}, u32[]{:S(2)}, u32[]{:S(2)}) collective-permute-start(f32[1,256,256]{2,1,0:T(8,128)S(1)} %get-tuple-element.24), channel_id=1, source_target_pairs={{0,8},{1,9},{2,10},{3,11},{4,12},{5,13},{6,14},{7,15},{8,0},{9,1},... | collective-permute-start | bytes 786440 | tf_op jit(solution)/shard_map/ppermute | solution.py:474
  48.1 14.8 %collective-permute-start.6 = (f32[16,128,256]{2,1,0:T(8,128)S(1)}, f32[16,128,256]{2,1,0:T(8,128)S(1)}, u32[]{:S(2)}, u32[]{:S(2)}) collective-permute-start(f32[16,128,256]{2,1,0:T(8,128)S(1)} %shard_map.73), channel_id=1, source_target_pairs={{0,4},{1,5},{2,6},{3,7},{4,0},{5,1},{6,2},{7,3},{8,12},{9,13},{10,... | collective-permute-start | bytes 6291464 | tf_op jit(solution)/shard_map/ppermute | solution.py:474
  52.7 14.5 %collective-permute-start.7 = (f32[16,128,256]{2,1,0:T(8,128)S(1)}, f32[16,128,256]{2,1,0:T(8,128)S(1)}, u32[]{:S(2)}, u32[]{:S(2)}) collective-permute-start(f32[16,128,256]{2,1,0:T(8,128)S(1)} %shard_map.75), channel_id=1, source_target_pairs={{0,4},{1,5},{2,6},{3,7},{4,0},{5,1},{6,2},{7,3},{8,12},{9,13},{10,... | collective-permute-start | bytes 6291464 | tf_op jit(solution)/shard_map/ppermute | solution.py:474
  57.7 14.2 %collective-permute-start.8 = (f32[16,128,256]{2,1,0:T(8,128)S(1)}, f32[16,128,256]{2,1,0:T(8,128)S(1)}, u32[]{:S(2)}, u32[]{:S(2)}) collective-permute-start(f32[16,128,256]{2,1,0:T(8,128)S(1)} %shard_map.77), channel_id=1, source_target_pairs={{0,4},{1,5},{2,6},{3,7},{4,0},{5,1},{6,2},{7,3},{8,12},{9,13},{10,... | collective-permute-start | bytes 6291464 | tf_op jit(solution)/shard_map/ppermute | solution.py:474
  62.4 16.4 %collective-permute-start.9 = (f32[16,128,256]{2,1,0:T(8,128)S(1)}, f32[16,128,256]{2,1,0:T(8,128)S(1)}, u32[]{:S(2)}, u32[]{:S(2)}) collective-permute-start(f32[16,128,256]{2,1,0:T(8,128)S(1)} %shard_map.79), channel_id=1, source_target_pairs={{0,4},{1,5},{2,6},{3,7},{4,0},{5,1},{6,2},{7,3},{8,12},{9,13},{10,... | collective-permute-start | bytes 6291464 | tf_op jit(solution)/shard_map/ppermute | solution.py:474
  66.4 29.1 %collective-permute-start.10 = (f32[8,128,256]{2,1,0:T(8,128)}, f32[8,128,256]{2,1,0:T(8,128)}, u32[]{:S(2)}, u32[]{:S(2)}) collective-permute-start(f32[8,128,256]{2,1,0:T(8,128)} %shard_map.74.refs_6_), channel_id=1, source_target_pairs={{0,8},{1,9},{2,10},{3,11},{4,12},{5,13},{6,14},{7,15},{8,0},{9,1},... | collective-permute-start | bytes 3145736 | tf_op jit(solution)/shard_map/ppermute | solution.py:474
  70.7 26.7 %collective-permute-start.14 = (f32[8,128,256]{2,1,0:T(8,128)}, f32[8,128,256]{2,1,0:T(8,128)}, u32[]{:S(2)}, u32[]{:S(2)}) collective-permute-start(f32[8,128,256]{2,1,0:T(8,128)} %shard_map.76.refs_7_), channel_id=1, source_target_pairs={{0,16},{1,17},{2,18},{3,19},{4,20},{5,21},{6,22},{7,23},{8,24},{9,... | collective-permute-start | bytes 3145736 | tf_op jit(solution)/shard_map/ppermute | solution.py:474
  71.9 5.2 %copy-start = (f32[16,128,256]{2,1,0:T(8,128)}, f32[16,128,256]{2,1,0:T(8,128)S(1)}, u32[]{:S(2)}) copy-start(f32[16,128,256]{2,1,0:T(8,128)S(1)} %collective-permute-done.8.refs_5_.refs_1_) | copy-start | bytes 6291460
  77.2 26.4 %collective-permute-start.18 = (f32[8,128,256]{2,1,0:T(8,128)}, f32[8,128,256]{2,1,0:T(8,128)}, u32[]{:S(2)}, u32[]{:S(2)}) collective-permute-start(f32[8,128,256]{2,1,0:T(8,128)} %shard_map.78.refs_8_), channel_id=1, source_target_pairs={{0,1},{1,0},{2,3},{3,2},{4,5},{5,4},{6,7},{7,6},{8,9},{9,8},{10,11... | collective-permute-start | bytes 3145736 | tf_op jit(solution)/shard_map/ppermute | solution.py:474
  82.3 32.9 %collective-permute-start.22 = (f32[8,128,256]{2,1,0:T(8,128)}, f32[8,128,256]{2,1,0:T(8,128)}, u32[]{:S(2)}, u32[]{:S(2)}) collective-permute-start(f32[8,128,256]{2,1,0:T(8,128)} %shard_map.80.refs_9_), channel_id=1, source_target_pairs={{0,8},{1,9},{2,10},{3,11},{4,12},{5,13},{6,14},{7,15},{8,0},{9,1},... | collective-permute-start | bytes 3145736 | tf_op jit(solution)/shard_map/ppermute | solution.py:474
  95.5 8.1 %copy-start.1 = (f32[16,128,256]{2,1,0:T(8,128)S(1)}, f32[16,128,256]{2,1,0:T(8,128)}, u32[]{:S(2)}) copy-start(f32[16,128,256]{2,1,0:T(8,128)} %copy-done) | copy-start | bytes 6291460
  96.8 21.1 %collective-permute-start.11 = (f32[4,128,256]{2,1,0:T(8,128)S(1)}, f32[4,128,256]{2,1,0:T(8,128)S(1)}, u32[]{:S(2)}, u32[]{:S(2)}) collective-permute-start(f32[4,128,256]{2,1,0:T(8,128)S(1)} %slice_add_fusion.6), channel_id=1, source_target_pairs={{0,16},{1,17},{2,18},{3,19},{4,20},{5,21},{6,22},{7,23},{8,24},{9,... | collective-permute-start | bytes 1572872 | tf_op jit(solution)/shard_map/ppermute | solution.py:474
  98.6 22.1 %collective-permute-start.15 = (f32[4,128,256]{2,1,0:T(8,128)S(1)}, f32[4,128,256]{2,1,0:T(8,128)S(1)}, u32[]{:S(2)}, u32[]{:S(2)}) collective-permute-start(f32[4,128,256]{2,1,0:T(8,128)S(1)} %slice_add_fusion.4), channel_id=1, source_target_pairs={{0,1},{1,0},{2,3},{3,2},{4,5},{5,4},{6,7},{7,6},{8,9},{9,8},{10,11... | collective-permute-start | bytes 1572872 | tf_op jit(solution)/shard_map/ppermute | solution.py:474
  104.7 20.7 %collective-permute-start.19 = (f32[4,128,256]{2,1,0:T(8,128)S(1)}, f32[4,128,256]{2,1,0:T(8,128)S(1)}, u32[]{:S(2)}, u32[]{:S(2)}) collective-permute-start(f32[4,128,256]{2,1,0:T(8,128)S(1)} %slice_add_fusion.2), channel_id=1, source_target_pairs={{0,8},{1,9},{2,10},{3,11},{4,12},{5,13},{6,14},{7,15},{8,0},{9,1},... | collective-permute-start | bytes 1572872 | tf_op jit(solution)/shard_map/ppermute | solution.py:474
  116.4 12.4 %collective-permute-start.23 = (f32[4,128,256]{2,1,0:T(8,128)S(1)}, f32[4,128,256]{2,1,0:T(8,128)S(1)}, u32[]{:S(2)}, u32[]{:S(2)}) collective-permute-start(f32[4,128,256]{2,1,0:T(8,128)S(1)} %slice_add_fusion), channel_id=1, source_target_pairs={{0,16},{1,17},{2,18},{3,19},{4,20},{5,21},{6,22},{7,23},{8,24},{9,... | collective-permute-start | bytes 1572872 | tf_op jit(solution)/shard_map/ppermute | solution.py:474
  119.0 12.5 %collective-permute-start.12 = (f32[2,128,256]{2,1,0:T(8,128)S(1)}, f32[2,128,256]{2,1,0:T(8,128)S(1)}, u32[]{:S(2)}, u32[]{:S(2)}) collective-permute-start(f32[2,128,256]{2,1,0:T(8,128)S(1)} %slice_add_fusion.19), channel_id=1, source_target_pairs={{0,1},{1,0},{2,3},{3,2},{4,5},{5,4},{6,7},{7,6},{8,9},{9,8},{10,11... | collective-permute-start | bytes 786440 | tf_op jit(solution)/shard_map/ppermute | solution.py:474
  121.6 13.4 %collective-permute-start.16 = (f32[2,128,256]{2,1,0:T(8,128)S(1)}, f32[2,128,256]{2,1,0:T(8,128)S(1)}, u32[]{:S(2)}, u32[]{:S(2)}) collective-permute-start(f32[2,128,256]{2,1,0:T(8,128)S(1)} %slice_add_fusion.16), channel_id=1, source_target_pairs={{0,2},{1,3},{2,0},{3,1},{4,6},{5,7},{6,4},{7,5},{8,10},{9,11},{10,... | collective-permute-start | bytes 786440 | tf_op jit(solution)/shard_map/ppermute | solution.py:474
  126.5 10.4 %collective-permute-start.20 = (f32[2,128,256]{2,1,0:T(8,128)S(1)}, f32[2,128,256]{2,1,0:T(8,128)S(1)}, u32[]{:S(2)}, u32[]{:S(2)}) collective-permute-start(f32[2,128,256]{2,1,0:T(8,128)S(1)} %slice_add_fusion.13), channel_id=1, source_target_pairs={{0,16},{1,17},{2,18},{3,19},{4,20},{5,21},{6,22},{7,23},{8,24},{9,... | collective-permute-start | bytes 786440 | tf_op jit(solution)/shard_map/ppermute | solution.py:474
  129.8 12.4 %collective-permute-start.24 = (f32[2,128,256]{2,1,0:T(8,128)S(1)}, f32[2,128,256]{2,1,0:T(8,128)S(1)}, u32[]{:S(2)}, u32[]{:S(2)}) collective-permute-start(f32[2,128,256]{2,1,0:T(8,128)S(1)} %slice_add_fusion.10), channel_id=1, source_target_pairs={{0,1},{1,0},{2,3},{3,2},{4,5},{5,4},{6,7},{7,6},{8,9},{9,8},{10,11... | collective-permute-start | bytes 786440 | tf_op jit(solution)/shard_map/ppermute | solution.py:474
  132.4 8.4 %collective-permute-start.13 = (f32[1,128,256]{2,1,0:T(8,128)S(1)}, f32[1,128,256]{2,1,0:T(8,128)S(1)}, u32[]{:S(2)}, u32[]{:S(2)}) collective-permute-start(f32[1,128,256]{2,1,0:T(8,128)S(1)} %slice_add_fusion.42), channel_id=1, source_target_pairs={{0,2},{1,3},{2,0},{3,1},{4,6},{5,7},{6,4},{7,5},{8,10},{9,11},{10,... | collective-permute-start | bytes 393224 | tf_op jit(solution)/shard_map/ppermute | solution.py:474
  136.0 5.0 %collective-permute-start.17 = (f32[1,128,256]{2,1,0:T(8,128)S(1)}, f32[1,128,256]{2,1,0:T(8,128)S(1)}, u32[]{:S(2)}, u32[]{:S(2)}) collective-permute-start(f32[1,128,256]{2,1,0:T(8,128)S(1)} %slice_add_fusion.38), channel_id=1, source_target_pairs={{0,8},{1,9},{2,10},{3,11},{4,12},{5,13},{6,14},{7,15},{8,0},{9,1},... | collective-permute-start | bytes 393224 | tf_op jit(solution)/shard_map/ppermute | solution.py:474
  137.8 8.5 %collective-permute-start.21 = (f32[1,128,256]{2,1,0:T(8,128)S(1)}, f32[1,128,256]{2,1,0:T(8,128)S(1)}, u32[]{:S(2)}, u32[]{:S(2)}) collective-permute-start(f32[1,128,256]{2,1,0:T(8,128)S(1)} %slice_add_fusion.34), channel_id=1, source_target_pairs={{0,2},{1,3},{2,0},{3,1},{4,6},{5,7},{6,4},{7,5},{8,10},{9,11},{10,... | collective-permute-start | bytes 393224 | tf_op jit(solution)/shard_map/ppermute | solution.py:474
  142.1 13.9 %collective-permute-start.26 = (f32[256,256]{1,0:T(8,128)S(1)}, f32[256,256]{1,0:T(8,128)S(1)}, u32[]{:S(2)}, u32[]{:S(2)}) collective-permute-start(f32[256,256]{1,0:T(8,128)S(1)} %shard_map.83.refs_7_), channel_id=1, source_target_pairs={{0,4},{1,5},{2,6},{3,7},{4,0},{5,1},{6,2},{7,3},{8,12},{9,13},{10,... | collective-permute-start | bytes 786440 | tf_op jit(solution)/shard_map/ppermute | solution.py:474
  143.1 25.6 %copy-start.3 = (f32[256,1536]{1,0:T(8,128)S(1)}, f32[256,1536]{1,0:T(8,128)}, u32[]{:S(2)}) copy-start(f32[256,1536]{1,0:T(8,128)} %get-tuple-element.13.refs_6_) | copy-start | bytes 4718596
  143.1 9.7 %collective-permute-start.25 = (f32[1,128,256]{2,1,0:T(8,128)S(1)}, f32[1,128,256]{2,1,0:T(8,128)S(1)}, u32[]{:S(2)}, u32[]{:S(2)}) collective-permute-start(f32[1,128,256]{2,1,0:T(8,128)S(1)} %slice_add_fusion.30), channel_id=1, source_target_pairs={{0,2},{1,3},{2,0},{3,1},{4,6},{5,7},{6,4},{7,5},{8,10},{9,11},{10,... | collective-permute-start | bytes 393224 | tf_op jit(solution)/shard_map/ppermute | solution.py:474
  145.6 11.2 %collective-permute-start.28 = (f32[256,256]{1,0:T(8,128)S(1)}, f32[256,256]{1,0:T(8,128)S(1)}, u32[]{:S(2)}, u32[]{:S(2)}) collective-permute-start(f32[256,256]{1,0:T(8,128)S(1)} %shard_map.83.refs_7_), channel_id=1, source_target_pairs={{0,8},{1,9},{2,10},{3,11},{4,12},{5,13},{6,14},{7,15},{8,0},{9,1},... | collective-permute-start | bytes 786440 | tf_op jit(solution)/shard_map/ppermute | solution.py:474
  153.9 9.3 %collective-permute-start.31 = (f32[256,256]{1,0:T(8,128)S(1)}, f32[256,256]{1,0:T(8,128)S(1)}, u32[]{:S(2)}, u32[]{:S(2)}) collective-permute-start(f32[256,256]{1,0:T(8,128)S(1)} %shard_map.86.refs_8_), channel_id=1, source_target_pairs={{0,16},{1,17},{2,18},{3,19},{4,20},{5,21},{6,22},{7,23},{8,24},{9,... | collective-permute-start | bytes 786440 | tf_op jit(solution)/shard_map/ppermute | solution.py:474
  155.4 8.5 %collective-permute-start.27 = (f32[256,256]{1,0:T(8,128)S(1)}, f32[256,256]{1,0:T(8,128)S(1)}, u32[]{:S(2)}, u32[]{:S(2)}) collective-permute-start(f32[256,256]{1,0:T(8,128)S(1)} %shard_map.86.refs_8_), channel_id=1, source_target_pairs={{0,4},{1,5},{2,6},{3,7},{4,0},{5,1},{6,2},{7,3},{8,12},{9,13},{10,... | collective-permute-start | bytes 786440 | tf_op jit(solution)/shard_map/ppermute | solution.py:474
  155.4 9.1 %collective-permute-start.29 = (f32[256,256]{1,0:T(8,128)S(1)}, f32[256,256]{1,0:T(8,128)S(1)}, u32[]{:S(2)}, u32[]{:S(2)}) collective-permute-start(f32[256,256]{1,0:T(8,128)S(1)} %shard_map.86.refs_8_), channel_id=1, source_target_pairs={{0,8},{1,9},{2,10},{3,11},{4,12},{5,13},{6,14},{7,15},{8,0},{9,1},... | collective-permute-start | bytes 786440 | tf_op jit(solution)/shard_map/ppermute | solution.py:474
  155.9 12.8 %collective-permute-start.30 = (f32[256,256]{1,0:T(8,128)S(1)}, f32[256,256]{1,0:T(8,128)S(1)}, u32[]{:S(2)}, u32[]{:S(2)}) collective-permute-start(f32[256,256]{1,0:T(8,128)S(1)} %shard_map.83.refs_7_), channel_id=1, source_target_pairs={{0,16},{1,17},{2,18},{3,19},{4,20},{5,21},{6,22},{7,23},{8,24},{9,... | collective-permute-start | bytes 786440 | tf_op jit(solution)/shard_map/ppermute | solution.py:474
  156.8 17.8 %collective-permute-start.32 = (f32[256,256]{1,0:T(8,128)S(1)}, f32[256,256]{1,0:T(8,128)S(1)}, u32[]{:S(2)}, u32[]{:S(2)}) collective-permute-start(f32[256,256]{1,0:T(8,128)S(1)} %collective-permute-done.28.refs_11_), channel_id=1, source_target_pairs={{0,16},{1,17},{2,18},{3,19},{4,20},{5,21},{6,22},{7,23},{8,24},{9,... | collective-permute-start | bytes 786440 | tf_op jit(solution)/shard_map/ppermute | solution.py:474
  163.1 11.4 %collective-permute-start.33 = (f32[256,256]{1,0:T(8,128)S(1)}, f32[256,256]{1,0:T(8,128)S(1)}, u32[]{:S(2)}, u32[]{:S(2)}) collective-permute-start(f32[256,256]{1,0:T(8,128)S(1)} %collective-permute-done.31.refs_14_), channel_id=1, source_target_pairs={{0,8},{1,9},{2,10},{3,11},{4,12},{5,13},{6,14},{7,15},{8,0},{9,1},... | collective-permute-start | bytes 786440 | tf_op jit(solution)/shard_map/ppermute | solution.py:474
  176.8 3.4 %collective-permute-start.38 = (f32[1,512,256]{2,1,0:T(8,128)S(1)}, f32[1,512,256]{2,1,0:T(8,128)S(1)}, u32[]{:S(2)}, u32[]{:S(2)}) collective-permute-start(f32[1,512,256]{2,1,0:T(8,128)S(1)} %get-tuple-element.20), channel_id=1, source_target_pairs={{0,4},{1,5},{2,6},{3,7},{4,0},{5,1},{6,2},{7,3},{8,12},{9,13},{10,... | collective-permute-start | bytes 1572872 | tf_op jit(solution)/shard_map/ppermute | solution.py:474
  176.8 2.3 %collective-permute-start.34 = (f32[256,256]{1,0:T(8,128)S(1)}, f32[256,256]{1,0:T(8,128)S(1)}, u32[]{:S(2)}, u32[]{:S(2)}) collective-permute-start(f32[256,256]{1,0:T(8,128)S(1)} %collective-permute-done.28.refs_11_), channel_id=1, source_target_pairs={{0,4},{1,5},{2,6},{3,7},{4,0},{5,1},{6,2},{7,3},{8,12},{9,13},{10,... | collective-permute-start | bytes 786440 | tf_op jit(solution)/shard_map/ppermute | solution.py:474
  177.3 2.1 %collective-permute-start.35 = (f32[256,256]{1,0:T(8,128)S(1)}, f32[256,256]{1,0:T(8,128)S(1)}, u32[]{:S(2)}, u32[]{:S(2)}) collective-permute-start(f32[256,256]{1,0:T(8,128)S(1)} %collective-permute-done.29.refs_12_), channel_id=1, source_target_pairs={{0,4},{1,5},{2,6},{3,7},{4,0},{5,1},{6,2},{7,3},{8,12},{9,13},{10,... | collective-permute-start | bytes 786440 | tf_op jit(solution)/shard_map/ppermute | solution.py:474
  177.3 2.5 %collective-permute-start.36 = (f32[256,256]{1,0:T(8,128)S(1)}, f32[256,256]{1,0:T(8,128)S(1)}, u32[]{:S(2)}, u32[]{:S(2)}) collective-permute-start(f32[256,256]{1,0:T(8,128)S(1)} %collective-permute-done.30.refs_13_), channel_id=1, source_target_pairs={{0,4},{1,5},{2,6},{3,7},{4,0},{5,1},{6,2},{7,3},{8,12},{9,13},{10,... | collective-permute-start | bytes 786440 | tf_op jit(solution)/shard_map/ppermute | solution.py:474
  177.8 2.4 %collective-permute-start.37 = (f32[256,256]{1,0:T(8,128)S(1)}, f32[256,256]{1,0:T(8,128)S(1)}, u32[]{:S(2)}, u32[]{:S(2)}) collective-permute-start(f32[256,256]{1,0:T(8,128)S(1)} %collective-permute-done.31.refs_14_), channel_id=1, source_target_pairs={{0,4},{1,5},{2,6},{3,7},{4,0},{5,1},{6,2},{7,3},{8,12},{9,13},{10,... | collective-permute-start | bytes 786440 | tf_op jit(solution)/shard_map/ppermute | solution.py:474

commit v5 on v4

--- a/solution.py
+++ b/solution.py
@@ -262,7 +262,7 @@
     for g in range(several * group):
         col = spread(inner, g % group) ^ (me_ref[0] & spread(inner, group - 1))
         unit = spread(outer_bits, step * several + g // group) | col
-        place = place_of(bits, unit)
+        place = place_of(bits, unit) % out_ref.shape[0]
         term = total[g * rows : (g + 1) * rows]
         if received:
             term = term + received[0][place]
@@ -279,6 +279,8 @@
     outer_bits = [bit for bit in bits if bit >= col_bits]
     group = 1 << len(inner)
     several = 1
+    together = int(sorted(bits[len(outer_bits) :], reverse=True) == inner)
+    held = group if together else units
 
     def place(number, piece, f, me_ref):
         unit = (spread(outer_bits, f * several + number) | base) ^ me_ref[0]
@@ -293,14 +295,16 @@
     ] + [pl.BlockSpec((depth, count), lambda f, me_ref: (0, 0))]
     operands = [tiles] * (several * pieces) + [seed]
     if received is not None:
-        half = received.shape[0] // units - 1
-        in_specs.append(pl.BlockSpec((units, rows, count), lambda f, me_ref: (half, 0, 0)))
+        skip = (received.shape[0] - units) // held
+        in_specs.append(
+            pl.BlockSpec((held, rows, count), lambda f, me_ref: (skip + f * together, 0, 0))
+        )
         operands.append(received)
     return call(
         functools.partial(shared_kernel, bits, inner, several, pieces),
         (units // (group * several),),
         in_specs,
-        pl.BlockSpec((units, rows, count), lambda f, me_ref: (0, 0, 0)),
+        pl.BlockSpec((held, rows, count), lambda f, me_ref: (f * together, 0, 0)),
         jax.ShapeDtypeStruct((units, rows, count), F32),
         6 * units * rows * depth * count,
         4 * units * rows * (depth + count),

time: 189 us -> 189 us (level)
  no operation moved by 1% of the time
where the time goes in v5:
time: 189 us; the launch traced here: 188 us
  Pallas kernels  78.6 us (42%)
  waiting for transfers between devices  54.6 us (29%)
  starting transfers between devices  38.6 us (20%)
  other arithmetic  14 us (7%)
    pallas_call x22, Pallas kernels, run(): pl.pallas_call(body, grid_spec=pltpu.PrefetchScalarGridSpec(num_scalar_pr...  78.6 us
    ppermute x39, waiting for transfers between devices, exchange(): lax.ppermute(array, AXES, [(w, w ^ 1 << bit) for w in range(devices)])  54.6 us
    ppermute x39, starting transfers between devices, exchange(): lax.ppermute(array, AXES, [(w, w ^ 1 << bit) for w in range(devices)])  38.6 us
    add x14, other arithmetic, halved(): away = sum((term[half:2 * half] for term in terms))  12.8 us
  transfers between devices with their start and end apart: 39, of which 19 were waited for; matrix products, arithmetic and copies ran while one was open for 7% of the time, Pallas kernels for 30%

profile of v5, /device:TPU:0, one launch (start us, length us, event | category | flops | bytes accessed | tf_op | source)
XLA Modules:
  0.0 188.1 jit_solution(17999711566004807422)
XLA Ops:
  0.6 4.3 %shard_map.68 = (f32[256,1536]{1,0:T(8,128)}, bf16[256,1536]{1,0:T(8,128)(2,1)}) custom-call(f32[2,768,256]{2,1,0:T(8,128)} %bitcast.122, f32[2,768,256]{2,1,0:T(8,128)} %bitcast.123, f32[2,768,256]{2,1,0:T(8,128)} %bitcast.124, f32[2,768,768]{2,1,0:T(8,128)} %bitcast.114, f32[2,768,768]{2,1,0:T(8,128)} %bitcast.115, f32[2,768,768]{2,1,0:T(8,128)} %bitcast.116, ...), custom_call_target="tpu_custom_call" | custom-call | flops 1811939328 | bytes 9437184 | tf_op jit(solution)/shard_map/pallas_call | solution.py:55
  5.0 1.1 copy-done.2
  6.1 3.0 %shard_map.70 = f32[4,256,256]{2,1,0:T(8,128)S(1)} custom-call(s32[1]{0:T(128)} %bitcast.me_ref, bf16[1536,4096]{1,0:T(8,128)(2,1)} %bitcast.71, bf16[1536,4096]{1,0:T(8,128)(2,1)} %bitcast.61, bf16[1536,4096]{1,0:T(8,128)(2,1)} %bitcast.62, bf16[1536,4096]{1,0:T(8,128)(2,1)} %bitcast.63, bf16[1536,4096]{1,0:T(8,128)(2,1)} %bitcast.64, ...), custom_call_target="tpu_custom_call" | custom-call | flops 805306368 | bytes 4194304 | tf_op jit(solution)/shard_map/pallas_call | solution.py:55
  9.6 3.0 %shard_map.71 = f32[4,256,256]{2,1,0:T(8,128)S(1)} custom-call(s32[1]{0:T(128)} %bitcast.me_ref, bf16[1536,4096]{1,0:T(8,128)(2,1)} %bitcast.72, bf16[1536,4096]{1,0:T(8,128)(2,1)} %bitcast.73, bf16[1536,4096]{1,0:T(8,128)(2,1)} %bitcast.74, bf16[1536,4096]{1,0:T(8,128)(2,1)} %bitcast.75, bf16[1536,4096]{1,0:T(8,128)(2,1)} %bitcast.76, ...), custom_call_target="tpu_custom_call" | custom-call | flops 805306368 | bytes 4194304 | tf_op jit(solution)/shard_map/pallas_call | solution.py:55
  12.8 5.1 %shard_map.69 = (f32[4,256,256]{2,1,0:T(8,128)S(1)}, f32[4,256,256]{2,1,0:T(8,128)}) custom-call(s32[1]{0:T(128)} %bitcast.me_ref, bf16[1536,4096]{1,0:T(8,128)(2,1)} %bitcast.86, bf16[1536,4096]{1,0:T(8,128)(2,1)} %bitcast.85, bf16[1536,4096]{1,0:T(8,128)(2,1)} %bitcast.84, bf16[1536,4096]{1,0:T(8,128)(2,1)} %bitcast.87, bf16[1536,4096]{1,0:T(8,128)(2,1)} %bitcast.88, ...), custom_call_target="tpu_custom_call" | custom-call | flops 1610612736 | bytes 8388608 | tf_op jit(solution)/shard_map/pallas_call | solution.py:55
  18.0 2.9 %collective-permute-start.1 = (f32[2,256,256]{2,1,0:T(8,128)S(1)}, f32[2,256,256]{2,1,0:T(8,128)S(1)}, u32[]{:S(2)}, u32[]{:S(2)}) collective-permute-start(f32[2,256,256]{2,1,0:T(8,128)S(1)} %slice_add_fusion.9), channel_id=1, source_target_pairs={{0,8},{1,9},{2,10},{3,11},{4,12},{5,13},{6,14},{7,15},{8,0},{9,1},... | collective-permute-start | bytes 1572872 | tf_op jit(solution)/shard_map/ppermute | solution.py:478
  20.9 1.1 slice_add_fusion.8
  22.0 1.6 collective-permute-start.4
  23.6 9.6 %collective-permute-done.1 = f32[2,256,256]{2,1,0:T(8,128)S(1)} collective-permute-done((f32[2,256,256]{2,1,0:T(8,128)S(1)}, f32[2,256,256]{2,1,0:T(8,128)S(1)}, u32[]{:S(2)}, u32[]{:S(2)}) %collective-permute-start.1) | collective-permute-done | bytes 524320 | tf_op jit(solution)/shard_map/ppermute | solution.py:478
  33.3 1.8 collective-permute-start.2
  35.1 0.9 collective-permute-done.4
  36.8 4.7 %collective-permute-done.2.refs_1_ = f32[1,256,256]{2,1,0:T(8,128)S(1)} collective-permute-done((f32[1,256,256]{2,1,0:T(8,128)S(1)}, f32[1,256,256]{2,1,0:T(8,128)S(1)}, u32[]{:S(2)}, u32[]{:S(2)}) %collective-permute-start.2) | collective-permute-done | bytes 262176 | tf_op jit(solution)/shard_map/ppermute | solution.py:478
  41.5 1.9 collective-permute-done.5.refs_3_
  43.6 4.5 %shard_map.73 = f32[16,128,256]{2,1,0:T(8,128)S(1)} custom-call(s32[1]{0:T(128)} %bitcast.4.me_ref.refs_0_, f32[8,2,2,512,1,512]{5,4,3,2,1,0:T(1,128)} %bitcast.12, f32[8,2,2,512,1,512]{5,4,3,2,1,0:T(1,128)} %bitcast.13, f32[8,2,2,512,1,512]{5,4,3,2,1,0:T(1,128)} %bitcast.14, f32[8,2,2,512,1,512]{5,4,3,2,1,0:T(1,128)} %bitcast.15, ...), custom_call_target="tpu_custom_call" | custom-call | flops 1610612736 | bytes 6291456 | tf_op jit(solution)/shard_map/pallas_call | solution.py:55
  48.2 4.5 %shard_map.75 = f32[16,128,256]{2,1,0:T(8,128)S(1)} custom-call(s32[1]{0:T(128)} %bitcast.4.me_ref.refs_0_, f32[8,2,2,512,1,512]{5,4,3,2,1,0:T(1,128)} %bitcast.16, f32[8,2,2,512,1,512]{5,4,3,2,1,0:T(1,128)} %bitcast.17, f32[8,2,2,512,1,512]{5,4,3,2,1,0:T(1,128)} %bitcast.18, f32[8,2,2,512,1,512]{5,4,3,2,1,0:T(1,128)} %bitcast.19, ...), custom_call_target="tpu_custom_call" | custom-call | flops 1610612736 | bytes 6291456 | tf_op jit(solution)/shard_map/pallas_call | solution.py:55
  53.3 4.5 %shard_map.77 = f32[16,128,256]{2,1,0:T(8,128)S(1)} custom-call(s32[1]{0:T(128)} %bitcast.4.me_ref.refs_0_, f32[8,2,2,512,1,512]{5,4,3,2,1,0:T(1,128)} %bitcast.20, f32[8,2,2,512,1,512]{5,4,3,2,1,0:T(1,128)} %bitcast.21, f32[8,2,2,512,1,512]{5,4,3,2,1,0:T(1,128)} %bitcast.22, f32[8,2,2,512,1,512]{5,4,3,2,1,0:T(1,128)} %bitcast.23, ...), custom_call_target="tpu_custom_call" | custom-call | flops 1610612736 | bytes 6291456 | tf_op jit(solution)/shard_map/pallas_call | solution.py:55
  57.9 4.5 %shard_map.79 = f32[16,128,256]{2,1,0:T(8,128)S(1)} custom-call(s32[1]{0:T(128)} %bitcast.4.me_ref.refs_0_, f32[8,2,2,512,1,512]{5,4,3,2,1,0:T(1,128)} %bitcast.24, f32[8,2,2,512,1,512]{5,4,3,2,1,0:T(1,128)} %bitcast.25, f32[8,2,2,512,1,512]{5,4,3,2,1,0:T(1,128)} %bitcast.26, f32[8,2,2,512,1,512]{5,4,3,2,1,0:T(1,128)} %bitcast.27, ...), custom_call_target="tpu_custom_call" | custom-call | flops 1610612736 | bytes 6291456 | tf_op jit(solution)/shard_map/pallas_call | solution.py:55
  62.9 3.3 %shard_map.74.refs_6_ = f32[8,128,256]{2,1,0:T(8,128)} custom-call(s32[1]{0:T(128)} %bitcast.4.me_ref.refs_0_, f32[8,2,2,512,1,512]{5,4,3,2,1,0:T(1,128)} %bitcast.28, f32[8,2,2,512,1,512]{5,4,3,2,1,0:T(1,128)} %bitcast.29, f32[8,2,2,512,1,512]{5,4,3,2,1,0:T(1,128)} %bitcast.30, f32[8,2,2,512,1,512]{5,4,3,2,1,0:T(1,128)} %bitcast.31, ...), custom_call_target="tpu_custom_call" | custom-call | flops 805306368 | bytes 3145728 | tf_op jit(solution)/shard_map/pallas_call | solution.py:55
  67.0 3.5 %shard_map.76.refs_7_ = f32[8,128,256]{2,1,0:T(8,128)} custom-call(s32[1]{0:T(128)} %bitcast.4.me_ref.refs_0_, f32[8,2,2,512,1,512]{5,4,3,2,1,0:T(1,128)} %bitcast.35, f32[8,2,2,512,1,512]{5,4,3,2,1,0:T(1,128)} %bitcast.33, f32[8,2,2,512,1,512]{5,4,3,2,1,0:T(1,128)} %bitcast.34, f32[8,2,2,512,1,512]{5,4,3,2,1,0:T(1,128)} %bitcast.32, ...), custom_call_target="tpu_custom_call" | custom-call | flops 805306368 | bytes 3145728 | tf_op jit(solution)/shard_map/pallas_call | solution.py:55
  70.6 1.2 collective-permute-start.14
  71.8 5.2 %shard_map.78.refs_8_ = f32[8,128,256]{2,1,0:T(8,128)} custom-call(s32[1]{0:T(128)} %bitcast.4.me_ref.refs_0_, f32[8,2,2,512,1,512]{5,4,3,2,1,0:T(1,128)} %bitcast.36, f32[8,2,2,512,1,512]{5,4,3,2,1,0:T(1,128)} %bitcast.37, f32[8,2,2,512,1,512]{5,4,3,2,1,0:T(1,128)} %bitcast.38, f32[8,2,2,512,1,512]{5,4,3,2,1,0:T(1,128)} %bitcast.39, ...), custom_call_target="tpu_custom_call" | custom-call | flops 805306368 | bytes 3145728 | tf_op jit(solution)/shard_map/pallas_call | solution.py:55
  76.9 1.6 collective-permute-start.18
  78.5 3.4 %shard_map.80.refs_9_ = f32[8,128,256]{2,1,0:T(8,128)} custom-call(s32[1]{0:T(128)} %bitcast.4.me_ref.refs_0_, f32[8,2,2,512,1,512]{5,4,3,2,1,0:T(1,128)} %bitcast.40, f32[8,2,2,512,1,512]{5,4,3,2,1,0:T(1,128)} %bitcast.41, f32[8,2,2,512,1,512]{5,4,3,2,1,0:T(1,128)} %bitcast.42, f32[8,2,2,512,1,512]{5,4,3,2,1,0:T(1,128)} %bitcast.43, ...), custom_call_target="tpu_custom_call" | custom-call | flops 805306368 | bytes 3145728 | tf_op jit(solution)/shard_map/pallas_call | solution.py:55
  81.9 1.5 collective-permute-start.22
  83.4 2.6 %shard_map.81.refs_0_ = f32[8,128,256]{2,1,0:T(8,128)S(1)} custom-call(s32[1]{0:T(128)} %bitcast.4.me_ref.refs_0_, f32[8,2,2,512,1,512]{5,4,3,2,1,0:T(1,128)} %bitcast.46, f32[8,2,2,512,1,512]{5,4,3,2,1,0:T(1,128)} %bitcast.45, f32[8,2,2,512,1,512]{5,4,3,2,1,0:T(1,128)} %bitcast.44, f32[8,2,2,512,1,512]{5,4,3,2,1,0:T(1,128)} %bitcast.47, ...), custom_call_target="tpu_custom_call" | custom-call | flops 805306368 | bytes 3145728 | tf_op jit(solution)/shard_map/pallas_call | solution.py:55
  86.0 2.6 %shard_map.82.refs_6_ = f32[8,128,256]{2,1,0:T(8,128)S(1)} custom-call(s32[1]{0:T(128)} %bitcast.4.me_ref.refs_0_, f32[8,2,2,512,1,512]{5,4,3,2,1,0:T(1,128)} %bitcast.48, f32[8,2,2,512,1,512]{5,4,3,2,1,0:T(1,128)} %bitcast.49, f32[8,2,2,512,1,512]{5,4,3,2,1,0:T(1,128)} %bitcast.50, f32[8,2,2,512,1,512]{5,4,3,2,1,0:T(1,128)} %bitcast.51, ...), custom_call_target="tpu_custom_call" | custom-call | flops 805306368 | bytes 3145728 | tf_op jit(solution)/shard_map/pallas_call | solution.py:55
  88.6 3.9 %shard_map.84.refs_0_ = f32[8,128,256]{2,1,0:T(8,128)S(1)} custom-call(s32[1]{0:T(128)} %bitcast.4.me_ref.refs_0_, f32[8,2,2,512,1,512]{5,4,3,2,1,0:T(1,128)} %bitcast.52, f32[8,2,2,512,1,512]{5,4,3,2,1,0:T(1,128)} %bitcast.53, f32[8,2,2,512,1,512]{5,4,3,2,1,0:T(1,128)} %bitcast.54, f32[8,2,2,512,1,512]{5,4,3,2,1,0:T(1,128)} %bitcast.55, ...), custom_call_target="tpu_custom_call" | custom-call | flops 805306368 | bytes 3145728 | tf_op jit(solution)/shard_map/pallas_call | solution.py:55
  92.5 2.6 %shard_map.85.refs_6_ = f32[8,128,256]{2,1,0:T(8,128)S(1)} custom-call(s32[1]{0:T(128)} %bitcast.4.me_ref.refs_0_, f32[8,2,2,512,1,512]{5,4,3,2,1,0:T(1,128)} %bitcast.56, f32[8,2,2,512,1,512]{5,4,3,2,1,0:T(1,128)} %bitcast.57, f32[8,2,2,512,1,512]{5,4,3,2,1,0:T(1,128)} %bitcast.58, f32[8,2,2,512,1,512]{5,4,3,2,1,0:T(1,128)} %bitcast.59, ...), custom_call_target="tpu_custom_call" | custom-call | flops 805306368 | bytes 3145728 | tf_op jit(solution)/shard_map/pallas_call | solution.py:55
  95.1 1.3 slice_add_fusion.6
  97.0 1.1 slice_add_fusion.4
  98.7 4.7 %collective-permute-done.18.refs_2_ = f32[8,128,256]{2,1,0:T(8,128)} collective-permute-done((f32[8,128,256]{2,1,0:T(8,128)}, f32[8,128,256]{2,1,0:T(8,128)}, u32[]{:S(2)}, u32[]{:S(2)}) %collective-permute-start.18) | collective-permute-done | bytes 1048608 | tf_op jit(solution)/shard_map/ppermute | solution.py:478
  103.3 1.1 slice_add_fusion.2
  104.5 1.6 collective-permute-start.19
  106.1 8.9 %collective-permute-done.22.refs_8_ = f32[8,128,256]{2,1,0:T(8,128)} collective-permute-done((f32[8,128,256]{2,1,0:T(8,128)}, f32[8,128,256]{2,1,0:T(8,128)}, u32[]{:S(2)}, u32[]{:S(2)}) %collective-permute-start.22) | collective-permute-done | bytes 1048608 | tf_op jit(solution)/shard_map/ppermute | solution.py:478
  115.0 1.1 slice_add_fusion
  116.2 1.6 collective-permute-start.23
  117.8 1.0 slice_add_fusion.19
  118.8 1.7 collective-permute-start.12
  120.4 1.0 slice_add_fusion.16
  121.5 2.6 %collective-permute-start.16 = (f32[2,128,256]{2,1,0:T(8,128)S(1)}, f32[2,128,256]{2,1,0:T(8,128)S(1)}, u32[]{:S(2)}, u32[]{:S(2)}) collective-permute-start(f32[2,128,256]{2,1,0:T(8,128)S(1)} %slice_add_fusion.16), channel_id=1, source_target_pairs={{0,2},{1,3},{2,0},{3,1},{4,6},{5,7},{6,4},{7,5},{8,10},{9,11},{10,... | collective-permute-start | bytes 786440 | tf_op jit(solution)/shard_map/ppermute | solution.py:478
  124.1 1.2 collective-permute-done.19.refs_3_
  125.3 1.0 slice_add_fusion.13
  126.3 1.6 collective-permute-start.20
  128.6 1.0 slice_add_fusion.10
  129.6 1.6 collective-permute-start.24
  131.3 1.0 slice_add_fusion.42
  132.2 2.7 %collective-permute-start.13 = (f32[1,128,256]{2,1,0:T(8,128)S(1)}, f32[1,128,256]{2,1,0:T(8,128)S(1)}, u32[]{:S(2)}, u32[]{:S(2)}) collective-permute-start(f32[1,128,256]{2,1,0:T(8,128)S(1)} %slice_add_fusion.42), channel_id=1, source_target_pairs={{0,2},{1,3},{2,0},{3,1},{4,6},{5,7},{6,4},{7,5},{8,10},{9,11},{10,... | collective-permute-start | bytes 393224 | tf_op jit(solution)/shard_map/ppermute | solution.py:478
  134.9 1.0 slice_add_fusion.38
  135.9 0.9 collective-permute-start.17
  136.7 0.9 slice_add_fusion.34
  138.1 2.6 %collective-permute-done.13.refs_5_ = f32[1,128,256]{2,1,0:T(8,128)S(1)} collective-permute-done((f32[1,128,256]{2,1,0:T(8,128)S(1)}, f32[1,128,256]{2,1,0:T(8,128)S(1)}, u32[]{:S(2)}, u32[]{:S(2)}) %collective-permute-start.13) | collective-permute-done | bytes 131104 | tf_op jit(solution)/shard_map/ppermute | solution.py:478
  140.9 1.0 shard_map.83.refs_7_
  142.0 1.0 slice_add_fusion.30
  143.0 2.4 %collective-permute-start.25 = (f32[1,128,256]{2,1,0:T(8,128)S(1)}, f32[1,128,256]{2,1,0:T(8,128)S(1)}, u32[]{:S(2)}, u32[]{:S(2)}) collective-permute-start(f32[1,128,256]{2,1,0:T(8,128)S(1)} %slice_add_fusion.30), channel_id=1, source_target_pairs={{0,2},{1,3},{2,0},{3,1},{4,6},{5,7},{6,4},{7,5},{8,10},{9,11},{10,... | collective-permute-start | bytes 393224 | tf_op jit(solution)/shard_map/ppermute | solution.py:478
  146.2 6.5 %collective-permute-done.25.refs_11_ = f32[1,128,256]{2,1,0:T(8,128)S(1)} collective-permute-done((f32[1,128,256]{2,1,0:T(8,128)S(1)}, f32[1,128,256]{2,1,0:T(8,128)S(1)}, u32[]{:S(2)}, u32[]{:S(2)}) %collective-permute-start.25) | collective-permute-done | bytes 131104 | tf_op jit(solution)/shard_map/ppermute | solution.py:478
  152.7 1.1 shard_map.86.refs_8_
  153.7 1.6 collective-permute-start.31
  156.6 1.2 collective-permute-start.32
  157.8 5.2 %collective-permute-done.31.refs_14_ = f32[256,256]{1,0:T(8,128)S(1)} collective-permute-done((f32[256,256]{1,0:T(8,128)S(1)}, f32[256,256]{1,0:T(8,128)S(1)}, u32[]{:S(2)}, u32[]{:S(2)}) %collective-permute-start.31) | collective-permute-done | bytes 262176 | tf_op jit(solution)/shard_map/ppermute | solution.py:478
  164.4 4.2 %collective-permute-done.30.refs_13_ = f32[256,256]{1,0:T(8,128)S(1)} collective-permute-done((f32[256,256]{1,0:T(8,128)S(1)}, f32[256,256]{1,0:T(8,128)S(1)}, u32[]{:S(2)}, u32[]{:S(2)}) %collective-permute-start.30) | collective-permute-done | bytes 262176 | tf_op jit(solution)/shard_map/ppermute | solution.py:478
  168.6 5.8 %shard_map.87 = (f32[1536,256]{1,0:T(8,128)S(1)}, f32[4096,256]{1,0:T(8,128)}) custom-call(s32[1]{0:T(128)} %bitcast.me_ref, bf16[1536,4096]{1,0:T(8,128)(2,1)} %bitcast.99, bf16[1536,4096]{1,0:T(8,128)(2,1)} %bitcast.97, bf16[1536,4096]{1,0:T(8,128)(2,1)} %bitcast.98, bf16[1536,4096]{1,0:T(8,128)(2,1)} %bitcast.96, bf16[1536,4096]{1,0:T(8,128)(2,1)} %bitcast.100, ...), custom_call_target="tpu_custom_call" | custom-call | flops 1610612736 | bytes 13631488 | tf_op jit(solution)/shard_map/pallas_call | solution.py:55
  174.4 2.2 %shard_map.88 = (f32[1536,256]{1,0:T(8,128)S(1)}, f32[4096,256]{1,0:T(8,128)}, f32[1,512,256]{2,1,0:T(8,128)S(1)}) custom-call(s32[1]{0:T(128)} %bitcast.me_ref, bf16[1536,4096]{1,0:T(8,128)(2,1)} %bitcast.102, bf16[1536,4096]{1,0:T(8,128)(2,1)} %bitcast.103, bf16[1536,4096]{1,0:T(8,128)(2,1)} %bitcast.104, ...), custom_call_target="tpu_custom_call", output_to_operand_aliasing={{1}: (10, {})} | custom-call | flops 402653184 | bytes 5767168 | tf_op jit(solution)/shard_map/pallas_call | solution.py:55
  177.7 1.3 collective-permute-done.34.refs_7_
  180.1 7.8 %shard_map.89 = (f32[2,768,256]{2,1,0:T(8,128)}, f32[4096,256]{1,0:T(8,128)}) custom-call(s32[1]{0:T(128)} %bitcast.me_ref, bf16[1536,4096]{1,0:T(8,128)(2,1)} %bitcast.108, bf16[1536,4096]{1,0:T(8,128)(2,1)} %bitcast.109, bf16[1536,4096]{1,0:T(8,128)(2,1)} %bitcast.110, bf16[1536,4096]{1,0:T(8,128)(2,1)} %bitcast.111, ...), custom_call_target="tpu_custom_call", output_to_operand_aliasing={{1}: (13, {})} | custom-call | flops 3019898880 | bytes 15728640 | tf_op jit(solution)/shard_map/pallas_call | solution.py:55
  (64 shorter events, 12.2 us)
Async XLA Ops:
  5.0 1.1 copy-start.2
  9.1 8.9 %collective-permute-start = (f32[4,256,256]{2,1,0:T(8,128)S(1)}, f32[4,256,256]{2,1,0:T(8,128)S(1)}, u32[]{:S(2)}, u32[]{:S(2)}) collective-permute-start(f32[4,256,256]{2,1,0:T(8,128)S(1)} %shard_map.70), channel_id=1, source_target_pairs={{0,4},{1,5},{2,6},{3,7},{4,0},{5,1},{6,2},{7,3},{8,12},{9,13},{10,... | collective-permute-start | bytes 3145736 | tf_op jit(solution)/shard_map/ppermute | solution.py:478
  12.6 8.3 %collective-permute-start.3 = (f32[4,256,256]{2,1,0:T(8,128)S(1)}, f32[4,256,256]{2,1,0:T(8,128)S(1)}, u32[]{:S(2)}, u32[]{:S(2)}) collective-permute-start(f32[4,256,256]{2,1,0:T(8,128)S(1)} %shard_map.71), channel_id=1, source_target_pairs={{0,4},{1,5},{2,6},{3,7},{4,0},{5,1},{6,2},{7,3},{8,12},{9,13},{10,... | collective-permute-start | bytes 3145736 | tf_op jit(solution)/shard_map/ppermute | solution.py:478
  18.0 18.0 %copy-start.5 = (f32[4,256,256]{2,1,0:T(8,128)S(1)}, f32[4,256,256]{2,1,0:T(8,128)}, u32[]{:S(2)}) copy-start(f32[4,256,256]{2,1,0:T(8,128)} %get-tuple-element.16) | copy-start | bytes 3145732
  18.0 15.2 %collective-permute-start.1 = (f32[2,256,256]{2,1,0:T(8,128)S(1)}, f32[2,256,256]{2,1,0:T(8,128)S(1)}, u32[]{:S(2)}, u32[]{:S(2)}) collective-permute-start(f32[2,256,256]{2,1,0:T(8,128)S(1)} %slice_add_fusion.9), channel_id=1, source_target_pairs={{0,8},{1,9},{2,10},{3,11},{4,12},{5,13},{6,14},{7,15},{8,0},{9,1},... | collective-permute-start | bytes 1572872 | tf_op jit(solution)/shard_map/ppermute | solution.py:478
  22.0 21.3 %copy-start.4 = (f32[1,512,256]{2,1,0:T(8,128)S(1)}, f32[1,512,256]{2,1,0:T(8,128)}, u32[]{:S(2)}) copy-start(f32[1,512,256]{2,1,0:T(8,128)} %param.8) | copy-start | bytes 1572868
  22.0 13.9 %collective-permute-start.4 = (f32[2,256,256]{2,1,0:T(8,128)S(1)}, f32[2,256,256]{2,1,0:T(8,128)S(1)}, u32[]{:S(2)}, u32[]{:S(2)}) collective-permute-start(f32[2,256,256]{2,1,0:T(8,128)S(1)} %slice_add_fusion.8), channel_id=1, source_target_pairs={{0,16},{1,17},{2,18},{3,19},{4,20},{5,21},{6,22},{7,23},{8,24},{9,... | collective-permute-start | bytes 1572872 | tf_op jit(solution)/shard_map/ppermute | solution.py:478
  33.3 8.2 %collective-permute-start.2 = (f32[1,256,256]{2,1,0:T(8,128)S(1)}, f32[1,256,256]{2,1,0:T(8,128)S(1)}, u32[]{:S(2)}, u32[]{:S(2)}) collective-permute-start(f32[1,256,256]{2,1,0:T(8,128)S(1)} %get-tuple-element.26), channel_id=1, source_target_pairs={{0,16},{1,17},{2,18},{3,19},{4,20},{5,21},{6,22},{7,23},{8,24},{9,... | collective-permute-start | bytes 786440 | tf_op jit(solution)/shard_map/ppermute | solution.py:478
  36.1 7.3 %collective-permute-start.5 = (f32[1,256,256]{2,1,0:T(8,128)S(1)}, f32[1,256,256]{2,1,0:T(8,128)S(1)}, u32[]{:S(2)}, u32[]{:S(2)}) collective-permute-start(f32[1,256,256]{2,1,0:T(8,128)S(1)} %get-tuple-element.24), channel_id=1, source_target_pairs={{0,8},{1,9},{2,10},{3,11},{4,12},{5,13},{6,14},{7,15},{8,0},{9,1},... | collective-permute-start | bytes 786440 | tf_op jit(solution)/shard_map/ppermute | solution.py:478
  48.1 14.8 %collective-permute-start.6 = (f32[16,128,256]{2,1,0:T(8,128)S(1)}, f32[16,128,256]{2,1,0:T(8,128)S(1)}, u32[]{:S(2)}, u32[]{:S(2)}) collective-permute-start(f32[16,128,256]{2,1,0:T(8,128)S(1)} %shard_map.73), channel_id=1, source_target_pairs={{0,4},{1,5},{2,6},{3,7},{4,0},{5,1},{6,2},{7,3},{8,12},{9,13},{10,... | collective-permute-start | bytes 6291464 | tf_op jit(solution)/shard_map/ppermute | solution.py:478
  52.7 14.3 %collective-permute-start.7 = (f32[16,128,256]{2,1,0:T(8,128)S(1)}, f32[16,128,256]{2,1,0:T(8,128)S(1)}, u32[]{:S(2)}, u32[]{:S(2)}) collective-permute-start(f32[16,128,256]{2,1,0:T(8,128)S(1)} %shard_map.75), channel_id=1, source_target_pairs={{0,4},{1,5},{2,6},{3,7},{4,0},{5,1},{6,2},{7,3},{8,12},{9,13},{10,... | collective-permute-start | bytes 6291464 | tf_op jit(solution)/shard_map/ppermute | solution.py:478
  57.7 14.0 %collective-permute-start.8 = (f32[16,128,256]{2,1,0:T(8,128)S(1)}, f32[16,128,256]{2,1,0:T(8,128)S(1)}, u32[]{:S(2)}, u32[]{:S(2)}) collective-permute-start(f32[16,128,256]{2,1,0:T(8,128)S(1)} %shard_map.77), channel_id=1, source_target_pairs={{0,4},{1,5},{2,6},{3,7},{4,0},{5,1},{6,2},{7,3},{8,12},{9,13},{10,... | collective-permute-start | bytes 6291464 | tf_op jit(solution)/shard_map/ppermute | solution.py:478
  62.4 16.1 %collective-permute-start.9 = (f32[16,128,256]{2,1,0:T(8,128)S(1)}, f32[16,128,256]{2,1,0:T(8,128)S(1)}, u32[]{:S(2)}, u32[]{:S(2)}) collective-permute-start(f32[16,128,256]{2,1,0:T(8,128)S(1)} %shard_map.79), channel_id=1, source_target_pairs={{0,4},{1,5},{2,6},{3,7},{4,0},{5,1},{6,2},{7,3},{8,12},{9,13},{10,... | collective-permute-start | bytes 6291464 | tf_op jit(solution)/shard_map/ppermute | solution.py:478
  66.2 28.9 %collective-permute-start.10 = (f32[8,128,256]{2,1,0:T(8,128)}, f32[8,128,256]{2,1,0:T(8,128)}, u32[]{:S(2)}, u32[]{:S(2)}) collective-permute-start(f32[8,128,256]{2,1,0:T(8,128)} %shard_map.74.refs_6_), channel_id=1, source_target_pairs={{0,8},{1,9},{2,10},{3,11},{4,12},{5,13},{6,14},{7,15},{8,0},{9,1},... | collective-permute-start | bytes 3145736 | tf_op jit(solution)/shard_map/ppermute | solution.py:478
  70.6 26.4 %collective-permute-start.14 = (f32[8,128,256]{2,1,0:T(8,128)}, f32[8,128,256]{2,1,0:T(8,128)}, u32[]{:S(2)}, u32[]{:S(2)}) collective-permute-start(f32[8,128,256]{2,1,0:T(8,128)} %shard_map.76.refs_7_), channel_id=1, source_target_pairs={{0,16},{1,17},{2,18},{3,19},{4,20},{5,21},{6,22},{7,23},{8,24},{9,... | collective-permute-start | bytes 3145736 | tf_op jit(solution)/shard_map/ppermute | solution.py:478
  71.8 5.2 %copy-start = (f32[16,128,256]{2,1,0:T(8,128)}, f32[16,128,256]{2,1,0:T(8,128)S(1)}, u32[]{:S(2)}) copy-start(f32[16,128,256]{2,1,0:T(8,128)S(1)} %collective-permute-done.8.refs_5_.refs_1_) | copy-start | bytes 6291460
  76.9 26.4 %collective-permute-start.18 = (f32[8,128,256]{2,1,0:T(8,128)}, f32[8,128,256]{2,1,0:T(8,128)}, u32[]{:S(2)}, u32[]{:S(2)}) collective-permute-start(f32[8,128,256]{2,1,0:T(8,128)} %shard_map.78.refs_8_), channel_id=1, source_target_pairs={{0,1},{1,0},{2,3},{3,2},{4,5},{5,4},{6,7},{7,6},{8,9},{9,8},{10,11... | collective-permute-start | bytes 3145736 | tf_op jit(solution)/shard_map/ppermute | solution.py:478
  81.9 33.1 %collective-permute-start.22 = (f32[8,128,256]{2,1,0:T(8,128)}, f32[8,128,256]{2,1,0:T(8,128)}, u32[]{:S(2)}, u32[]{:S(2)}) collective-permute-start(f32[8,128,256]{2,1,0:T(8,128)} %shard_map.80.refs_9_), channel_id=1, source_target_pairs={{0,8},{1,9},{2,10},{3,11},{4,12},{5,13},{6,14},{7,15},{8,0},{9,1},... | collective-permute-start | bytes 3145736 | tf_op jit(solution)/shard_map/ppermute | solution.py:478
  95.1 8.2 %copy-start.1 = (f32[16,128,256]{2,1,0:T(8,128)S(1)}, f32[16,128,256]{2,1,0:T(8,128)}, u32[]{:S(2)}) copy-start(f32[16,128,256]{2,1,0:T(8,128)} %copy-done) | copy-start | bytes 6291460
  96.4 21.3 %collective-permute-start.11 = (f32[4,128,256]{2,1,0:T(8,128)S(1)}, f32[4,128,256]{2,1,0:T(8,128)S(1)}, u32[]{:S(2)}, u32[]{:S(2)}) collective-permute-start(f32[4,128,256]{2,1,0:T(8,128)S(1)} %slice_add_fusion.6), channel_id=1, source_target_pairs={{0,16},{1,17},{2,18},{3,19},{4,20},{5,21},{6,22},{7,23},{8,24},{9,... | collective-permute-start | bytes 1572872 | tf_op jit(solution)/shard_map/ppermute | solution.py:478
  98.1 22.3 %collective-permute-start.15 = (f32[4,128,256]{2,1,0:T(8,128)S(1)}, f32[4,128,256]{2,1,0:T(8,128)S(1)}, u32[]{:S(2)}, u32[]{:S(2)}) collective-permute-start(f32[4,128,256]{2,1,0:T(8,128)S(1)} %slice_add_fusion.4), channel_id=1, source_target_pairs={{0,1},{1,0},{2,3},{3,2},{4,5},{5,4},{6,7},{7,6},{8,9},{9,8},{10,11... | collective-permute-start | bytes 1572872 | tf_op jit(solution)/shard_map/ppermute | solution.py:478
  104.5 20.8 %collective-permute-start.19 = (f32[4,128,256]{2,1,0:T(8,128)S(1)}, f32[4,128,256]{2,1,0:T(8,128)S(1)}, u32[]{:S(2)}, u32[]{:S(2)}) collective-permute-start(f32[4,128,256]{2,1,0:T(8,128)S(1)} %slice_add_fusion.2), channel_id=1, source_target_pairs={{0,8},{1,9},{2,10},{3,11},{4,12},{5,13},{6,14},{7,15},{8,0},{9,1},... | collective-permute-start | bytes 1572872 | tf_op jit(solution)/shard_map/ppermute | solution.py:478
  116.2 12.4 %collective-permute-start.23 = (f32[4,128,256]{2,1,0:T(8,128)S(1)}, f32[4,128,256]{2,1,0:T(8,128)S(1)}, u32[]{:S(2)}, u32[]{:S(2)}) collective-permute-start(f32[4,128,256]{2,1,0:T(8,128)S(1)} %slice_add_fusion), channel_id=1, source_target_pairs={{0,16},{1,17},{2,18},{3,19},{4,20},{5,21},{6,22},{7,23},{8,24},{9,... | collective-permute-start | bytes 1572872 | tf_op jit(solution)/shard_map/ppermute | solution.py:478
  118.8 12.5 %collective-permute-start.12 = (f32[2,128,256]{2,1,0:T(8,128)S(1)}, f32[2,128,256]{2,1,0:T(8,128)S(1)}, u32[]{:S(2)}, u32[]{:S(2)}) collective-permute-start(f32[2,128,256]{2,1,0:T(8,128)S(1)} %slice_add_fusion.19), channel_id=1, source_target_pairs={{0,1},{1,0},{2,3},{3,2},{4,5},{5,4},{6,7},{7,6},{8,9},{9,8},{10,11... | collective-permute-start | bytes 786440 | tf_op jit(solution)/shard_map/ppermute | solution.py:478
  121.5 13.4 %collective-permute-start.16 = (f32[2,128,256]{2,1,0:T(8,128)S(1)}, f32[2,128,256]{2,1,0:T(8,128)S(1)}, u32[]{:S(2)}, u32[]{:S(2)}) collective-permute-start(f32[2,128,256]{2,1,0:T(8,128)S(1)} %slice_add_fusion.16), channel_id=1, source_target_pairs={{0,2},{1,3},{2,0},{3,1},{4,6},{5,7},{6,4},{7,5},{8,10},{9,11},{10,... | collective-permute-start | bytes 786440 | tf_op jit(solution)/shard_map/ppermute | solution.py:478
  126.3 10.4 %collective-permute-start.20 = (f32[2,128,256]{2,1,0:T(8,128)S(1)}, f32[2,128,256]{2,1,0:T(8,128)S(1)}, u32[]{:S(2)}, u32[]{:S(2)}) collective-permute-start(f32[2,128,256]{2,1,0:T(8,128)S(1)} %slice_add_fusion.13), channel_id=1, source_target_pairs={{0,16},{1,17},{2,18},{3,19},{4,20},{5,21},{6,22},{7,23},{8,24},{9,... | collective-permute-start | bytes 786440 | tf_op jit(solution)/shard_map/ppermute | solution.py:478
  129.6 12.4 %collective-permute-start.24 = (f32[2,128,256]{2,1,0:T(8,128)S(1)}, f32[2,128,256]{2,1,0:T(8,128)S(1)}, u32[]{:S(2)}, u32[]{:S(2)}) collective-permute-start(f32[2,128,256]{2,1,0:T(8,128)S(1)} %slice_add_fusion.10), channel_id=1, source_target_pairs={{0,1},{1,0},{2,3},{3,2},{4,5},{5,4},{6,7},{7,6},{8,9},{9,8},{10,11... | collective-permute-start | bytes 786440 | tf_op jit(solution)/shard_map/ppermute | solution.py:478
  132.2 8.4 %collective-permute-start.13 = (f32[1,128,256]{2,1,0:T(8,128)S(1)}, f32[1,128,256]{2,1,0:T(8,128)S(1)}, u32[]{:S(2)}, u32[]{:S(2)}) collective-permute-start(f32[1,128,256]{2,1,0:T(8,128)S(1)} %slice_add_fusion.42), channel_id=1, source_target_pairs={{0,2},{1,3},{2,0},{3,1},{4,6},{5,7},{6,4},{7,5},{8,10},{9,11},{10,... | collective-permute-start | bytes 393224 | tf_op jit(solution)/shard_map/ppermute | solution.py:478
  135.9 5.0 %collective-permute-start.17 = (f32[1,128,256]{2,1,0:T(8,128)S(1)}, f32[1,128,256]{2,1,0:T(8,128)S(1)}, u32[]{:S(2)}, u32[]{:S(2)}) collective-permute-start(f32[1,128,256]{2,1,0:T(8,128)S(1)} %slice_add_fusion.38), channel_id=1, source_target_pairs={{0,8},{1,9},{2,10},{3,11},{4,12},{5,13},{6,14},{7,15},{8,0},{9,1},... | collective-permute-start | bytes 393224 | tf_op jit(solution)/shard_map/ppermute | solution.py:478
  137.7 8.5 %collective-permute-start.21 = (f32[1,128,256]{2,1,0:T(8,128)S(1)}, f32[1,128,256]{2,1,0:T(8,128)S(1)}, u32[]{:S(2)}, u32[]{:S(2)}) collective-permute-start(f32[1,128,256]{2,1,0:T(8,128)S(1)} %slice_add_fusion.34), channel_id=1, source_target_pairs={{0,2},{1,3},{2,0},{3,1},{4,6},{5,7},{6,4},{7,5},{8,10},{9,11},{10,... | collective-permute-start | bytes 393224 | tf_op jit(solution)/shard_map/ppermute | solution.py:478
  141.9 13.9 %collective-permute-start.26 = (f32[256,256]{1,0:T(8,128)S(1)}, f32[256,256]{1,0:T(8,128)S(1)}, u32[]{:S(2)}, u32[]{:S(2)}) collective-permute-start(f32[256,256]{1,0:T(8,128)S(1)} %shard_map.83.refs_7_), channel_id=1, source_target_pairs={{0,4},{1,5},{2,6},{3,7},{4,0},{5,1},{6,2},{7,3},{8,12},{9,13},{10,... | collective-permute-start | bytes 786440 | tf_op jit(solution)/shard_map/ppermute | solution.py:478
  143.0 25.6 %copy-start.3 = (f32[256,1536]{1,0:T(8,128)S(1)}, f32[256,1536]{1,0:T(8,128)}, u32[]{:S(2)}) copy-start(f32[256,1536]{1,0:T(8,128)} %get-tuple-element.13.refs_6_) | copy-start | bytes 4718596
  143.0 9.7 %collective-permute-start.25 = (f32[1,128,256]{2,1,0:T(8,128)S(1)}, f32[1,128,256]{2,1,0:T(8,128)S(1)}, u32[]{:S(2)}, u32[]{:S(2)}) collective-permute-start(f32[1,128,256]{2,1,0:T(8,128)S(1)} %slice_add_fusion.30), channel_id=1, source_target_pairs={{0,2},{1,3},{2,0},{3,1},{4,6},{5,7},{6,4},{7,5},{8,10},{9,11},{10,... | collective-permute-start | bytes 393224 | tf_op jit(solution)/shard_map/ppermute | solution.py:478
  145.4 11.2 %collective-permute-start.28 = (f32[256,256]{1,0:T(8,128)S(1)}, f32[256,256]{1,0:T(8,128)S(1)}, u32[]{:S(2)}, u32[]{:S(2)}) collective-permute-start(f32[256,256]{1,0:T(8,128)S(1)} %shard_map.83.refs_7_), channel_id=1, source_target_pairs={{0,8},{1,9},{2,10},{3,11},{4,12},{5,13},{6,14},{7,15},{8,0},{9,1},... | collective-permute-start | bytes 786440 | tf_op jit(solution)/shard_map/ppermute | solution.py:478
  153.7 9.3 %collective-permute-start.31 = (f32[256,256]{1,0:T(8,128)S(1)}, f32[256,256]{1,0:T(8,128)S(1)}, u32[]{:S(2)}, u32[]{:S(2)}) collective-permute-start(f32[256,256]{1,0:T(8,128)S(1)} %shard_map.86.refs_8_), channel_id=1, source_target_pairs={{0,16},{1,17},{2,18},{3,19},{4,20},{5,21},{6,22},{7,23},{8,24},{9,... | collective-permute-start | bytes 786440 | tf_op jit(solution)/shard_map/ppermute | solution.py:478
  155.3 8.5 %collective-permute-start.27 = (f32[256,256]{1,0:T(8,128)S(1)}, f32[256,256]{1,0:T(8,128)S(1)}, u32[]{:S(2)}, u32[]{:S(2)}) collective-permute-start(f32[256,256]{1,0:T(8,128)S(1)} %shard_map.86.refs_8_), channel_id=1, source_target_pairs={{0,4},{1,5},{2,6},{3,7},{4,0},{5,1},{6,2},{7,3},{8,12},{9,13},{10,... | collective-permute-start | bytes 786440 | tf_op jit(solution)/shard_map/ppermute | solution.py:478
  155.3 9.1 %collective-permute-start.29 = (f32[256,256]{1,0:T(8,128)S(1)}, f32[256,256]{1,0:T(8,128)S(1)}, u32[]{:S(2)}, u32[]{:S(2)}) collective-permute-start(f32[256,256]{1,0:T(8,128)S(1)} %shard_map.86.refs_8_), channel_id=1, source_target_pairs={{0,8},{1,9},{2,10},{3,11},{4,12},{5,13},{6,14},{7,15},{8,0},{9,1},... | collective-permute-start | bytes 786440 | tf_op jit(solution)/shard_map/ppermute | solution.py:478
  155.8 12.8 %collective-permute-start.30 = (f32[256,256]{1,0:T(8,128)S(1)}, f32[256,256]{1,0:T(8,128)S(1)}, u32[]{:S(2)}, u32[]{:S(2)}) collective-permute-start(f32[256,256]{1,0:T(8,128)S(1)} %shard_map.83.refs_7_), channel_id=1, source_target_pairs={{0,16},{1,17},{2,18},{3,19},{4,20},{5,21},{6,22},{7,23},{8,24},{9,... | collective-permute-start | bytes 786440 | tf_op jit(solution)/shard_map/ppermute | solution.py:478
  156.6 17.8 %collective-permute-start.32 = (f32[256,256]{1,0:T(8,128)S(1)}, f32[256,256]{1,0:T(8,128)S(1)}, u32[]{:S(2)}, u32[]{:S(2)}) collective-permute-start(f32[256,256]{1,0:T(8,128)S(1)} %collective-permute-done.28.refs_11_), channel_id=1, source_target_pairs={{0,16},{1,17},{2,18},{3,19},{4,20},{5,21},{6,22},{7,23},{8,24},{9,... | collective-permute-start | bytes 786440 | tf_op jit(solution)/shard_map/ppermute | solution.py:478
  163.0 11.4 %collective-permute-start.33 = (f32[256,256]{1,0:T(8,128)S(1)}, f32[256,256]{1,0:T(8,128)S(1)}, u32[]{:S(2)}, u32[]{:S(2)}) collective-permute-start(f32[256,256]{1,0:T(8,128)S(1)} %collective-permute-done.31.refs_14_), channel_id=1, source_target_pairs={{0,8},{1,9},{2,10},{3,11},{4,12},{5,13},{6,14},{7,15},{8,0},{9,1},... | collective-permute-start | bytes 786440 | tf_op jit(solution)/shard_map/ppermute | solution.py:478
  176.7 3.4 %collective-permute-start.38 = (f32[1,512,256]{2,1,0:T(8,128)S(1)}, f32[1,512,256]{2,1,0:T(8,128)S(1)}, u32[]{:S(2)}, u32[]{:S(2)}) collective-permute-start(f32[1,512,256]{2,1,0:T(8,128)S(1)} %get-tuple-element.20), channel_id=1, source_target_pairs={{0,4},{1,5},{2,6},{3,7},{4,0},{5,1},{6,2},{7,3},{8,12},{9,13},{10,... | collective-permute-start | bytes 1572872 | tf_op jit(solution)/shard_map/ppermute | solution.py:478
  176.7 2.3 %collective-permute-start.34 = (f32[256,256]{1,0:T(8,128)S(1)}, f32[256,256]{1,0:T(8,128)S(1)}, u32[]{:S(2)}, u32[]{:S(2)}) collective-permute-start(f32[256,256]{1,0:T(8,128)S(1)} %collective-permute-done.28.refs_11_), channel_id=1, source_target_pairs={{0,4},{1,5},{2,6},{3,7},{4,0},{5,1},{6,2},{7,3},{8,12},{9,13},{10,... | collective-permute-start | bytes 786440 | tf_op jit(solution)/shard_map/ppermute | solution.py:478
  177.2 2.1 %collective-permute-start.35 = (f32[256,256]{1,0:T(8,128)S(1)}, f32[256,256]{1,0:T(8,128)S(1)}, u32[]{:S(2)}, u32[]{:S(2)}) collective-permute-start(f32[256,256]{1,0:T(8,128)S(1)} %collective-permute-done.29.refs_12_), channel_id=1, source_target_pairs={{0,4},{1,5},{2,6},{3,7},{4,0},{5,1},{6,2},{7,3},{8,12},{9,13},{10,... | collective-permute-start | bytes 786440 | tf_op jit(solution)/shard_map/ppermute | solution.py:478
  177.2 2.5 %collective-permute-start.36 = (f32[256,256]{1,0:T(8,128)S(1)}, f32[256,256]{1,0:T(8,128)S(1)}, u32[]{:S(2)}, u32[]{:S(2)}) collective-permute-start(f32[256,256]{1,0:T(8,128)S(1)} %collective-permute-done.30.refs_13_), channel_id=1, source_target_pairs={{0,4},{1,5},{2,6},{3,7},{4,0},{5,1},{6,2},{7,3},{8,12},{9,13},{10,... | collective-permute-start | bytes 786440 | tf_op jit(solution)/shard_map/ppermute | solution.py:478
  177.7 2.4 %collective-permute-start.37 = (f32[256,256]{1,0:T(8,128)S(1)}, f32[256,256]{1,0:T(8,128)S(1)}, u32[]{:S(2)}, u32[]{:S(2)}) collective-permute-start(f32[256,256]{1,0:T(8,128)S(1)} %collective-permute-done.31.refs_14_), channel_id=1, source_target_pairs={{0,4},{1,5},{2,6},{3,7},{4,0},{5,1},{6,2},{7,3},{8,12},{9,13},{10,... | collective-permute-start | bytes 786440 | tf_op jit(solution)/shard_map/ppermute | solution.py:478
